TPU v7x, 32 devices: a whole 2x2x4 slice. The times are simulated.
32 devices in a mesh: dp: 16 (over z, y, core), tensor: 2 (over x).
Axes of the slice: x: 2, y: 2, z: 4, core: 2. Of those that a mesh axis runs over, the one named last changes fastest.
Arguments:
- hidden: bfloat16 [8192, 2048], P('dp'), may hold values from -6 to 6
- segment_ids: int32 [8192], P('dp'), may hold values from 0 to 19, never falling along the last dimension, each value on 1 to 800 neighbouring positions
- cotangent: bfloat16 [8192, 2048], P('dp'), may hold values from -6 to 6
- w_zx: bfloat16 [2, 2048, 4096], P(None, 'dp', 'tensor'), may hold values from -0.125 to 0.125
- w_dt: bfloat16 [2048, 64], P('dp', 'tensor'), may hold values from -0.125 to 0.125
- w_bc: bfloat16 [2048, 256], P('dp'), may hold values from -0.125 to 0.125
- w_out: bfloat16 [4096, 2048], P('tensor', 'dp'), may hold values from -0.09375 to 0.09375
- conv_x: float32 [4, 4096], P(None, 'tensor'), may hold values from -3 to 3
- conv_bias_x: float32 [4096], P('tensor'), may hold values from -3 to 3
- conv_bc: float32 [4, 256], replicated, may hold values from -3 to 3
- conv_bias_bc: float32 [256], replicated, may hold values from -3 to 3
- dt_bias: float32 [64], P('tensor'), may hold values from -9 to -3
- a_log: float32 [64], P('tensor'), may hold values from -1 to 2
- d_skip: float32 [64], P('tensor'), may hold values from 0.5 to 1.5
- pre_gain: float32 [2048], replicated, may hold values from 0.1 to 1.9
- gate_gain: float32 [4096], P('tensor'), may hold values from 0.1 to 1.9
Outputs:
- output: bfloat16 [8192, 2048], P('dp')
- grad_hidden: bfloat16 [8192, 2048], P('dp')
- grad_w_zx: float32 [2, 2048, 4096], P(None, 'dp', 'tensor')
- grad_w_dt: float32 [2048, 64], P('dp', 'tensor')
- grad_w_bc: float32 [2048, 256], P('dp', 'tensor')
- grad_w_out: float32 [4096, 2048], P('tensor', 'dp')
- grad_conv_x: float32 [4, 4096], P(None, 'tensor')
- grad_conv_bias_x: float32 [4096], P('tensor')
- grad_conv_bc: float32 [4, 256], replicated
- grad_conv_bias_bc: float32 [256], replicated
- grad_dt_bias: float32 [64], P('tensor')
- grad_a_log: float32 [64], P('tensor')
- grad_d_skip: float32 [64], P('tensor')
- grad_pre_gain: float32 [2048], replicated
- grad_gate_gain: float32 [4096], P('tensor')
Inputs may be any that keep to these rules, and one draw needn't show every extreme that they name: `segment_ids`: never falling along the tokens; each document has 1 to 800 tokens, and one has exactly 800.
All inputs are finite; a program needn't handle non-finite values.
Results may differ from a plain program's by a relative error of at most 0.0096.
Values may be sent and summed in bfloat16 or wider, within the bound.
No kernel may reach another device: no remote copies, remote signals or barrier semaphores. Data moves between devices by JAX's collectives and lax.ppermute only.
A program may use at most 192 MiB of HBM per device.

v0:
```python
import jax
import jax.numpy as jnp
from jax import lax
from jax.sharding import PartitionSpec as P

SPAN = 256


epsilon = 1e-05
highest = lax.Precision.HIGHEST


def rounded(value):
    return lax.optimization_barrier(value.astype(jnp.bfloat16)).astype(jnp.float32)


def causal_conv(values, weights, bias, segs):
    width = weights.shape[0]
    length = values.shape[1]
    padded = jnp.pad(values, ((0, 0), (width - 1, 0), (0, 0)))
    pad_segs = jnp.pad(segs, ((0, 0), (width - 1, 0)), constant_values=-1)
    total = jnp.zeros(values.shape, jnp.float32) + bias
    for offset in range(width):
        same = (pad_segs[:, offset : offset + length] == segs).astype(jnp.float32)
        total = total + weights[offset] * padded[:, offset : offset + length] * same[..., None]
    return total


def state_scan(x_act, b_act, c_act, steps, rates, segs):
    groups, length, heads, hsize = x_act.shape
    count = length // SPAN

    def blocks(value):
        return jnp.moveaxis(value.reshape((groups, count, SPAN) + value.shape[2:]), 1, 0)

    causal = jnp.arange(SPAN)[:, None] >= jnp.arange(SPAN)[None, :]

    def one_block(carry, item):
        state, last_seg = carry
        x_blk, b_blk, c_blk, d_blk, s_blk = item
        cums = jnp.cumsum(d_blk * rates, axis=1)
        inner = jnp.einsum("gin,gjn->gij", c_blk, b_blk, precision=highest)
        keep = ((s_blk[:, :, None] == s_blk[:, None, :]) & causal[None])[..., None]
        gaps = cums[:, :, None, :] - cums[:, None, :, :]
        decay = jnp.where(keep, jnp.exp(jnp.where(keep, gaps, 0.0)), 0.0)
        mixing = inner[..., None] * decay * d_blk[:, None, :, :]
        intra = jnp.einsum("gijh,gjhp->gihp", mixing, x_blk, precision=highest)
        enter = jnp.exp(cums) * (s_blk == last_seg[:, None]).astype(jnp.float32)[..., None]
        carried = jnp.einsum("gin,ghnp->gihp", c_blk, state, precision=highest) * enter[..., None]
        tail = (
            jnp.exp(cums[:, -1:, :] - cums)
            * (s_blk == s_blk[:, -1:]).astype(jnp.float32)[..., None]
            * d_blk
        )
        fresh = jnp.einsum("gjn,gjhp->ghnp", b_blk, x_blk * tail[..., None], precision=highest)
        passing = jnp.exp(cums[:, -1, :]) * (s_blk[:, -1] == last_seg).astype(jnp.float32)[:, None]
        state = state * passing[:, :, None, None] + fresh
        return ((state, s_blk[:, -1]), intra + carried)

    start = (
        jnp.zeros((groups, heads, b_act.shape[-1], hsize), jnp.float32),
        jnp.full((groups,), -1, jnp.int32),
    )
    items = (blocks(x_act), blocks(b_act), blocks(c_act), blocks(steps), blocks(segs))
    final, outs = lax.scan(jax.checkpoint(one_block), start, items)
    return jnp.moveaxis(outs, 0, 1).reshape(x_act.shape)


def gate_mix(x_act, bc_act, gate, dt_raw, dt_bias, a_log, d_skip, segs):
    groups, length, inner = x_act.shape
    heads = dt_raw.shape[-1]
    x_heads = x_act.reshape(groups, length, heads, inner // heads)
    half = bc_act.shape[-1] // 2
    steps = jax.nn.softplus(dt_raw + dt_bias)
    rates = -jnp.exp(a_log)
    mixed = state_scan(x_heads, bc_act[..., :half], bc_act[..., half:], steps, rates, segs)
    mixed = mixed + d_skip[:, None] * x_heads
    return mixed.reshape(groups, length, inner) * jax.nn.silu(gate)


def norm_back(d_norm, inputs, scales, cot_rows, gain, width):
    weighted = d_norm * gain
    change = (
        weighted * scales
        - inputs * scales**3 * jnp.sum(weighted * inputs, -1, keepdims=True) / width
    )
    return (change + cot_rows, jnp.sum(d_norm * inputs * scales, 0))


def local(
    hidden,
    segment_ids,
    cotangent,
    w_zx,
    w_dt,
    w_bc,
    w_out,
    conv_x,
    conv_bias_x,
    conv_bc,
    conv_bias_bc,
    dt_bias,
    a_log,
    d_skip,
    pre_gain,
    gate_gain,
):
    tokens_here, width = hidden.shape
    n_tensor = lax.axis_size("tensor")
    tensor_index = lax.axis_index("tensor")
    full_zx, full_dt, full_bc, full_out = (
        lax.all_gather(w_zx, "dp", axis=1, tiled=True),
        lax.all_gather(w_dt, "dp", axis=0, tiled=True),
        lax.all_gather(w_bc, "dp", axis=0, tiled=True),
        lax.all_gather(w_out, "dp", axis=1, tiled=True),
    )
    inner_here = full_zx.shape[2]
    inner_all = inner_here * n_tensor
    row_count = tokens_here // n_tensor
    row_start = tensor_index * row_count
    inputs = hidden.astype(jnp.float32)
    scales = lax.rsqrt(jnp.mean(inputs * inputs, -1, keepdims=True) + epsilon)
    normed = (inputs * scales * pre_gain).astype(jnp.bfloat16)
    proj_zx = jnp.einsum("td,kdi->kti", normed, full_zx, preferred_element_type=jnp.float32)
    proj_bc = jnp.dot(normed, full_bc, preferred_element_type=jnp.float32)
    proj_dt = jnp.dot(normed, full_dt, preferred_element_type=jnp.float32)
    segs = segment_ids[None]

    def conv_part(x_raw, bc_raw, taps_x, bias_x, taps_bc, bias_bc):
        x_out = jax.nn.silu(causal_conv(x_raw[None], taps_x, bias_x, segs))[0]
        bc_out = jax.nn.silu(causal_conv(bc_raw[None], taps_bc, bias_bc, segs))[0]
        return (x_out, bc_out)

    (x_act, bc_act), conv_pull = jax.vjp(
        conv_part, proj_zx[1], proj_bc, conv_x, conv_bias_x, conv_bc, conv_bias_bc
    )

    def mixer(x_in, bc_in, gate_in, dt_in, bias_in, alog_in, skip_in):
        return gate_mix(
            x_in[None], bc_in[None], gate_in[None], dt_in[None], bias_in, alog_in, skip_in, segs
        )[0]

    gated, mixer_pull = jax.vjp(
        mixer, rounded(x_act), rounded(bc_act), proj_zx[0], proj_dt, dt_bias, a_log, d_skip
    )
    total_sq = lax.psum(jnp.sum(gated * gated, -1), "tensor")
    gate_scale = lax.rsqrt(total_sq / inner_all + epsilon)[:, None]
    normal = (gated * gate_scale * gate_gain).astype(jnp.bfloat16)
    summed = lax.psum(jnp.dot(normal, full_out, preferred_element_type=jnp.float32), "tensor")
    output = (inputs + summed).astype(jnp.bfloat16)
    cot_full = cotangent.astype(jnp.float32)
    grad_out = lax.dot_general(
        normal, cotangent, (((0,), (0,)), ((), ())), preferred_element_type=jnp.float32
    )
    d_normal = lax.dot_general(
        cotangent, full_out, (((1,), (1,)), ((), ())), preferred_element_type=jnp.float32
    )
    grad_gate = jnp.sum(d_normal * gated * gate_scale, 0)
    dot_total = lax.psum(jnp.sum(d_normal * gate_gain * gated, -1), "tensor")
    d_gated = (
        d_normal * gate_gain * gate_scale - gated * gate_scale**3 * dot_total[:, None] / inner_all
    )
    d_x_act, d_bc_act, d_gate_in, d_dt_in, grad_dt_bias, grad_a_log, grad_d_skip = mixer_pull(
        d_gated
    )
    d_x_raw, d_bc_raw, grad_conv_x, grad_bias_x, grad_conv_bc, grad_bias_bc = conv_pull(
        (d_x_act, d_bc_act)
    )
    bc_cols = full_bc.shape[1] // n_tensor
    col_start = tensor_index * bc_cols
    d_bc_full = lax.psum(d_bc_raw, "tensor")
    d_bc_own = lax.dynamic_slice_in_dim(d_bc_full, col_start, bc_cols, 1).astype(jnp.bfloat16)
    d_zx = jnp.stack([d_gate_in, d_x_raw]).astype(jnp.bfloat16)
    d_dt_low = d_dt_in.astype(jnp.bfloat16)
    w_bc_own = lax.dynamic_slice_in_dim(full_bc, col_start, bc_cols, 1)
    grad_zx = jnp.einsum("td,kti->kdi", normed, d_zx, preferred_element_type=jnp.float32)
    grad_dt = lax.dot_general(
        normed, d_dt_low, (((0,), (0,)), ((), ())), preferred_element_type=jnp.float32
    )
    grad_bc = lax.dot_general(
        normed, d_bc_own, (((0,), (0,)), ((), ())), preferred_element_type=jnp.float32
    )
    total = jnp.einsum("kti,kdi->td", d_zx, full_zx, preferred_element_type=jnp.float32)
    total = total + lax.dot_general(
        d_dt_low, full_dt, (((1,), (1,)), ((), ())), preferred_element_type=jnp.float32
    )
    d_norm_all = lax.psum(
        total
        + lax.dot_general(
            d_bc_own, w_bc_own, (((1,), (1,)), ((), ())), preferred_element_type=jnp.float32
        ),
        "tensor",
    )
    change, unused = norm_back(d_norm_all, inputs, scales, cot_full, pre_gain, width)
    grad_hidden = change.astype(jnp.bfloat16)
    grad_pre = jnp.sum(
        lax.dynamic_slice_in_dim(d_norm_all * inputs * scales, row_start, row_count, 0), 0
    )
    grad_zx, grad_dt, grad_out, grad_bc = (
        lax.psum_scatter(grad_zx, "dp", scatter_dimension=1, tiled=True),
        lax.psum_scatter(grad_dt, "dp", scatter_dimension=0, tiled=True),
        lax.psum_scatter(grad_out, "dp", scatter_dimension=1, tiled=True),
        lax.psum_scatter(grad_bc, "dp", scatter_dimension=0, tiled=True),
    )
    grad_conv_x, grad_bias_x, grad_dt_bias, grad_a_log, grad_d_skip, grad_gate = lax.psum(
        (grad_conv_x, grad_bias_x, grad_dt_bias, grad_a_log, grad_d_skip, grad_gate), "dp"
    )
    grad_conv_bc, grad_bias_bc, grad_pre = lax.psum(
        (grad_conv_bc, grad_bias_bc, grad_pre), ("dp", "tensor")
    )
    return (
        output,
        grad_hidden,
        grad_zx,
        grad_dt,
        grad_bc,
        grad_out,
        grad_conv_x,
        grad_bias_x,
        grad_conv_bc,
        grad_bias_bc,
        grad_dt_bias,
        grad_a_log,
        grad_d_skip,
        grad_pre,
        grad_gate,
    )


def solution(mesh):
    in_specs = (
        P("dp", None),
        P("dp"),
        P("dp", None),
        P(None, "dp", "tensor"),
        P("dp", "tensor"),
        P("dp", None),
        P("tensor", "dp"),
        P(None, "tensor"),
        P("tensor"),
        P(),
        P(),
        P("tensor"),
        P("tensor"),
        P("tensor"),
        P(),
        P("tensor"),
    )
    out_specs = (
        P("dp", None),
        P("dp", None),
        P(None, "dp", "tensor"),
        P("dp", "tensor"),
        P("dp", "tensor"),
        P("tensor", "dp"),
        P(None, "tensor"),
        P("tensor"),
        P(),
        P(),
        P("tensor"),
        P("tensor"),
        P("tensor"),
        P(),
        P("tensor"),
    )
    return jax.shard_map(local, mesh=mesh, in_specs=in_specs, out_specs=out_specs, check_vma=False)
```

profile of v0, /device:TPU:0, one launch (start us, length us, event | category | flops | bytes accessed | tf_op | source)
XLA Modules:
  0.0 1487.5 jit_solution(9202784934913625717)
XLA Ops:
  11.6 23.8 %all_gather.12 = bf16[2048,32]{0,1:T(8,128)(2,1)S(1)} all-gather(bf16[128,32]{0,1:T(8,128)(2,1)} %param.24), channel_id=1, replica_groups=mesh['dp'=16,'tensor'=2] {'dp'}, dimensions={0}, use_global_device_ids=true | all-gather | bytes 139264 | tf_op jit(solution)/shard_map/all_gather | solution.py:113
  42.2 8.6 all-gather.6.cloned.1.call-done
  56.4 122.7 %all-gather.4.cloned.1.call-done = bf16[2,2048,2048]{2,1,0:T(8,128)(2,1)} async-done(((bf16[2,128,2048]{2,1,0:T(8,128)(2,1)}), bf16[2,2048,2048]{2,1,0:T(8,128)(2,1)}) %all-gather.4.cloned.1.call-update) | async-done | bytes 16777232 | tf_op jit(solution)/shard_map/all_gather | solution.py:112
  179.0 11.7 convolution_bitcast_fusion.2
  194.0 5.1 fusion.169
  199.1 5.5 reshape.1214
  204.6 7.8 copy.266
  214.9 55.0 %while.46 = (s32[]{:T(128)}, f32[1,32,128,64]{2,3,1,0:T(8,128)S(1)}, s32[1]{0:T(128)}, f32[2,1,256,32,64]{2,4,3,1,0:T(8,128)}, f32[2,1,32,128,64]{3,4,2,1,0:T(8,...) while((s32[]{:T(128)}, ...), condition=%wide.region_4.5_spmd.clone, body=%wide.region_1.4_spmd.clone.sunk | while | flops 3336020992 | bytes 69288512 | solution.py:65
  228.7 9.6 fusion.275
  255.9 9.6 fusion.275
  269.9 9.1 copy.286
  279.0 7.8 reshape.1211
  286.8 5.6 fusion.154
  292.4 4.9 psum.98
  297.4 12.6 fusion.162
  309.9 4.9 psum.100
  314.9 10.2 fusion.152
  325.0 7.8 reshape.1212
  332.8 7.8 copy.277
  345.2 208.0 %while.47 = (s32[]{:T(128)}, f32[32]{0:T(128)}, f32[1,32,128,64]{2,3,1,0:T(8,128)}, f32[2,1,256,32,64]{2,4,3,1,0:T(8,128)}, f32[2,1,256,128]{3,2,0,1:T(8,128)}, ...) while((s32[]{:T(128)}, f32[32]{0:T(128)}, ...), condition=%wide.region_24.25_spmd.clone, body=%wide.region_10.24_spmd.clone.sunk | while | flops 7600219136 | bytes 66734348 | solution.py:65
  349.5 3.9 dynamic-slice_bitcast_fusion.9
  367.0 16.1 %fusion.294 = (f32[256,32]{0,1:T(8,128)}, f32[256,32]{0,1:T(8,128)}, f32[256,32]{0,1:T(8,128)}, f32[256,256]{1,0:T(8,128)}) fusion(f32[256,32]{0,1:T(8,128)} %copy.380, f32[256,32]{0,1:T(8,128)} %copy.381, f32[256,256]{1,0:T(8,128)S(1)} %fusion.293, pred[256,256]{1,0:T(8,128)(4,1)S(1)} %compare_and_fusion.2, ...), kind=kOutput, calls=%fused_computation.78.clone.1 | convolution fusion | flops 1641979904 | bytes 4947968 | tf_op jit(solution)/shard_map/transpose(jvp())/while/body/eval_jaxpr/checkpoint/gijh,gjhp->gihp/dot_general | solution.py:47
  395.2 5.4 fusion.296
  424.0 10.3 fusion.300
  438.9 4.7 fusion.302
  452.3 3.9 dynamic-slice_bitcast_fusion.9
  471.1 16.1 %fusion.294 = (f32[256,32]{0,1:T(8,128)}, f32[256,32]{0,1:T(8,128)}, f32[256,32]{0,1:T(8,128)}, f32[256,256]{1,0:T(8,128)}) fusion(f32[256,32]{0,1:T(8,128)} %copy.380, f32[256,32]{0,1:T(8,128)} %copy.381, f32[256,256]{1,0:T(8,128)S(1)} %fusion.293, pred[256,256]{1,0:T(8,128)(4,1)S(1)} %compare_and_fusion.2, ...), kind=kOutput, calls=%fused_computation.78.clone.1 | convolution fusion | flops 1641979904 | bytes 4947968 | tf_op jit(solution)/shard_map/transpose(jvp())/while/body/eval_jaxpr/checkpoint/gijh,gjhp->gihp/dot_general | solution.py:47
  499.3 5.4 fusion.296
  528.6 10.3 fusion.300
  543.6 4.7 fusion.302
  557.1 16.1 %all-reduce.30 = bf16[512,256]{1,0:T(8,128)(2,1)S(1)} all-reduce(f32[512,256]{1,0:T(8,128)S(1)} %fusion.172), channel_id=1, replica_groups=mesh['dp'=16,'tensor'=2] {'tensor'}, use_global_device_ids=true, to_apply=%region_25.26 | all-reduce | flops 131072 | bytes 786432 | tf_op jit(solution)/shard_map/psum | solution.py:171
  573.3 9.1 copy.289
  582.4 7.8 reshape.1213
  590.3 12.2 multiply_reduce_fusion.5
  602.6 6.4 broadcast_multiply_fusion.1
  609.3 9.4 fusion.151
  619.4 13.1 fusion.164
  635.9 9.8 fusion.190
  647.2 18.7 %convolution_bitcast_fusion.1 = f32[2,2048,2048]{1,2,0:T(8,128)} fusion(bf16[1,512,2048]{2,1,0:T(8,128)(2,1)} %fusion.151, bf16[1,512,2048]{2,1,0:T(8,128)(2,1)} %get-tuple-element.1043, bf16[512,2048]{1,0:T(8,128)(2,1)S(1)} %copy-done.7), kind=kOutput, calls=%fused_computation.179 | convolution fusion | flops 8592031744 | bytes 39845888 | tf_op jit(solution)/shard_map/td,kti->kdi/dot_general | solution.py:176
  669.3 13.4 fusion.188
  687.2 58.3 %all-reduce.24 = (f32[4,2048]{1,0:T(4,128)}, f32[2048]{0:T(1024)}, f32[32]{0:T(128)}, f32[32]{0:T(128)}, f32[32]{0:T(128)}, /*index=5*/f32[2048]{0:T(1024)}) all-reduce(f32[4,2048]{1,0:T(4,128)S(1)} %pad_add_fusion.6, f32[2048]{0:T(1024)S(1)} %get-tuple-element.931, ...), channel_id=1, replica_groups=mesh['dp'=16,'tensor'=2] {'dp'}, use_global_device_ids=true, to_apply=%region_36.37 | all-reduce | flops 12384 | bytes 99072 | tf_op jit(solution)/shard_map/psum | solution.py:205
  745.6 95.9 %all-reduce.29.cloned.1.call-done = (f32[512,2048]{1,0:T(8,128)}, f32[512,2048]{1,0:T(8,128)}) async-done(((f32[512,2048]{1,0:T(8,128)}, f32[512,2048]{1,0:T(8,128)}), (f32[512,2048]{1,0:T(8,128)}, f32[512,2048]{1,0:T(8,128)})) %all-reduce.29.cloned.1.call-update) | async-done | bytes 8388624 | tf_op jit(solution)/shard_map/psum | solution.py:149
  844.0 40.0 %all-reduce.23 = (f32[4,256]{1,0:T(4,128)}, f32[256]{0:T(256)}, f32[2048]{0:T(1024)}) all-reduce(f32[4,256]{1,0:T(4,128)S(1)} %pad_add_fusion.7, f32[256]{0:T(256)S(1)} %get-tuple-element.936, f32[2048]{0:T(1024)S(1)} %fusion.166), channel_id=1, replica_groups=mesh['dp'=16,'tensor'=2] {'dp','tensor'}, use_global_device_ids=true, to_apply=%region_43.44 | all-reduce | flops 3328 | bytes 26624 | tf_op jit(solution)/shard_map/psum | solution.py:208
  890.0 5.4 fusion.144
  895.5 283.1 %reduce-scatter.5.cloned.1.call-done = f32[2,128,2048]{1,2,0:T(8,128)} async-done(((f32[2,2048,2048]{1,2,0:T(8,128)}), f32[2,128,2048]{1,2,0:T(8,128)}) %reduce-scatter.5.cloned.1.call-update) | async-done | bytes 2097168 | tf_op jit(solution)/shard_map/reduce_scatter | solution.py:200
  1181.5 55.4 %reduce-scatter.7.cloned.1.call-done = f32[128,32]{0,1:T(8,128)} async-done(((f32[2048,32]{0,1:T(8,128)}), f32[128,32]{0,1:T(8,128)}) %reduce-scatter.7.cloned.1.call-update) | async-done | bytes 16400 | tf_op jit(solution)/shard_map/reduce_scatter | solution.py:201
  1236.9 60.7 %reduce-scatter.9.cloned.1.call-done = f32[128,128]{1,0:T(8,128)} async-done(((f32[2048,128]{1,0:T(8,128)}), f32[128,128]{1,0:T(8,128)}) %reduce-scatter.9.cloned.1.call-update) | async-done | bytes 65552 | tf_op jit(solution)/shard_map/reduce_scatter | solution.py:203
  1297.6 182.8 %reduce-scatter.11.cloned.1.call-done = f32[2048,128]{1,0:T(8,128)} async-done(((f32[2048,2048]{1,0:T(8,128)}), f32[2048,128]{1,0:T(8,128)}) %reduce-scatter.11.cloned.1.call-update) | async-done | bytes 1048592 | tf_op jit(solution)/shard_map/reduce_scatter | solution.py:202
  (377 shorter events, 211.8 us)
Async XLA Ops:
  7.2 29.4 %copy-start.2 = (bf16[512,2048]{1,0:T(8,128)(2,1)S(1)}, bf16[512,2048]{1,0:T(8,128)(2,1)}, u32[]{:S(2)}) copy-start(bf16[512,2048]{1,0:T(8,128)(2,1)} %param.20) | copy-start | bytes 6291460
  7.2 32.0 %copy-start.63 = (f32[32]{0:T(128)S(1)}, f32[32]{0:T(128)}, u32[]{:S(2)}) copy-start(f32[32]{0:T(128)} %param.31) | copy-start | bytes 388
  7.2 43.7 %all-gather.6.cloned.1.call-start = ((), (), s32[]{:S(2)}) async-start(), calls=%async_computation.5 | async-start | bytes 1114112 | tf_op jit(solution)/shard_map/all_gather | solution.py:114
  7.9 171.1 %all-gather.4.cloned.1.call-start = ((), (), s32[]{:S(2)}) async-start(), calls=%async_computation.4 | async-start | bytes 17825792 | tf_op jit(solution)/shard_map/all_gather | solution.py:112
  8.7 288.7 %all-gather.8.cloned.1.call-start = ((), (), s32[]{:S(2)}) async-start(), calls=%async_computation.6 | async-start | bytes 8912896 | tf_op jit(solution)/shard_map/all_gather | solution.py:115
  9.4 31.8 %copy-start.64 = (f32[32]{0:T(128)S(1)}, f32[32]{0:T(128)}, u32[]{:S(2)}) copy-start(f32[32]{0:T(128)} %param.33) | copy-start | bytes 388
  9.4 32.0 %copy-start.65 = (f32[32]{0:T(128)S(1)}, f32[32]{0:T(128)}, u32[]{:S(2)}) copy-start(f32[32]{0:T(128)} %param.32) | copy-start | bytes 388
  9.4 32.5 %copy-start.26 = (s32[512]{0:T(512)S(1)}, s32[512]{0:T(512)}, u32[]{:S(2)}) copy-start(s32[512]{0:T(512)} %param.21) | copy-start | bytes 6148
  9.5 32.6 %copy-start.61 = (f32[4,256]{1,0:T(4,128)S(1)}, f32[4,256]{1,0:T(4,128)}, u32[]{:S(2)}) copy-start(f32[4,256]{1,0:T(4,128)} %param.29) | copy-start | bytes 12292
  9.5 32.6 %copy-start.46 = (f32[4,2048]{1,0:T(4,128)S(1)}, f32[4,2048]{1,0:T(4,128)}, u32[]{:S(2)}) copy-start(f32[4,2048]{1,0:T(4,128)} %param.27) | copy-start | bytes 98308
  9.5 832.0 %all-reduce.29.cloned.1.call-start = ((), (), s32[]{:S(2)}) async-start(), calls=%async_computation.11 | async-start | bytes 16777216 | tf_op jit(solution)/shard_map/psum | solution.py:149
  39.2 15.1 %copy-start.62 = (f32[256]{0:T(256)S(1)}, f32[256]{0:T(256)}, u32[]{:S(2)}) copy-start(f32[256]{0:T(256)} %param.30) | copy-start | bytes 3076
  40.6 138.4 %copy-start.6 = (bf16[512,2048]{1,0:T(8,128)(2,1)S(1)}, bf16[512,2048]{1,0:T(8,128)(2,1)}, u32[]{:S(2)}) copy-start(bf16[512,2048]{1,0:T(8,128)(2,1)} %copy-done.5) | copy-start | bytes 6291460
  41.4 273.5 %copy-start.27 = (f32[2048]{0:T(1024)}, f32[2048]{0:T(1024)S(1)}, u32[]{:S(2)}) copy-start(f32[2048]{0:T(1024)S(1)} %mul.1178) | copy-start | bytes 24580
  42.1 151.9 %copy-start.29 = (f32[1,512]{1,0:T(1,128)}, f32[1,512]{1,0:T(1,128)S(1)}, u32[]{:S(2)}) copy-start(f32[1,512]{1,0:T(1,128)S(1)} %get-tuple-element.1068) | copy-start | bytes 6148
  42.1 151.9 %copy-start.31 = (f32[1,512]{1,0:T(1,128)}, f32[1,512]{1,0:T(1,128)S(1)}, u32[]{:S(2)}) copy-start(f32[1,512]{1,0:T(1,128)S(1)} %get-tuple-element.1069) | copy-start | bytes 6148
  42.1 151.9 %copy-start.33 = (f32[1,512]{1,0:T(1,128)}, f32[1,512]{1,0:T(1,128)S(1)}, u32[]{:S(2)}) copy-start(f32[1,512]{1,0:T(1,128)S(1)} %get-tuple-element.1070) | copy-start | bytes 6148
  42.1 148.6 %copy-start.50 = (f32[1,256]{1,0:T(1,128)}, f32[1,256]{1,0:T(1,128)S(1)}, u32[]{:S(2)}) copy-start(f32[1,256]{1,0:T(1,128)S(1)} %get-tuple-element.1060) | copy-start | bytes 3076
  42.1 148.6 %copy-start.51 = (f32[1,256]{1,0:T(1,128)}, f32[1,256]{1,0:T(1,128)S(1)}, u32[]{:S(2)}) copy-start(f32[1,256]{1,0:T(1,128)S(1)} %get-tuple-element.1061) | copy-start | bytes 3076
  42.1 148.6 %copy-start.52 = (f32[1,256]{1,0:T(1,128)}, f32[1,256]{1,0:T(1,128)S(1)}, u32[]{:S(2)}) copy-start(f32[1,256]{1,0:T(1,128)S(1)} %get-tuple-element.1062) | copy-start | bytes 3076
  42.1 148.6 %copy-start.53 = (f32[1,256]{1,0:T(1,128)}, f32[1,256]{1,0:T(1,128)S(1)}, u32[]{:S(2)}) copy-start(f32[1,256]{1,0:T(1,128)S(1)} %get-tuple-element.1063) | copy-start | bytes 3076
  42.2 151.8 %copy-start.36 = (f32[1,2048]{1,0:T(1,128)}, f32[1,2048]{1,0:T(1,128)S(1)}, u32[]{:S(2)}) copy-start(f32[1,2048]{1,0:T(1,128)S(1)} %get-tuple-element.1056) | copy-start | bytes 24580
  42.2 151.8 %copy-start.38 = (f32[1,2048]{1,0:T(1,128)}, f32[1,2048]{1,0:T(1,128)S(1)}, u32[]{:S(2)}) copy-start(f32[1,2048]{1,0:T(1,128)S(1)} %get-tuple-element.1057) | copy-start | bytes 24580
  42.2 151.8 %copy-start.40 = (f32[1,2048]{1,0:T(1,128)}, f32[1,2048]{1,0:T(1,128)S(1)}, u32[]{:S(2)}) copy-start(f32[1,2048]{1,0:T(1,128)S(1)} %get-tuple-element.1058) | copy-start | bytes 24580
  42.2 151.8 %copy-start.42 = (f32[1,2048]{1,0:T(1,128)}, f32[1,2048]{1,0:T(1,128)S(1)}, u32[]{:S(2)}) copy-start(f32[1,2048]{1,0:T(1,128)S(1)} %get-tuple-element.1059) | copy-start | bytes 24580
  297.4 17.5 %copy-start.58 = (f32[512]{0:T(512)}, f32[512]{0:T(512)S(1)}, u32[]{:S(2)}) copy-start(f32[512]{0:T(512)S(1)} %get-tuple-element.1067) | copy-start | bytes 6148
  366.0 17.1 %copy-start.17 = (f32[256,256]{1,0:T(8,128)}, f32[256,256]{1,0:T(8,128)S(1)}, u32[]{:S(2)}) copy-start(f32[256,256]{1,0:T(8,128)S(1)} %fusion.293) | copy-start | bytes 786436 | tf_op jit(solution)/shard_map/transpose(jvp())/while
  367.0 16.1 %copy-start.20 = (pred[256,256]{1,0:T(8,128)(4,1)}, pred[256,256]{1,0:T(8,128)(4,1)S(1)}, u32[]{:S(2)}) copy-start(pred[256,256]{1,0:T(8,128)(4,1)S(1)} %compare_and_fusion.2) | copy-start | bytes 196612 | tf_op jit(solution)/shard_map/transpose(jvp())/while
  424.0 10.7 copy-start.18
  434.3 12.2 copy-start.4
  434.3 12.2 copy-start.44
  470.0 17.1 %copy-start.17 = (f32[256,256]{1,0:T(8,128)}, f32[256,256]{1,0:T(8,128)S(1)}, u32[]{:S(2)}) copy-start(f32[256,256]{1,0:T(8,128)S(1)} %fusion.293) | copy-start | bytes 786436 | tf_op jit(solution)/shard_map/transpose(jvp())/while
  471.1 16.1 %copy-start.20 = (pred[256,256]{1,0:T(8,128)(4,1)}, pred[256,256]{1,0:T(8,128)(4,1)S(1)}, u32[]{:S(2)}) copy-start(pred[256,256]{1,0:T(8,128)(4,1)S(1)} %compare_and_fusion.2) | copy-start | bytes 196612 | tf_op jit(solution)/shard_map/transpose(jvp())/while
  528.6 10.8 copy-start
  528.6 10.8 copy-start.18
  539.0 12.2 copy-start.4
  539.0 12.2 copy-start.44
  590.2 12.3 copy-start.37
  590.2 12.3 copy-start.39
  590.2 12.3 copy-start.41
  590.3 12.3 copy-start.43
  619.4 13.1 copy-start.22
  645.7 532.9 %reduce-scatter.5.cloned.1.call-start = ((), (), s32[]{:S(2)}) async-start(), calls=%async_computation.7 | async-start | bytes 35651584 | tf_op jit(solution)/shard_map/reduce_scatter | solution.py:200
  665.9 571.0 %reduce-scatter.7.cloned.1.call-start = ((), (), s32[]{:S(2)}) async-start(), calls=%async_computation.8 | async-start | bytes 278528 | tf_op jit(solution)/shard_map/reduce_scatter | solution.py:201
  667.2 630.4 %reduce-scatter.9.cloned.1.call-start = ((), (), s32[]{:S(2)}) async-start(), calls=%async_computation.9 | async-start | bytes 1114112 | tf_op jit(solution)/shard_map/reduce_scatter | solution.py:203
  669.0 811.4 %reduce-scatter.11.cloned.1.call-start = ((), (), s32[]{:S(2)}) async-start(), calls=%async_computation.10 | async-start | bytes 17825792 | tf_op jit(solution)/shard_map/reduce_scatter | solution.py:202
  684.3 199.7 %copy-start.35 = (f32[2048]{0:T(1024)S(1)}, f32[2048]{0:T(1024)}, u32[]{:S(2)}) copy-start(f32[2048]{0:T(1024)} %param.34) | copy-start | bytes 24580
  844.0 43.8 %copy-start.57 = (f32[512]{0:T(512)S(1)}, f32[512]{0:T(512)}, u32[]{:S(2)}) copy-start(f32[512]{0:T(512)} %get-tuple-element.1064) | copy-start | bytes 6148
  (38 other events, 201.0 us)
Sparse Core Ops, SparseCore 0:
  10.2 40.6 all-gather.5
  53.1 125.8 all-gather.3
  181.2 76.2 all-gather.7
  645.8 195.6 all-reduce.28
  845.6 332.9 reduce-scatter.4
  1182.5 54.3 reduce-scatter.6
  1241.1 56.4 reduce-scatter.8
  1302.9 177.5 reduce-scatter.10
where the time goes:
time: 1500 us; the launch traced here: 1490 us
  waiting for transfers between devices  811 us (54%)
  matrix products  223 us (15%)
  local copies, waits for them, and re-layouts  157 us (10%)
  blocking collectives  148 us (10%)
  other arithmetic  126 us (8%)
  between operations  15.1 us (1%)
    reduce_scatter x1, waiting for transfers between devices, local(): lax.psum_scatter(grad_zx, 'dp', scatter_dimension=1, tiled=True)  283 us
    reduce_scatter x1, waiting for transfers between devices, local(): lax.psum_scatter(grad_out, 'dp', scatter_dimension=1, tiled=True)  183 us
    all_gather x1, waiting for transfers between devices, local(): lax.all_gather(w_zx, 'dp', axis=1, tiled=True)  123 us
    psum x1, waiting for transfers between devices, local(): lax.psum(jnp.dot(normal, full_out, preferred_element_type=jnp.float32), '...  95.9 us
    dot_general x6, matrix products, one_block(): intra = jnp.einsum('gijh,gjhp->gihp', mixing, x_blk, precision=highest)  72.1 us
    reduce_scatter x1, waiting for transfers between devices, local(): lax.psum_scatter(grad_bc, 'dp', scatter_dimension=0, tiled=True)  60.7 us
    psum x1, blocking collectives, local(): lax.psum((grad_conv_x, grad_bias_x, grad_dt_bias, grad_a_log, grad_d_skip...  58.3 us
    reduce_scatter x1, waiting for transfers between devices, local(): lax.psum_scatter(grad_dt, 'dp', scatter_dimension=0, tiled=True)  55.4 us
  transfers between devices with their start and end apart: 8, of which 7 were waited for; matrix products, arithmetic and copies ran while one was open for 11% of the time, Pallas kernels for 0%

commit v1 on v0

v1 whole, which is shorter than its diff:
```python
import functools

import jax
import jax.numpy as jnp
import numpy as np
from jax import lax
from jax.experimental import pallas as pl
from jax.experimental.pallas import tpu as pltpu
from jax.sharding import PartitionSpec as P

EPS = 1e-05
Q = 128
NEG = -1e30
F32 = jnp.float32
BF16 = jnp.bfloat16
HIGH = lax.Precision.HIGHEST
VMEM_LIMIT = 56 * 1024 * 1024


def dot(a, b, dims, precision=None):
    return lax.dot_general(a, b, (dims, ((), ())), precision=precision, preferred_element_type=F32)


def params():
    return pltpu.CompilerParams(vmem_limit_bytes=VMEM_LIMIT)


def ring_order(chips):
    if chips == 8:
        return [0, 2, 4, 6, 7, 5, 3, 1]
    half = chips // 2
    return list(range(half)) + list(range(chips - 1, half - 1, -1))


class Ring:
    def __init__(self, n_dp):
        self.n = n_dp // 2
        self.order = ring_order(self.n)
        place = [0] * self.n
        for position, chip in enumerate(self.order):
            place[chip] = position
        me = lax.axis_index("dp")
        self.core = me % 2
        self.pos = jnp.asarray(place, jnp.int32)[me // 2]
        self.right = self.perm(1)
        self.left = self.perm(-1)
        self.full = self.n // 2 - 1

    def perm(self, step):
        pairs = []
        for p in range(self.n):
            for c in range(2):
                pairs.append((self.order[p] * 2 + c, self.order[(p + step) % self.n] * 2 + c))
        return pairs

    def chip(self, step):
        return jnp.asarray(self.order, jnp.int32)[(self.pos + step) % self.n]

    def go_right(self, v):
        return lax.ppermute(v, "dp", self.right)

    def go_left(self, v):
        return lax.ppermute(v, "dp", self.left)

    def swap(self, v):
        return lax.ppermute(v, "dp", [(i, i ^ 1) for i in range(2 * self.n)])

    def chip_sum(self, v):
        dist = 2
        while dist < 2 * self.n:
            v = v + lax.ppermute(v, "dp", [(i, i ^ dist) for i in range(2 * self.n)])
            dist *= 2
        return v


def half_rows(rows):
    return (rows // 2 + 15) // 16 * 16


def ring_gather(ring, unit):
    h = half_rows(unit.shape[0])
    r, l = [unit], [unit]
    for _ in range(ring.full):
        r.append(ring.go_right(r[-1]))
        l.append(ring.go_left(l[-1]))
    top = ring.go_right(r[-1][:h])
    bottom = ring.go_left(l[-1][h:])
    return [unit] + r[1:] + l[1:] + [top, bottom]


def gather_steps(ring):
    return [0] + [-k for k in range(1, ring.full + 1)] + list(range(1, ring.full + 1)) + [ring.n // 2]


def ring_scatter(ring, block, rows):
    h = half_rows(rows)
    far = block(ring.n // 2)
    r = ring.go_right(far[:h].astype(BF16))
    l = ring.go_left(far[h:].astype(BF16))
    for j in range(ring.full, 0, -1):
        br, bl = block(j), block(-j)
        if j == ring.full:
            br = jnp.concatenate([br[:h] + r.astype(F32), br[h:]])
            bl = jnp.concatenate([bl[:h], bl[h:] + l.astype(F32)])
        else:
            br = br + r.astype(F32)
            bl = bl + l.astype(F32)
        r = ring.go_right(br.astype(BF16))
        l = ring.go_left(bl.astype(BF16))
    return block(0) + r.astype(F32) + l.astype(F32)


def proj_kernel(n_blocks, dd, offs, *refs):
    blocks, act, out = refs[:n_blocks], refs[n_blocks], refs[n_blocks + 1]
    pieces, cols = [], []
    for b in range(n_blocks - 2):
        pieces.append(blocks[b][...])
    pieces.append(jnp.concatenate([blocks[-2][...], blocks[-1][...]], axis=0))
    for b in range(n_blocks - 1):
        off = pl.multiple_of(offs[b], dd)
        cols.append(act[:, pl.ds(off, dd)])
    out[...] = dot(
        jnp.concatenate(pieces, axis=1), jnp.concatenate(cols, axis=1), (((1,), (1,)))
    )


def proj(blocks, act, offs):
    rows, dd = blocks[0].shape
    tokens, width = act.shape
    tile = 256
    n = len(blocks)
    specs = [pl.BlockSpec(b.shape, lambda i, o: (0, 0)) for b in blocks]
    return pl.pallas_call(
        functools.partial(proj_kernel, n, dd),
        out_shape=jax.ShapeDtypeStruct((rows, tokens), F32),
        grid_spec=pltpu.PrefetchScalarGridSpec(
            num_scalar_prefetch=1,
            grid=(tokens // tile,),
            in_specs=specs + [pl.BlockSpec((tile, width), lambda i, o: (i, 0))],
            out_specs=pl.BlockSpec((rows, tile), lambda i, o: (0, i)),
        ),
        compiler_params=params(),
        cost_estimate=pl.CostEstimate(
            flops=2 * rows * tokens * width,
            bytes_accessed=2 * rows * width + 2 * tokens * width + 4 * rows * tokens,
            transcendentals=0,
        ),
    )(offs, *blocks, act)


def back_kernel(sizes, dd, offs, *refs):
    out = refs[-1]
    at = 0
    groups = []
    for n_blocks in sizes:
        blocks = refs[at : at + n_blocks]
        vt = refs[at + n_blocks]
        at += n_blocks + 1
        groups.append((blocks, vt[...].T))
    for b in range(sizes[0] - 1):
        off = pl.multiple_of(offs[b], dd)
        total = None
        for blocks, v in groups:
            w = blocks[b][...]
            if b == len(blocks) - 2:
                w = jnp.concatenate([w, blocks[b + 1][...]], axis=0)
            part = dot(v, w, (((1,), (0,))))
            total = part if total is None else total + part
        out[:, pl.ds(off, dd)] = total.astype(out.dtype)


def back(groups, offs, width):
    dd = groups[0][0][0].shape[1]
    tokens = groups[0][1].shape[1]
    tile = 256
    args, specs = [], []
    flops = 0
    for blocks, vt in groups:
        args += list(blocks) + [vt]
        specs += [pl.BlockSpec(b.shape, lambda i, o: (0, 0)) for b in blocks]
        specs += [pl.BlockSpec((vt.shape[0], tile), lambda i, o: (0, i))]
        flops += 2 * vt.shape[0] * tokens * width
    return pl.pallas_call(
        functools.partial(back_kernel, [len(g[0]) for g in groups], dd),
        out_shape=jax.ShapeDtypeStruct((tokens, width), BF16),
        grid_spec=pltpu.PrefetchScalarGridSpec(
            num_scalar_prefetch=1,
            grid=(tokens // tile,),
            in_specs=specs,
            out_specs=pl.BlockSpec((tile, width), lambda i, o: (i, 0)),
        ),
        compiler_params=params(),
        cost_estimate=pl.CostEstimate(
            flops=flops, bytes_accessed=flops // 1024 + 2 * tokens * width, transcendentals=0
        ),
    )(offs, *args)


HEAD = 64
STATE = 128


def head_terms(raw, hp_ref):
    pre = raw + hp_ref[:, 0:1]
    small = jnp.exp(-jnp.abs(pre))
    one = 1.0 + small
    away = one - 1.0
    log1p = jnp.where(away == 0.0, small, jnp.log(one) * (small / jnp.where(away == 0.0, 1.0, away)))
    dt = jnp.maximum(pre, 0.0) + log1p
    logistic = jnp.where(pre >= 0.0, 1.0, small) / one
    rows = lax.broadcasted_iota(jnp.int32, (Q, Q), 0)
    lanes = lax.broadcasted_iota(jnp.int32, (Q, Q), 1)
    upto = (rows <= lanes).astype(F32)
    logs = dt * hp_ref[:, 1:2]
    cums = dot(logs, upto, (((1,), (0,))), HIGH)
    return dt, logistic, cums


def to_columns(cums):
    n = cums.shape[0]
    square = jnp.concatenate([cums, jnp.zeros((Q - n, Q), F32)], axis=0)
    return square.T


def pair_bias(segr_ref, segc_ref):
    rows = lax.broadcasted_iota(jnp.int32, (Q, Q), 0)
    lanes = lax.broadcasted_iota(jnp.int32, (Q, Q), 1)
    keep = (segc_ref[...] == segr_ref[...]) & (rows <= lanes)
    return jnp.where(keep, 0.0, NEG)


def fwd_kernel(
    heads, xr_ref, mask_ref, segr_ref, segc_ref, par_ref, hp_ref,
    y_ref, xa_ref, u_ref, s_ref, prev, state, parb, xt,
):
    first = (pl.program_id(0) == 0) & (pl.program_id(1) == 0)
    chans = heads * HEAD
    wide = chans + 2 * STATE

    @pl.when(first)
    def _():
        for k in range(6):
            parb[k] = jnp.broadcast_to(par_ref[:, k : k + 1], (wide, Q))

    @pl.when(pl.program_id(1) == 0)
    def _():
        prev[...] = jnp.zeros_like(prev)
        state[...] = jnp.zeros_like(state)

    lane = lax.broadcasted_iota(jnp.int32, (HEAD, Q), 1)
    m1, m2, m3 = mask_ref[0:1, :], mask_ref[1:2, :], mask_ref[2:3, :]

    def conv(r0):
        rows = slice(r0, r0 + HEAD)
        cur = xr_ref[rows, :]
        old = prev[rows, :]
        u = parb[4, rows, :] + parb[3, rows, :] * cur
        u = u + parb[2, rows, :] * (m1 * pltpu.roll(jnp.where(lane >= Q - 1, old, cur), 1, 1))
        u = u + parb[1, rows, :] * (m2 * pltpu.roll(jnp.where(lane >= Q - 2, old, cur), 2, 1))
        u = u + parb[0, rows, :] * (m3 * pltpu.roll(jnp.where(lane >= Q - 3, old, cur), 3, 1))
        prev[rows, :] = cur
        u_ref[rows, :] = u
        xa = (u * (0.5 * jnp.tanh(0.5 * u) + 0.5)).astype(BF16)
        xa_ref[rows, :] = xa
        return xa

    for r0 in range(chans, wide, HEAD):
        conv(r0)
    bt = xa_ref[chans : chans + STATE, :]
    ct = xa_ref[chans + STATE : wide, :]
    mix = dot(bt.T, ct, (((1,), (0,))))
    dt, _, cums = head_terms(xr_ref[wide:, :], hp_ref)
    cols = to_columns(cums)
    bias = pair_bias(segr_ref, segc_ref)
    enter = jnp.exp(cums) * mask_ref[3:4, :]
    last = jnp.broadcast_to(cums[:, Q - 1 : Q], cums.shape)
    tail = jnp.exp(last - cums) * mask_ref[4:5, :]
    passing = jnp.exp(last) * mask_ref[5:6, :]
    s_in = state[...].astype(BF16)
    s_ref[...] = s_in
    carried = dot(s_in, ct, (((1,), (0,))))
    for h in range(heads):
        rows = slice(h * HEAD, (h + 1) * HEAD)
        xa = conv(h * HEAD).astype(F32)
        decay = jnp.exp(cums[h : h + 1, :] - cols[:, h : h + 1] + bias)
        mixing = (mix * decay).astype(BF16)
        xd = xa * dt[h : h + 1, :]
        xt[rows, :] = (xd * tail[h : h + 1, :]).astype(BF16)
        y = dot(xd.astype(BF16), mixing, (((1,), (0,))))
        y = y + enter[h : h + 1, :] * carried[rows, :] + parb[5, rows, :] * xa
        y_ref[rows, :] = y
    fresh = dot(xt[...], bt, (((1,), (1,))))
    for h in range(heads):
        rows = slice(h * HEAD, (h + 1) * HEAD)
        state[rows, :] = state[rows, :] * passing[h : h + 1, :] + fresh[rows, :]


def scan_forward(xr, masks, segr, segc, par, hp, heads, seqs):
    rows, tokens = xr.shape
    chans = heads * HEAD
    wide = chans + 2 * STATE
    count = tokens // seqs // Q
    at = lambda s, k: (0, s * count + k)
    whole = lambda s, k: (0, 0)
    return pl.pallas_call(
        functools.partial(fwd_kernel, heads),
        grid=(seqs, count),
        out_shape=(
            jax.ShapeDtypeStruct((chans, tokens), F32),
            jax.ShapeDtypeStruct((wide, tokens), BF16),
            jax.ShapeDtypeStruct((wide, tokens), F32),
            jax.ShapeDtypeStruct((chans, tokens), BF16),
        ),
        in_specs=[
            pl.BlockSpec((rows, Q), at),
            pl.BlockSpec((8, Q), at),
            pl.BlockSpec((1, Q), at),
            pl.BlockSpec((Q, 1), lambda s, k: (s * count + k, 0)),
            pl.BlockSpec(par.shape, whole),
            pl.BlockSpec(hp.shape, whole),
        ],
        out_specs=(
            pl.BlockSpec((chans, Q), at),
            pl.BlockSpec((wide, Q), at),
            pl.BlockSpec((wide, Q), at),
            pl.BlockSpec((chans, STATE), at),
        ),
        scratch_shapes=[
            pltpu.VMEM((wide, Q), F32),
            pltpu.VMEM((chans, STATE), F32),
            pltpu.VMEM((6, wide, Q), F32),
            pltpu.VMEM((chans, Q), BF16),
        ],
        compiler_params=params(),
        cost_estimate=pl.CostEstimate(
            flops=20_000_000_000, bytes_accessed=18 * wide * tokens, transcendentals=0
        ),
    )(xr, masks, segr, segc, par, hp)


def bwd_kernel(
    heads, xr_ref, mask_ref, segr_ref, segc_ref, par_ref, hp_ref, xa_ref, u_ref, s_ref, dy_ref, y_ref,
    dx_ref, dbc_ref, ddt_ref, cg_ref, hg_ref,
    dstate, parb, after, nmask, xt, dye,
):
    first = (pl.program_id(0) == 0) & (pl.program_id(1) == 0)
    chans = heads * HEAD
    wide = chans + 2 * STATE

    @pl.when(first)
    def _():
        for k in range(6):
            parb[k] = jnp.broadcast_to(par_ref[:, k : k + 1], (wide, Q))
        cg_ref[...] = jnp.zeros_like(cg_ref)
        hg_ref[...] = jnp.zeros_like(hg_ref)

    @pl.when(pl.program_id(1) == 0)
    def _():
        dstate[...] = jnp.zeros_like(dstate)
        after[...] = jnp.zeros_like(after)
        nmask[...] = jnp.zeros_like(nmask)

    lane = lax.broadcasted_iota(jnp.int32, (HEAD, Q), 1)
    lane8 = lax.broadcasted_iota(jnp.int32, (8, Q), 1)
    sub8 = lax.broadcasted_iota(jnp.int32, (8, Q), 0)
    masks = mask_ref[...]
    shifted_masks = jnp.where(lane8 <= sub8, nmask[...], masks)
    nmask[...] = masks

    def conv_back(r0, dxa, out, out0):
        rows = slice(r0, r0 + HEAD)
        u = u_ref[rows, :]
        sig = 0.5 * jnp.tanh(0.5 * u) + 0.5
        dc = dxa * (sig * (1.0 + u * (1.0 - sig)))
        xr = xr_ref[rows, :]
        old = after[rows, :]
        after[rows, :] = dc
        dx = parb[3, rows, :] * dc
        cg_ref[4, rows, :] += dc
        cg_ref[3, rows, :] += xr * dc
        for k in (1, 2, 3):
            e = jnp.where(lane < k, old, dc) * shifted_masks[k - 1 : k, :]
            e = pltpu.roll(e, Q - k, 1)
            dx = dx + parb[3 - k, rows, :] * e
            cg_ref[3 - k, rows, :] += xr * e
        out[out0 : out0 + HEAD, :] = dx.astype(out.dtype)

    bt = xa_ref[chans : chans + STATE, :]
    ct = xa_ref[chans + STATE : wide, :]
    mix = dot(bt.T, ct, (((1,), (0,))))
    dt, logistic, cums = head_terms(xr_ref[wide:, :], hp_ref)
    cols = to_columns(cums)
    bias = pair_bias(segr_ref, segc_ref)
    enter = jnp.exp(cums) * masks[3:4, :]
    last = jnp.broadcast_to(cums[:, Q - 1 : Q], cums.shape)
    tail = jnp.exp(last - cums) * masks[4:5, :]
    passing = jnp.exp(last) * masks[5:6, :]
    ds = dstate[...].astype(BF16)
    spread = dot(ds, bt, (((1,), (0,))))
    dmix = jnp.zeros((Q, Q), F32)
    s_in = s_ref[...]
    direct, cross, skip, outward, through, inward = [], [], [], [], [], []
    for h in range(heads):
        rows = slice(h * HEAD, (h + 1) * HEAD)
        xa = xa_ref[rows, :].astype(F32)
        dyb = dy_ref[rows, :]
        dy = dyb.astype(F32)
        decay = jnp.exp(cums[h : h + 1, :] - cols[:, h : h + 1] + bias)
        mixing = (mix * decay).astype(BF16)
        xd = xa * dt[h : h + 1, :]
        xdb = xd.astype(BF16)
        xt[rows, :] = (xd * tail[h : h + 1, :]).astype(BF16)
        dye[rows, :] = (dy * enter[h : h + 1, :]).astype(BF16)
        dmix = dmix + dot(xdb, dyb, (((0,), (0,)))) * decay
        near = dot(dyb, mixing, (((1,), (1,))))
        far = tail[h : h + 1, :] * spread[rows, :]
        pull = near + far
        direct.append(jnp.sum(xa * pull, axis=0, keepdims=True))
        cross.append(jnp.sum(xdb.astype(F32) * near, axis=0, keepdims=True))
        outward.append(jnp.sum(xd * far, axis=0, keepdims=True))
        through.append(jnp.sum(dstate[rows, :] * s_in[rows, :].astype(F32), axis=0, keepdims=True))
        skip.append(jnp.sum(xa * dy, axis=0, keepdims=True))
        inward.append(jnp.sum(y_ref[rows, :] * dy, axis=0, keepdims=True))
        dxa = dt[h : h + 1, :] * pull + parb[5, rows, :] * dy
        conv_back(h * HEAD, dxa, dx_ref, h * HEAD)
    pad = ddt_ref.shape[0] - heads
    if pad:
        zero = [jnp.zeros((pad, Q), F32)]
        direct, cross, skip = direct + zero, cross + zero, skip + zero
        outward, through, inward = outward + zero, through + zero, inward + zero
    direct, cross, skip, outward, through, inward = (
        jnp.concatenate(v, axis=0) for v in (direct, cross, skip, outward, through, inward)
    )
    dlog = inward - hp_ref[:, 2:3] * skip - cross
    rows = lax.broadcasted_iota(jnp.int32, (Q, Q), 0)
    lanes = lax.broadcasted_iota(jnp.int32, (Q, Q), 1)
    dl = dot(dlog, (rows >= lanes).astype(F32), (((1,), (0,))), HIGH)
    dl = dl + dot(outward, (rows < lanes).astype(F32), (((1,), (0,))), HIGH)
    dl = dl + passing * jnp.sum(through, axis=1, keepdims=True)
    ddt = (direct + hp_ref[:, 1:2] * dl) * logistic
    ddt_ref[...] = ddt
    hg_ref[0] += ddt
    hg_ref[1] += dt * dl
    hg_ref[2] += skip
    dmixb = dmix.astype(BF16)
    xtv, dyev = xt[...], dye[...]
    dbt = dot(ct, dmixb, (((1,), (1,)))) + dot(ds, xtv, (((0,), (0,))))
    dct = dot(bt, dmixb, (((1,), (0,)))) + dot(s_ref[...], dyev, (((0,), (0,))))
    dbca = jnp.concatenate([dbt, dct], axis=0)
    for r0 in range(0, 2 * STATE, HEAD):
        conv_back(chans + r0, dbca[r0 : r0 + HEAD, :], dbc_ref, r0)
    fresh = dot(dyev, ct, (((1,), (1,))))
    for h in range(heads):
        rows = slice(h * HEAD, (h + 1) * HEAD)
        dstate[rows, :] = dstate[rows, :] * passing[h : h + 1, :] + fresh[rows, :]


def scan_backward(xr, masks, segr, segc, par, hp, xa, u, s_in, dy, y, heads, seqs):
    rows, tokens = xr.shape
    chans = heads * HEAD
    wide = chans + 2 * STATE
    count = tokens // seqs // Q
    padded = rows - wide
    at = lambda s, k: (0, s * count + count - 1 - k)
    whole = lambda s, k: (0, 0)
    whole3 = lambda s, k: (0, 0, 0)
    return pl.pallas_call(
        functools.partial(bwd_kernel, heads),
        grid=(seqs, count),
        out_shape=(
            jax.ShapeDtypeStruct((chans, tokens), BF16),
            jax.ShapeDtypeStruct((2 * STATE, tokens), F32),
            jax.ShapeDtypeStruct((padded, tokens), F32),
            jax.ShapeDtypeStruct((5, wide, Q), F32),
            jax.ShapeDtypeStruct((3, padded, Q), F32),
        ),
        in_specs=[
            pl.BlockSpec((rows, Q), at),
            pl.BlockSpec((8, Q), at),
            pl.BlockSpec((1, Q), at),
            pl.BlockSpec((Q, 1), lambda s, k: (s * count + count - 1 - k, 0)),
            pl.BlockSpec(par.shape, whole),
            pl.BlockSpec(hp.shape, whole),
            pl.BlockSpec((wide, Q), at),
            pl.BlockSpec((wide, Q), at),
            pl.BlockSpec((chans, STATE), at),
            pl.BlockSpec((chans, Q), at),
            pl.BlockSpec((chans, Q), at),
        ],
        out_specs=(
            pl.BlockSpec((chans, Q), at),
            pl.BlockSpec((2 * STATE, Q), at),
            pl.BlockSpec((padded, Q), at),
            pl.BlockSpec((5, wide, Q), whole3),
            pl.BlockSpec((3, padded, Q), whole3),
        ),
        scratch_shapes=[
            pltpu.VMEM((chans, STATE), F32),
            pltpu.VMEM((6, wide, Q), F32),
            pltpu.VMEM((wide, Q), F32),
            pltpu.VMEM((8, Q), F32),
            pltpu.VMEM((chans, Q), BF16),
            pltpu.VMEM((chans, Q), BF16),
        ],
        compiler_params=params(),
        cost_estimate=pl.CostEstimate(
            flops=40_000_000_000, bytes_accessed=18 * wide * tokens, transcendentals=0
        ),
    )(xr, masks, segr, segc, par, hp, xa, u, s_in, dy, y)


def block_masks(segs, seqs):
    s = segs.reshape(seqs, -1)
    length = s.shape[1]
    rows = []
    for k in (1, 2, 3):
        old = jnp.pad(s, ((0, 0), (k, 0)), constant_values=-1)[:, :length]
        rows.append(old == s)
    b = s.reshape(seqs, length // Q, Q)
    ends = b[:, :, -1:]
    before = jnp.concatenate([jnp.full((seqs, 1, 1), -1, s.dtype), ends[:, :-1]], axis=1)
    rows += [b == before, b == ends, jnp.broadcast_to(ends == before, b.shape)]
    rows = [r.reshape(1, -1).astype(F32) for r in rows]
    return jnp.concatenate(rows + [jnp.zeros((2, segs.shape[0]), F32)], axis=0)


def local(
    hidden, segment_ids, cotangent, w_zx, w_dt, w_bc, w_out, conv_x, conv_bias_x, conv_bc, conv_bias_bc,
    dt_bias, a_log, d_skip, pre_gain, gate_gain,
):
    n_dp, n_t = lax.axis_size("dp"), lax.axis_size("tensor")
    t_index = lax.axis_index("tensor")
    ring = Ring(n_dp)
    core = ring.core
    mine, width = hidden.shape
    rows_dp = w_zx.shape[1]
    inner_here = w_zx.shape[2]
    chans = inner_here // 2
    heads = w_dt.shape[1] // 2
    padded = max(16, heads)
    wide = chans + 2 * STATE
    inner_all = inner_here * n_t

    def tensor_sum(v):
        if n_t == 2:
            return v + lax.ppermute(v, "tensor", [(0, 1), (1, 0)])
        return lax.psum(v, "tensor")

    def pick(v, which, axis=0):
        size = v.shape[axis] // 2
        return lax.dynamic_slice_in_dim(v, which * size, size, axis)

    def in_order(own, other, axis):
        return jnp.where(
            core == 0, jnp.concatenate([own, other], axis), jnp.concatenate([other, own], axis)
        )

    w_xt, w_zt = w_zx[1].T, w_zx[0].T
    w_dtt = jnp.pad(w_dt.T.reshape(2, heads, rows_dp), ((0, 0), (0, padded - heads), (0, 0)))
    w_dtt = w_dtt.reshape(2 * padded, rows_dp)
    w_bct = w_bc.T

    def unit_x(which):
        return jnp.concatenate([pick(w_xt, which), w_bct, pick(w_dtt, which)], axis=0)

    ux = in_order(unit_x(core), ring.swap(unit_x(1 - core)), 1)
    uz = in_order(pick(w_zt, core), ring.swap(pick(w_zt, 1 - core)), 1)
    uo = in_order(pick(w_out, core), ring.swap(pick(w_out, 1 - core)), 1)
    dd = ux.shape[1]
    offs = jnp.stack([ring.chip(s) for s in gather_steps(ring)]).astype(jnp.int32) * dd

    gx = ring_gather(ring, ux)
    gz = ring_gather(ring, uz)
    go = ring_gather(ring, uo)

    inputs = hidden.astype(F32)
    scales = lax.rsqrt(jnp.mean(inputs * inputs, -1, keepdims=True) + EPS)
    normed_own = (inputs * scales * pre_gain).astype(BF16)
    normed = jnp.concatenate([normed_own, ring.swap(normed_own)], axis=0)
    cots = jnp.concatenate([cotangent, ring.swap(cotangent)], axis=0)
    segs = jnp.concatenate([segment_ids, ring.swap(segment_ids)])
    masks = block_masks(segs, 2)
    segr, segc = segs[None, :], segs[:, None]

    def own_chans(v):
        return pick(v, core, v.ndim - 1)

    taps = jnp.concatenate([own_chans(conv_x), conv_bc], axis=1)
    biases = jnp.concatenate([own_chans(conv_bias_x), conv_bias_bc])
    skips = jnp.repeat(own_chans(d_skip), HEAD)
    par = jnp.concatenate(
        [taps, biases[None], jnp.pad(skips, (0, 2 * STATE))[None], jnp.zeros((2, wide), F32)], axis=0
    ).T
    a_own = -jnp.exp(own_chans(a_log))
    hp = jnp.stack([own_chans(dt_bias), a_own, own_chans(d_skip)], axis=1)
    hp = jnp.pad(hp, ((0, padded - heads), (0, 5)))

    xr = proj(gx, normed, offs)
    y, xa, u, s_in = scan_forward(xr, masks, segr, segc, par, hp, heads, 2)
    z = proj(gz, normed, offs)
    sig = jax.nn.sigmoid(z)
    silu = z * sig
    g = y * silu

    def group_sum(v):
        return tensor_sum(v + ring.swap(jnp.concatenate([v[:, mine:], v[:, :mine]], axis=1)))

    total_sq = group_sum(jnp.sum(g * g, 0, keepdims=True))
    s = lax.rsqrt(total_sq / inner_all + EPS)
    gain = own_chans(gate_gain)[:, None]
    gs = g * s
    ynt = (gs * gain).astype(BF16)

    def term(vt, act):
        def block(step):
            cut = lax.dynamic_slice_in_dim(act, ring.chip(step) * dd, dd, 1)
            return dot(vt, cut, (((1,), (0,))))

        return block

    sum_out = ring_scatter(ring, term(ynt, cots), chans)

    def own_rows(partial):
        return (partial[:mine].astype(F32) + ring.swap(partial[mine:]).astype(F32)).astype(BF16)

    def over_tensor(v):
        if n_t == 2:
            return v.astype(F32) + lax.ppermute(v, "tensor", [(0, 1), (1, 0)]).astype(F32)
        return lax.psum(v.astype(F32), "tensor")

    out_part = back([(go, ynt)], offs, width)
    output = (inputs + over_tensor(own_rows(out_part))).astype(BF16)

    dyn = proj(go, cots, offs)
    grad_gate = jnp.sum(dyn * gs, 1)
    wide_dyn = dyn * gain
    q_total = group_sum(jnp.sum(wide_dyn * g, 0, keepdims=True))
    dg = wide_dyn * s - g * (s * s * s * q_total / inner_all)
    dzt = (dg * y * (sig * (1.0 + z * (1.0 - sig)))).astype(BF16)
    dyt = (dg * silu).astype(BF16)

    sum_z = ring_scatter(ring, term(dzt, normed), chans)

    dxt, dbc, ddt, cg, hg = scan_backward(
        xr, masks, segr, segc, par, hp, xa, u, s_in, dyt, y, heads, 2
    )
    sum_x = ring_scatter(ring, term(dxt, normed), chans)

    quarter = 2 * STATE // (2 * n_t)
    dbc_low = dbc.astype(BF16)
    dbc_own = over_tensor(
        (dbc_low[:, :mine].astype(F32) + ring.swap(dbc_low[:, mine:]).astype(F32)).astype(BF16)
    ).astype(BF16)

    def bc_rows(v, start):
        return lax.dynamic_slice_in_dim(v, start, quarter, 0)

    ours = bc_rows(dbc_own, (t_index * 2 + core) * quarter)
    theirs = ring.swap(bc_rows(dbc_own, (t_index * 2 + 1 - core) * quarter))
    dbc_quarter = jnp.concatenate([ours, theirs], axis=1)
    ddt_low = ddt.astype(BF16)
    small = jnp.concatenate([dbc_quarter, ddt_low], axis=0)
    sum_small = ring_scatter(ring, term(small, normed), quarter + padded)

    row = lax.broadcasted_iota(jnp.int32, (2 * STATE, 1), 0)
    both = jnp.concatenate([dbc_own, ring.swap(dbc_own)], axis=1)
    here = row // quarter == t_index * 2 + core
    dbc_here = jnp.where(here, both, jnp.zeros_like(both))
    dxe = jnp.concatenate([dxt, dbc_here, ddt_low], axis=0)
    dn_own = own_rows(back([(gz, dzt), (gx, dxe)], offs, width))
    dn = over_tensor(dn_own)
    weighted = dn * pre_gain
    change = weighted * scales - inputs * scales**3 * (
        jnp.sum(weighted * inputs, -1, keepdims=True) / width
    )
    grad_hidden = (change + cotangent.astype(F32)).astype(BF16)
    pre_part = jnp.sum(dn_own.astype(F32) * inputs * scales, 0)

    cg = jnp.sum(cg, 2)
    hg = jnp.sum(hg, 2)[:, :heads]
    hg = hg * jnp.stack([jnp.ones_like(a_own), a_own, jnp.ones_like(a_own)])
    split = jnp.concatenate([cg[:, :chans].reshape(-1), grad_gate, hg.reshape(-1)])
    shared = jnp.concatenate([cg[:, chans:].reshape(-1), pre_part])
    both_sums = ring.chip_sum(jnp.concatenate([split, shared]))
    split, shared = both_sums[: split.shape[0]], both_sums[split.shape[0] :]
    split_other = ring.swap(split)
    shared = tensor_sum(shared + ring.swap(shared))

    def parts(v):
        a = v[: 5 * chans].reshape(5, chans)
        b = v[5 * chans : 6 * chans]
        c = v[6 * chans :].reshape(3, heads)
        return a, b, c

    (a0, b0, c0), (a1, b1, c1) = parts(split), parts(split_other)
    cg_x = in_order(a0, a1, 1)
    grad_gate = in_order(b0, b1, 0)
    hg = in_order(c0, c1, 1)
    cg_bc = shared[: 5 * 2 * STATE].reshape(5, 2 * STATE)
    grad_pre = shared[5 * 2 * STATE :]

    def finish(total):
        keep = pick(total, core, 1)
        return keep, ring.swap(pick(total, 1 - core, 1))

    kx, ox = finish(sum_x)
    kz, oz = finish(sum_z)
    ko, oo = finish(sum_out)
    grad_zx = jnp.stack([in_order(kz, oz, 0).T, in_order(kx, ox, 0).T])
    grad_out = in_order(ko, oo, 0)
    ks, os = finish(sum_small)
    grad_bc = in_order(ks[:quarter], os[:quarter], 0).T
    grad_dt = in_order(ks[quarter : quarter + heads], os[quarter : quarter + heads], 0).T
    return (
        output, grad_hidden, grad_zx, grad_dt, grad_bc, grad_out, cg_x[:4], cg_x[4], cg_bc[:4], cg_bc[4],
        hg[0], hg[1], hg[2], grad_pre, grad_gate,
    )


def solution(mesh):
    in_specs = (
        P("dp", None), P("dp"), P("dp", None), P(None, "dp", "tensor"), P("dp", "tensor"), P("dp", None),
        P("tensor", "dp"), P(None, "tensor"), P("tensor"), P(), P(), P("tensor"), P("tensor"), P("tensor"),
        P(), P("tensor"),
    )
    out_specs = (
        P("dp", None), P("dp", None), P(None, "dp", "tensor"), P("dp", "tensor"), P("dp", "tensor"),
        P("tensor", "dp"), P(None, "tensor"), P("tensor"), P(), P(), P("tensor"), P("tensor"), P("tensor"),
        P(), P("tensor"),
    )
    return jax.shard_map(local, mesh=mesh, in_specs=in_specs, out_specs=out_specs, check_vma=False)
```

time: 1500 us -> 538 us (0.36)
  waiting for transfers between devices: 811 us -> 190 us
  matrix products: 223 us -> 36.1 us
  blocking collectives: 148 us -> 0 us
  local copies, waits for them, and re-layouts: 157 us -> 50.2 us
  Pallas kernels: 0 us -> 99.5 us
  starting transfers between devices: 0.53 us -> 70.6 us
  other arithmetic: 126 us -> 69.8 us
    reduce_scatter x4 -> x0, waiting for transfers between devices: 582 us -> none  [the longest x1 283 us: local(): lax.psum_scatter(grad_zx, 'dp', scatter_dimension=1, tiled=True)]
    ppermute x0 -> x84, waiting for transfers between devices: none -> 190 us  [the longest x28 107 us: go_right(): return lax.ppermute(v, 'dp', self.right)]
    dot_general x36 -> x32, matrix products: 211 us -> 36.1 us  [dot(): lax.dot_general(a, b, (dims, ((), ())), precision=precision, preferred_el...]
    all_gather x3 -> x0, waiting for transfers between devices: 131 us -> none  [the longest x1 123 us: local(): lax.all_gather(w_zx, 'dp', axis=1, tiled=True)]
    psum x5 -> x0, blocking collectives: 124 us -> none  [the longest x1 58.3 us: local(): lax.psum((grad_conv_x, grad_bias_x, grad_dt_bias, grad_a_log, grad_d_skip...]
    pallas_call x0 -> x7, Pallas kernels: none -> 99.5 us  [the longest x3 30.6 us: proj(): pl.pallas_call(functools.partial(proj_kernel, n, dd), out_shape=jax.Shape...]
    psum x1 -> x0, waiting for transfers between devices: 95.9 us -> none  [local(): lax.psum(jnp.dot(normal, full_out, preferred_element_type=jnp.float32), '...]
    ppermute x0 -> x84, starting transfers between devices: none -> 70.6 us  [the longest x28 34.4 us: go_right(): return lax.ppermute(v, 'dp', self.right)]
  transfers between devices with their start and end apart: 8 -> 84, of which waited for: 7 -> 33; matrix products, arithmetic and copies ran while one was open for 11% -> 22% of each run, Pallas kernels for 0% -> 14%
where the time goes in v1:
time: 538 us; the launch traced here: 531 us
  waiting for transfers between devices  190 us (35%)
  Pallas kernels  99.5 us (18%)
  starting transfers between devices  70.6 us (13%)
  other arithmetic  69.8 us (13%)
  local copies, waits for them, and re-layouts  50.2 us (9%)
  matrix products  36.1 us (7%)
  between operations  14.5 us (3%)
    ppermute x28, waiting for transfers between devices, go_right(): return lax.ppermute(v, 'dp', self.right)  107 us
    ppermute x3, waiting for transfers between devices, over_tensor(): lax.ppermute(v, 'tensor', [(0, 1), (1, 0)]).astype(F32)  49.4 us
    dot_general x32, matrix products, dot(): lax.dot_general(a, b, (dims, ((), ())), precision=precision, preferred_el...  36.1 us
    ppermute x28, starting transfers between devices, go_right(): return lax.ppermute(v, 'dp', self.right)  34.4 us
    pallas_call x3, Pallas kernels, proj(): pl.pallas_call(functools.partial(proj_kernel, n, dd), out_shape=jax.Shape...  30.6 us
    pallas_call x2, Pallas kernels, back(): pl.pallas_call(functools.partial(back_kernel, [len(g[0]) for g in groups]...  27.7 us
    ppermute x28, waiting for transfers between devices, go_left(): return lax.ppermute(v, 'dp', self.left)  27.6 us
    pallas_call x1, Pallas kernels, scan_backward(): pl.pallas_call(functools.partial(bwd_kernel, heads), grid=(seqs, count),...  25.2 us
  transfers between devices with their start and end apart: 84, of which 33 were waited for; matrix products, arithmetic and copies ran while one was open for 22% of the time, Pallas kernels for 14%

profile of v1, /device:TPU:0, one launch (start us, length us, event | category | flops | bytes accessed | tf_op | source)
XLA Modules:
  0.0 530.7 jit_solution(639941218102992758)
XLA Ops:
  12.7 2.2 maximum_select_fusion.5.refs_0_
  14.9 2.6 collective-permute-start.21
  23.7 6.8 %collective-permute-done.21.refs_1_ = bf16[1024,256]{1,0:T(8,128)(2,1)} collective-permute-done((bf16[1024,256]{1,0:T(8,128)(2,1)}, bf16[1024,256]{1,0:T(8,128)(2,1)}, u32[]{:S(2)}, u32[]{:S(2)}) %collective-permute-start.21) | collective-permute-done | bytes 524320 | tf_op jit(solution)/shard_map/ppermute | solution.py:60
  33.0 8.8 %collective-permute-done.1.refs_1_ = bf16[1024,256]{1,0:T(8,128)(2,1)} collective-permute-done((bf16[1024,256]{1,0:T(8,128)(2,1)}, bf16[1024,256]{1,0:T(8,128)(2,1)}, u32[]{:S(2)}, u32[]{:S(2)}) %collective-permute-start.1) | collective-permute-done | bytes 524320 | tf_op jit(solution)/shard_map/ppermute | solution.py:60
  43.9 12.1 %collective-permute-done.10.refs_1_.refs_11_ = bf16[1296,256]{1,0:T(8,128)(2,1)} collective-permute-done((bf16[1296,256]{1,0:T(8,128)(2,1)S(1)}, bf16[1296,256]{1,0:T(8,128)(2,1)}, u32[]{:S(2)}, u32[]{:S(2)}) %collective-permute-start.10) | collective-permute-done | bytes 663584 | tf_op jit(solution)/shard_map/ppermute | solution.py:60
  58.1 9.1 %collective-permute-done.22.refs_2_ = bf16[1024,256]{1,0:T(8,128)(2,1)} collective-permute-done((bf16[1024,256]{1,0:T(8,128)(2,1)}, bf16[1024,256]{1,0:T(8,128)(2,1)}, u32[]{:S(2)}, u32[]{:S(2)}) %collective-permute-start.22) | collective-permute-done | bytes 524320 | tf_op jit(solution)/shard_map/ppermute | solution.py:60
  82.2 5.2 stack.30
  89.9 3.2 constant_dynamic-update-slice_fusion.2
  95.7 2.1 collective-permute-start.3
  99.0 9.3 %collective-permute-done.23.refs_3_ = bf16[1024,256]{1,0:T(8,128)(2,1)} collective-permute-done((bf16[1024,256]{1,0:T(8,128)(2,1)}, bf16[1024,256]{1,0:T(8,128)(2,1)}, u32[]{:S(2)}, u32[]{:S(2)}) %collective-permute-start.23) | collective-permute-done | bytes 524320 | tf_op jit(solution)/shard_map/ppermute | solution.py:60
  113.7 5.8 %collective-permute-done.3.refs_3_ = bf16[1024,256]{1,0:T(8,128)(2,1)} collective-permute-done((bf16[1024,256]{1,0:T(8,128)(2,1)}, bf16[1024,256]{1,0:T(8,128)(2,1)}, u32[]{:S(2)}, u32[]{:S(2)}) %collective-permute-start.3) | collective-permute-done | bytes 524320 | tf_op jit(solution)/shard_map/ppermute | solution.py:60
  124.6 4.2 pad_maximum_fusion.refs_9_
  128.8 4.8 collective-permute-done.12.refs_3_.refs_13_
  135.8 3.4 collective-permute-done.27.refs_7_
  142.0 9.8 %shard_map.642 = f32[1024,1024]{1,0:T(8,128)} custom-call(s32[8]{0:T(128)} %broadcast_multiply_fusion.1.offs, bf16[1024,256]{1,0:T(8,128)(2,1)} %maximum_select_fusion.5.refs_0_, bf16[1024,256]{1,0:T(8,128)(2,1)} %collective-permute-done.21.refs_1_, bf16[1024,256]{1,0:T(8,128)(2,1)} %collective-permute-done.22.refs_2_, ...), custom_call_target="tpu_custom_call" | custom-call | flops 4294967296 | bytes 12582912 | tf_op jit(solution)/shard_map/pallas_call | solution.py:133
  153.2 11.1 %shard_map.640.xr_ref = f32[1296,1024]{1,0:T(8,128)} custom-call(s32[8]{0:T(128)} %broadcast_multiply_fusion.1.offs, bf16[1296,256]{1,0:T(8,128)(2,1)} %copy-done.26, bf16[1296,256]{1,0:T(8,128)(2,1)} %collective-permute-done.10.refs_1_.refs_11_, bf16[1296,256]{1,0:T(8,128)(2,1)} %collective-permute-done.11.refs_2_.refs_12_, bf16[1296,256]{1,0:T(8,128)(2,1)} %copy-done.47, ...), custom_call_target="tpu_custom_call" | custom-call | flops 5435817984 | bytes 14811136 | tf_op jit(solution)/shard_map/pallas_call | solution.py:133
  164.4 16.0 %shard_map.641 = (f32[1024,1024]{1,0:T(8,128)}, bf16[1280,1024]{1,0:T(8,128)(2,1)}, f32[1280,1024]{1,0:T(8,128)}, bf16[1024,1024]{1,0:T(8,128)(2,1)}) custom-call(f32[1296,1024]{1,0:T(8,128)} %shard_map.640.xr_ref, f32[8,1024]{1,0:T(8,128)} %concatenate.168.mask_ref, s32[1,1024]{1,0:T(1,128)} %bitcast.147, s32[1024,1]{1,0:T(8,128)} %copy.123.segc_ref, ...), custom_call_target="tpu_custom_call" | custom-call | flops 20000000000 | bytes 23592960 | tf_op jit(solution)/shard_map/pallas_call | solution.py:305
  180.3 5.0 multiply_reduce_fusion.2
  185.5 3.2 constant_dynamic-update-slice_fusion.1.refs_9_
  190.4 9.7 %shard_map.644 = f32[1024,1024]{1,0:T(8,128)} custom-call(s32[8]{0:T(128)} %broadcast_multiply_fusion.1.offs, bf16[1024,256]{1,0:T(8,128)(2,1)} %maximum_select_fusion.4.refs_0_, bf16[1024,256]{1,0:T(8,128)(2,1)} %collective-permute-done.1.refs_1_, bf16[1024,256]{1,0:T(8,128)(2,1)} %collective-permute-done.2.refs_2_, ...), custom_call_target="tpu_custom_call" | custom-call | flops 4294967296 | bytes 12582912 | tf_op jit(solution)/shard_map/pallas_call | solution.py:133
  200.2 3.8 multiply_reduce_fusion
  204.2 3.3 fusion.39
  208.0 2.9 fusion.43
  211.3 4.6 multiply_convert_fusion
  215.9 25.2 %shard_map.645 = (bf16[1024,1024]{1,0:T(8,128)(2,1)}, f32[256,1024]{1,0:T(8,128)}, f32[16,1024]{1,0:T(8,128)}, f32[5,1280,128]{2,1,0:T(8,128)}, f32[3,16,128]{2,1,0:T(8,128)}) custom-call(f32[1296,1024]{1,0:T(8,128)} %shard_map.640.xr_ref, f32[8,1024]{1,0:T(8,128)} %concatenate.168.mask_ref, s32[1,1024]{1,0:T(1,128)} %bitcast.148, ...), custom_call_target="tpu_custom_call" | custom-call | flops 40000000000 | bytes 23592960 | tf_op jit(solution)/shard_map/pallas_call | solution.py:467
  241.2 2.8 reduce_sum.76
  244.0 2.6 convolution_convert_fusion
  246.6 2.8 fusion.55
  268.0 9.9 %shard_map.643 = bf16[1024,2048]{1,0:T(8,128)(2,1)} custom-call(s32[8]{0:T(128)} %broadcast_multiply_fusion.1.offs, bf16[1024,256]{1,0:T(8,128)(2,1)} %maximum_select_fusion.4.refs_0_, bf16[1024,256]{1,0:T(8,128)(2,1)} %collective-permute-done.1.refs_1_, bf16[1024,256]{1,0:T(8,128)(2,1)} %collective-permute-done.2.refs_2_, ...), custom_call_target="tpu_custom_call" | custom-call | flops 4294967296 | bytes 8388608 | tf_op jit(solution)/shard_map/pallas_call | solution.py:183
  287.3 2.8 collective-permute-done.41
  302.8 4.6 collective-permute-done.64
  330.9 17.8 %shard_map.646 = bf16[1024,2048]{1,0:T(8,128)(2,1)} custom-call(s32[8]{0:T(128)} %broadcast_multiply_fusion.1.offs, bf16[1024,256]{1,0:T(8,128)(2,1)} %maximum_select_fusion.5.refs_0_, bf16[1024,256]{1,0:T(8,128)(2,1)} %collective-permute-done.21.refs_1_, bf16[1024,256]{1,0:T(8,128)(2,1)} %collective-permute-done.22.refs_2_, ...), custom_call_target="tpu_custom_call" | custom-call | flops 9730785280 | bytes 13697024 | tf_op jit(solution)/shard_map/pallas_call | solution.py:183
  355.5 2.0 fusion.25
  357.5 6.9 %collective-permute-done.51 = bf16[1024,256]{1,0:T(8,128)(2,1)S(1)} collective-permute-done((bf16[1024,256]{1,0:T(8,128)(2,1)S(1)}, bf16[1024,256]{1,0:T(8,128)(2,1)S(1)}, u32[]{:S(2)}, u32[]{:S(2)}) %collective-permute-start.51) | collective-permute-done | bytes 524320 | tf_op jit(solution)/shard_map/ppermute | solution.py:60
  371.5 17.0 %collective-permute-done.43 = bf16[1024,256]{1,0:T(8,128)(2,1)S(1)} collective-permute-done((bf16[1024,256]{1,0:T(8,128)(2,1)S(1)}, bf16[1024,256]{1,0:T(8,128)(2,1)S(1)}, u32[]{:S(2)}, u32[]{:S(2)}) %collective-permute-start.43) | collective-permute-done | bytes 524320 | tf_op jit(solution)/shard_map/ppermute | solution.py:60
  392.1 8.4 %collective-permute-done.52 = bf16[1024,256]{1,0:T(8,128)(2,1)S(1)} collective-permute-done((bf16[1024,256]{1,0:T(8,128)(2,1)S(1)}, bf16[1024,256]{1,0:T(8,128)(2,1)S(1)}, u32[]{:S(2)}, u32[]{:S(2)}) %collective-permute-start.52) | collective-permute-done | bytes 524320 | tf_op jit(solution)/shard_map/ppermute | solution.py:60
  408.7 6.7 %collective-permute-done.56 = bf16[1024,256]{1,0:T(8,128)(2,1)S(1)} collective-permute-done((bf16[1024,256]{1,0:T(8,128)(2,1)S(1)}, bf16[1024,256]{1,0:T(8,128)(2,1)S(1)}, u32[]{:S(2)}, u32[]{:S(2)}) %collective-permute-start.56) | collective-permute-done | bytes 524320 | tf_op jit(solution)/shard_map/ppermute | solution.py:63
  417.3 6.6 %collective-permute-done.48 = bf16[1024,256]{1,0:T(8,128)(2,1)S(1)} collective-permute-done((bf16[1024,256]{1,0:T(8,128)(2,1)S(1)}, bf16[1024,256]{1,0:T(8,128)(2,1)S(1)}, u32[]{:S(2)}, u32[]{:S(2)}) %collective-permute-start.48) | collective-permute-done | bytes 524320 | tf_op jit(solution)/shard_map/ppermute | solution.py:63
  428.1 8.1 %collective-permute-done.53 = bf16[1024,256]{1,0:T(8,128)(2,1)S(1)} collective-permute-done((bf16[1024,256]{1,0:T(8,128)(2,1)S(1)}, bf16[1024,256]{1,0:T(8,128)(2,1)S(1)}, u32[]{:S(2)}, u32[]{:S(2)}) %collective-permute-start.53) | collective-permute-done | bytes 524320 | tf_op jit(solution)/shard_map/ppermute | solution.py:60
  439.1 3.7 add_convert_fusion.1
  443.6 2.7 collective-permute-done.76
  450.5 25.3 %collective-permute-done.40 = bf16[512,2048]{1,0:T(8,128)(2,1)S(1)} collective-permute-done((bf16[512,2048]{1,0:T(8,128)(2,1)S(1)}, bf16[512,2048]{1,0:T(8,128)(2,1)S(1)}, u32[]{:S(2)}, u32[]{:S(2)}) %collective-permute-start.40) | collective-permute-done | bytes 2097184 | tf_op jit(solution)/shard_map/ppermute | solution.py:628
  479.3 2.8 pad_maximum_fusion.2
  482.6 2.3 maximum_select_fusion.2
  484.9 2.9 copy.127
  489.0 3.8 collective-permute-done.80
  492.9 24.1 %collective-permute-done.32 = bf16[512,2048]{1,0:T(8,128)(2,1)} collective-permute-done((bf16[512,2048]{1,0:T(8,128)(2,1)}, bf16[512,2048]{1,0:T(8,128)(2,1)}, u32[]{:S(2)}, u32[]{:S(2)}) %collective-permute-start.32) | collective-permute-done | bytes 2097184 | tf_op jit(solution)/shard_map/ppermute | solution.py:628
  517.0 7.5 %fusion.8 = (bf16[512,2048]{1,0:T(8,128)(2,1)}, bf16[512,2048]{1,0:T(8,128)(2,1)}) fusion(bf16[512,2048]{1,0:T(8,128)(2,1)S(1)} %copy-done.5, bf16[512,2048]{1,0:T(8,128)(2,1)} %param.59, bf16[512,2048]{1,0:T(8,128)(2,1)} %copy-done.15, bf16[512,2048]{1,0:T(8,128)(2,1)} %copy-done.7, f32[512]{0:T(512)S(1)} %broadcast_multiply_fusion, f32[512]{0:T(512)S(1)} %copy-done.63, ...), kind=kLoop, calls=%fused_computation.32 | loop fusion | flops 17825792 | bytes 16791552 | tf_op jit(solution)/shard_map/convert_element_type | solution.py:676
  (492 shorter events, 167.8 us)
Async XLA Ops:
  5.0 16.7 %collective-permute-start.9 = (bf16[1296,128]{1,0:T(8,128)(2,1)}, bf16[1296,128]{1,0:T(8,128)(2,1)}, u32[]{:S(2)}, u32[]{:S(2)}) collective-permute-start(bf16[1296,128]{1,0:T(8,128)(2,1)} %pad_maximum_fusion.9), channel_id=1, source_target_pairs={{0,2},{2,0},{4,6},{6,4},{8,10},{10,8},{12,14},{14,12},{16,18},{18,... | collective-permute-start | bytes 995336 | tf_op jit(solution)/shard_map/ppermute | solution.py:66
  14.9 15.6 %collective-permute-start.21 = (bf16[1024,256]{1,0:T(8,128)(2,1)}, bf16[1024,256]{1,0:T(8,128)(2,1)}, u32[]{:S(2)}, u32[]{:S(2)}) collective-permute-start(bf16[1024,256]{1,0:T(8,128)(2,1)} %maximum_select_fusion.5.refs_0_), channel_id=1, source_target_pairs={{0,8},{2,10},{8,16},{10,18},{16,24},{18,26},{24,28},{26,30},{28,20... | collective-permute-start | bytes 1572872 | tf_op jit(solution)/shard_map/ppermute | solution.py:60
  17.5 15.1 %collective-permute-start.24 = (bf16[1024,256]{1,0:T(8,128)(2,1)}, bf16[1024,256]{1,0:T(8,128)(2,1)}, u32[]{:S(2)}, u32[]{:S(2)}) collective-permute-start(bf16[1024,256]{1,0:T(8,128)(2,1)} %maximum_select_fusion.5.refs_0_), channel_id=1, source_target_pairs={{0,4},{2,6},{8,0},{10,2},{16,8},{18,10},{24,16},{26,18},{28,24},{3... | collective-permute-start | bytes 1572872 | tf_op jit(solution)/shard_map/ppermute | solution.py:63
  19.5 22.2 %collective-permute-start.1 = (bf16[1024,256]{1,0:T(8,128)(2,1)}, bf16[1024,256]{1,0:T(8,128)(2,1)}, u32[]{:S(2)}, u32[]{:S(2)}) collective-permute-start(bf16[1024,256]{1,0:T(8,128)(2,1)} %maximum_select_fusion.4.refs_0_), channel_id=1, source_target_pairs={{0,8},{2,10},{8,16},{10,18},{16,24},{18,26},{24,28},{26,30},{28,20... | collective-permute-start | bytes 1572872 | tf_op jit(solution)/shard_map/ppermute | solution.py:60
  21.5 22.3 %collective-permute-start.4 = (bf16[1024,256]{1,0:T(8,128)(2,1)}, bf16[1024,256]{1,0:T(8,128)(2,1)}, u32[]{:S(2)}, u32[]{:S(2)}) collective-permute-start(bf16[1024,256]{1,0:T(8,128)(2,1)} %maximum_select_fusion.4.refs_0_), channel_id=1, source_target_pairs={{0,4},{2,6},{8,0},{10,2},{16,8},{18,10},{24,16},{26,18},{28,24},{3... | collective-permute-start | bytes 1572872 | tf_op jit(solution)/shard_map/ppermute | solution.py:63
  23.1 101.0 %collective-permute-start.18 = (bf16[512,2048]{1,0:T(8,128)(2,1)S(1)}, bf16[512,2048]{1,0:T(8,128)(2,1)}, u32[]{:S(2)}, u32[]{:S(2)}) collective-permute-start(bf16[512,2048]{1,0:T(8,128)(2,1)S(1)} %copy-done.6), channel_id=1, source_target_pairs={{0,2},{2,0},{4,6},{6,4},{8,10},{10,8},{12,14},{14,12},{16,18},{18,... | collective-permute-start | bytes 6291464 | tf_op jit(solution)/shard_map/ppermute | solution.py:66
  30.5 25.5 %collective-permute-start.10 = (bf16[1296,256]{1,0:T(8,128)(2,1)S(1)}, bf16[1296,256]{1,0:T(8,128)(2,1)}, u32[]{:S(2)}, u32[]{:S(2)}) collective-permute-start(bf16[1296,256]{1,0:T(8,128)(2,1)S(1)} %maximum_select_fusion.3.refs_0_.refs_10_), channel_id=1, source_target_pairs={{0,8},{2,10},{8,16},{10,18},{16,24},{18,26},{24,28},{26,30},{28,20... | collective-permute-start | bytes 1990664 | tf_op jit(solution)/shard_map/ppermute | solution.py:60
  32.5 25.5 %collective-permute-start.13 = (bf16[1296,256]{1,0:T(8,128)(2,1)S(1)}, bf16[1296,256]{1,0:T(8,128)(2,1)}, u32[]{:S(2)}, u32[]{:S(2)}) collective-permute-start(bf16[1296,256]{1,0:T(8,128)(2,1)S(1)} %maximum_select_fusion.3.refs_0_.refs_10_), channel_id=1, source_target_pairs={{0,4},{2,6},{8,0},{10,2},{16,8},{18,10},{24,16},{26,18},{28,24},{3... | collective-permute-start | bytes 1990664 | tf_op jit(solution)/shard_map/ppermute | solution.py:63
  41.7 25.5 %collective-permute-start.22 = (bf16[1024,256]{1,0:T(8,128)(2,1)}, bf16[1024,256]{1,0:T(8,128)(2,1)}, u32[]{:S(2)}, u32[]{:S(2)}) collective-permute-start(bf16[1024,256]{1,0:T(8,128)(2,1)} %collective-permute-done.21.refs_1_), channel_id=1, source_target_pairs={{0,8},{2,10},{8,16},{10,18},{16,24},{18,26},{24,28},{26,30},{28,20... | collective-permute-start | bytes 1572872 | tf_op jit(solution)/shard_map/ppermute | solution.py:60
  43.8 25.5 %collective-permute-start.25 = (bf16[1024,256]{1,0:T(8,128)(2,1)}, bf16[1024,256]{1,0:T(8,128)(2,1)}, u32[]{:S(2)}, u32[]{:S(2)}) collective-permute-start(bf16[1024,256]{1,0:T(8,128)(2,1)} %collective-permute-done.24.refs_4_), channel_id=1, source_target_pairs={{0,4},{2,6},{8,0},{10,2},{16,8},{18,10},{24,16},{26,18},{28,24},{3... | collective-permute-start | bytes 1572872 | tf_op jit(solution)/shard_map/ppermute | solution.py:63
  56.0 37.2 %collective-permute-start.2 = (bf16[1024,256]{1,0:T(8,128)(2,1)}, bf16[1024,256]{1,0:T(8,128)(2,1)}, u32[]{:S(2)}, u32[]{:S(2)}) collective-permute-start(bf16[1024,256]{1,0:T(8,128)(2,1)} %collective-permute-done.1.refs_1_), channel_id=1, source_target_pairs={{0,8},{2,10},{8,16},{10,18},{16,24},{18,26},{24,28},{26,30},{28,20... | collective-permute-start | bytes 1572872 | tf_op jit(solution)/shard_map/ppermute | solution.py:60
  58.0 37.1 %collective-permute-start.5 = (bf16[1024,256]{1,0:T(8,128)(2,1)}, bf16[1024,256]{1,0:T(8,128)(2,1)}, u32[]{:S(2)}, u32[]{:S(2)}) collective-permute-start(bf16[1024,256]{1,0:T(8,128)(2,1)} %collective-permute-done.4.refs_4_), channel_id=1, source_target_pairs={{0,4},{2,6},{8,0},{10,2},{16,8},{18,10},{24,16},{26,18},{28,24},{3... | collective-permute-start | bytes 1572872 | tf_op jit(solution)/shard_map/ppermute | solution.py:63
  67.2 28.5 %collective-permute-start.11 = (bf16[1296,256]{1,0:T(8,128)(2,1)}, bf16[1296,256]{1,0:T(8,128)(2,1)}, u32[]{:S(2)}, u32[]{:S(2)}) collective-permute-start(bf16[1296,256]{1,0:T(8,128)(2,1)} %collective-permute-done.10.refs_1_.refs_11_), channel_id=1, source_target_pairs={{0,8},{2,10},{8,16},{10,18},{16,24},{18,26},{24,28},{26,30},{28,20... | collective-permute-start | bytes 1990664 | tf_op jit(solution)/shard_map/ppermute | solution.py:60
  69.2 28.5 %collective-permute-start.14 = (bf16[1296,256]{1,0:T(8,128)(2,1)}, bf16[1296,256]{1,0:T(8,128)(2,1)}, u32[]{:S(2)}, u32[]{:S(2)}) collective-permute-start(bf16[1296,256]{1,0:T(8,128)(2,1)} %collective-permute-done.13.refs_4_.refs_14_), channel_id=1, source_target_pairs={{0,4},{2,6},{8,0},{10,2},{16,8},{18,10},{24,16},{26,18},{28,24},{3... | collective-permute-start | bytes 1990664 | tf_op jit(solution)/shard_map/ppermute | solution.py:63
  93.1 15.2 %collective-permute-start.23 = (bf16[1024,256]{1,0:T(8,128)(2,1)}, bf16[1024,256]{1,0:T(8,128)(2,1)}, u32[]{:S(2)}, u32[]{:S(2)}) collective-permute-start(bf16[1024,256]{1,0:T(8,128)(2,1)} %collective-permute-done.22.refs_2_), channel_id=1, source_target_pairs={{0,8},{2,10},{8,16},{10,18},{16,24},{18,26},{24,28},{26,30},{28,20... | collective-permute-start | bytes 1572872 | tf_op jit(solution)/shard_map/ppermute | solution.py:60
  95.1 15.2 %collective-permute-start.26 = (bf16[1024,256]{1,0:T(8,128)(2,1)}, bf16[1024,256]{1,0:T(8,128)(2,1)}, u32[]{:S(2)}, u32[]{:S(2)}) collective-permute-start(bf16[1024,256]{1,0:T(8,128)(2,1)} %collective-permute-done.25.refs_5_), channel_id=1, source_target_pairs={{0,4},{2,6},{8,0},{10,2},{16,8},{18,10},{24,16},{26,18},{28,24},{3... | collective-permute-start | bytes 1572872 | tf_op jit(solution)/shard_map/ppermute | solution.py:63
  95.7 23.8 %collective-permute-start.3 = (bf16[1024,256]{1,0:T(8,128)(2,1)}, bf16[1024,256]{1,0:T(8,128)(2,1)}, u32[]{:S(2)}, u32[]{:S(2)}) collective-permute-start(bf16[1024,256]{1,0:T(8,128)(2,1)} %collective-permute-done.2.refs_2_), channel_id=1, source_target_pairs={{0,8},{2,10},{8,16},{10,18},{16,24},{18,26},{24,28},{26,30},{28,20... | collective-permute-start | bytes 1572872 | tf_op jit(solution)/shard_map/ppermute | solution.py:60
  97.8 23.8 %collective-permute-start.6 = (bf16[1024,256]{1,0:T(8,128)(2,1)}, bf16[1024,256]{1,0:T(8,128)(2,1)}, u32[]{:S(2)}, u32[]{:S(2)}) collective-permute-start(bf16[1024,256]{1,0:T(8,128)(2,1)} %collective-permute-done.5.refs_5_), channel_id=1, source_target_pairs={{0,4},{2,6},{8,0},{10,2},{16,8},{18,10},{24,16},{26,18},{28,24},{3... | collective-permute-start | bytes 1572872 | tf_op jit(solution)/shard_map/ppermute | solution.py:63
  108.3 25.3 %collective-permute-start.12 = (bf16[1296,256]{1,0:T(8,128)(2,1)}, bf16[1296,256]{1,0:T(8,128)(2,1)S(1)}, u32[]{:S(2)}, u32[]{:S(2)}) collective-permute-start(bf16[1296,256]{1,0:T(8,128)(2,1)} %collective-permute-done.11.refs_2_.refs_12_), channel_id=1, source_target_pairs={{0,8},{2,10},{8,16},{10,18},{16,24},{18,26},{24,28},{26,30},{28,20... | collective-permute-start | bytes 1990664 | tf_op jit(solution)/shard_map/ppermute | solution.py:60
  110.3 25.4 %collective-permute-start.15 = (bf16[1296,256]{1,0:T(8,128)(2,1)}, bf16[1296,256]{1,0:T(8,128)(2,1)S(1)}, u32[]{:S(2)}, u32[]{:S(2)}) collective-permute-start(bf16[1296,256]{1,0:T(8,128)(2,1)} %collective-permute-done.14.refs_5_.refs_15_), channel_id=1, source_target_pairs={{0,4},{2,6},{8,0},{10,2},{16,8},{18,10},{24,16},{26,18},{28,24},{3... | collective-permute-start | bytes 1990664 | tf_op jit(solution)/shard_map/ppermute | solution.py:63
  119.5 65.9 %collective-permute-start.33 = (bf16[512,2048]{1,0:T(8,128)(2,1)}, bf16[512,2048]{1,0:T(8,128)(2,1)}, u32[]{:S(2)}, u32[]{:S(2)}) collective-permute-start(bf16[512,2048]{1,0:T(8,128)(2,1)} %param.59), channel_id=1, source_target_pairs={{0,2},{2,0},{4,6},{6,4},{8,10},{10,8},{12,14},{14,12},{16,18},{18,... | collective-permute-start | bytes 6291464 | tf_op jit(solution)/shard_map/ppermute | solution.py:66
  121.6 17.7 %collective-permute-start.27 = (bf16[512,256]{1,0:T(8,128)(2,1)S(1)}, bf16[512,256]{1,0:T(8,128)(2,1)S(1)}, u32[]{:S(2)}, u32[]{:S(2)}) collective-permute-start(bf16[512,256]{1,0:T(8,128)(2,1)S(1)} %slice.341), channel_id=1, source_target_pairs={{0,8},{2,10},{8,16},{10,18},{16,24},{18,26},{24,28},{26,30},{28,20... | collective-permute-start | bytes 786440 | tf_op jit(solution)/shard_map/ppermute | solution.py:60
  124.1 17.2 %collective-permute-start.28 = (bf16[512,256]{1,0:T(8,128)(2,1)S(1)}, bf16[512,256]{1,0:T(8,128)(2,1)S(1)}, u32[]{:S(2)}, u32[]{:S(2)}) collective-permute-start(bf16[512,256]{1,0:T(8,128)(2,1)S(1)} %slice.342), channel_id=1, source_target_pairs={{0,4},{2,6},{8,0},{10,2},{16,8},{18,10},{24,16},{26,18},{28,24},{3... | collective-permute-start | bytes 786440 | tf_op jit(solution)/shard_map/ppermute | solution.py:63
  133.7 56.8 %collective-permute-start.7 = (bf16[512,256]{1,0:T(8,128)(2,1)S(1)}, bf16[512,256]{1,0:T(8,128)(2,1)}, u32[]{:S(2)}, u32[]{:S(2)}) collective-permute-start(bf16[512,256]{1,0:T(8,128)(2,1)S(1)} %slice.333), channel_id=1, source_target_pairs={{0,8},{2,10},{8,16},{10,18},{16,24},{18,26},{24,28},{26,30},{28,20... | collective-permute-start | bytes 786440 | tf_op jit(solution)/shard_map/ppermute | solution.py:60
  135.7 54.7 %collective-permute-start.8 = (bf16[512,256]{1,0:T(8,128)(2,1)S(1)}, bf16[512,256]{1,0:T(8,128)(2,1)}, u32[]{:S(2)}, u32[]{:S(2)}) collective-permute-start(bf16[512,256]{1,0:T(8,128)(2,1)S(1)} %slice.334), channel_id=1, source_target_pairs={{0,4},{2,6},{8,0},{10,2},{16,8},{18,10},{24,16},{26,18},{28,24},{3... | collective-permute-start | bytes 786440 | tf_op jit(solution)/shard_map/ppermute | solution.py:63
  262.7 22.8 %collective-permute-start.36 = (bf16[256,512]{1,0:T(8,128)(2,1)}, bf16[256,512]{1,0:T(8,128)(2,1)S(1)}, u32[]{:S(2)}, u32[]{:S(2)}) collective-permute-start(bf16[256,512]{1,0:T(8,128)(2,1)} %slice.350), channel_id=1, source_target_pairs={{0,2},{2,0},{4,6},{6,4},{8,10},{10,8},{12,14},{14,12},{16,18},{18,... | collective-permute-start | bytes 786440 | tf_op jit(solution)/shard_map/ppermute | solution.py:66
  265.9 17.0 %collective-permute-start.69 = (bf16[512,256]{1,0:T(8,128)(2,1)}, bf16[512,256]{1,0:T(8,128)(2,1)}, u32[]{:S(2)}, u32[]{:S(2)}) collective-permute-start(bf16[512,256]{1,0:T(8,128)(2,1)} %get-tuple-element.120), channel_id=1, source_target_pairs={{0,8},{2,10},{8,16},{10,18},{16,24},{18,26},{24,28},{26,30},{28,20... | collective-permute-start | bytes 786440 | tf_op jit(solution)/shard_map/ppermute | solution.py:60
  267.5 18.6 %collective-permute-start.73 = (bf16[512,256]{1,0:T(8,128)(2,1)}, bf16[512,256]{1,0:T(8,128)(2,1)}, u32[]{:S(2)}, u32[]{:S(2)}) collective-permute-start(bf16[512,256]{1,0:T(8,128)(2,1)} %get-tuple-element.121), channel_id=1, source_target_pairs={{0,4},{2,6},{8,0},{10,2},{16,8},{18,10},{24,16},{26,18},{28,24},{3... | collective-permute-start | bytes 786440 | tf_op jit(solution)/shard_map/ppermute | solution.py:63
  279.1 13.8 %collective-permute-start.45 = (bf16[512,256]{1,0:T(8,128)(2,1)S(1)}, bf16[512,256]{1,0:T(8,128)(2,1)S(1)}, u32[]{:S(2)}, u32[]{:S(2)}) collective-permute-start(bf16[512,256]{1,0:T(8,128)(2,1)S(1)} %get-tuple-element.123), channel_id=1, source_target_pairs={{0,4},{2,6},{8,0},{10,2},{16,8},{18,10},{24,16},{26,18},{28,24},{3... | collective-permute-start | bytes 786440 | tf_op jit(solution)/shard_map/ppermute | solution.py:63
  286.2 151.5 %collective-permute-start.31 = (bf16[512,2048]{1,0:T(8,128)(2,1)}, bf16[512,2048]{1,0:T(8,128)(2,1)}, u32[]{:S(2)}, u32[]{:S(2)}) collective-permute-start(bf16[512,2048]{1,0:T(8,128)(2,1)} %slice.346), channel_id=1, source_target_pairs={{0,2},{2,0},{4,6},{6,4},{8,10},{10,8},{12,14},{14,12},{16,18},{18,... | collective-permute-start | bytes 6291464 | tf_op jit(solution)/shard_map/ppermute | solution.py:66
  293.0 62.4 %collective-permute-start.70 = (bf16[1024,256]{1,0:T(8,128)(2,1)}, bf16[1024,256]{1,0:T(8,128)(2,1)}, u32[]{:S(2)}, u32[]{:S(2)}) collective-permute-start(bf16[1024,256]{1,0:T(8,128)(2,1)} %pad_maximum_fusion.7), channel_id=1, source_target_pairs={{0,8},{2,10},{8,16},{10,18},{16,24},{18,26},{24,28},{26,30},{28,20... | collective-permute-start | bytes 1572872 | tf_op jit(solution)/shard_map/ppermute | solution.py:60
  295.1 72.8 %collective-permute-start.74 = (bf16[1024,256]{1,0:T(8,128)(2,1)}, bf16[1024,256]{1,0:T(8,128)(2,1)}, u32[]{:S(2)}, u32[]{:S(2)}) collective-permute-start(bf16[1024,256]{1,0:T(8,128)(2,1)} %pad_maximum_fusion.8), channel_id=1, source_target_pairs={{0,4},{2,6},{8,0},{10,2},{16,8},{18,10},{24,16},{26,18},{28,24},{3... | collective-permute-start | bytes 1572872 | tf_op jit(solution)/shard_map/ppermute | solution.py:63
  323.7 27.0 %collective-permute-start.42 = (bf16[1024,256]{1,0:T(8,128)(2,1)}, bf16[1024,256]{1,0:T(8,128)(2,1)}, u32[]{:S(2)}, u32[]{:S(2)}) collective-permute-start(bf16[1024,256]{1,0:T(8,128)(2,1)} %pad_maximum_fusion.3), channel_id=1, source_target_pairs={{0,8},{2,10},{8,16},{10,18},{16,24},{18,26},{24,28},{26,30},{28,20... | collective-permute-start | bytes 1572872 | tf_op jit(solution)/shard_map/ppermute | solution.py:60
  326.3 26.6 %collective-permute-start.46 = (bf16[1024,256]{1,0:T(8,128)(2,1)}, bf16[1024,256]{1,0:T(8,128)(2,1)S(1)}, u32[]{:S(2)}, u32[]{:S(2)}) collective-permute-start(bf16[1024,256]{1,0:T(8,128)(2,1)} %pad_maximum_fusion.4), channel_id=1, source_target_pairs={{0,4},{2,6},{8,0},{10,2},{16,8},{18,10},{24,16},{26,18},{28,24},{3... | collective-permute-start | bytes 1572872 | tf_op jit(solution)/shard_map/ppermute | solution.py:63
  350.7 13.8 %collective-permute-start.51 = (bf16[1024,256]{1,0:T(8,128)(2,1)S(1)}, bf16[1024,256]{1,0:T(8,128)(2,1)S(1)}, u32[]{:S(2)}, u32[]{:S(2)}) collective-permute-start(bf16[1024,256]{1,0:T(8,128)(2,1)S(1)} %copy-done.40), channel_id=1, source_target_pairs={{0,8},{2,10},{8,16},{10,18},{16,24},{18,26},{24,28},{26,30},{28,20... | collective-permute-start | bytes 1572872 | tf_op jit(solution)/shard_map/ppermute | solution.py:60
  355.4 70.8 %collective-permute-start.39 = (bf16[512,2048]{1,0:T(8,128)(2,1)S(1)}, bf16[512,2048]{1,0:T(8,128)(2,1)S(1)}, u32[]{:S(2)}, u32[]{:S(2)}) collective-permute-start(bf16[512,2048]{1,0:T(8,128)(2,1)S(1)} %slice.352), channel_id=1, source_target_pairs={{0,2},{2,0},{4,6},{6,4},{8,10},{10,8},{12,14},{14,12},{16,18},{18,... | collective-permute-start | bytes 6291464 | tf_op jit(solution)/shard_map/ppermute | solution.py:66
  364.5 38.3 %collective-permute-start.71 = (bf16[1024,256]{1,0:T(8,128)(2,1)S(1)}, bf16[1024,256]{1,0:T(8,128)(2,1)S(1)}, u32[]{:S(2)}, u32[]{:S(2)}) collective-permute-start(bf16[1024,256]{1,0:T(8,128)(2,1)S(1)} %fusion.25), channel_id=1, source_target_pairs={{0,8},{2,10},{8,16},{10,18},{16,24},{18,26},{24,28},{26,30},{28,20... | collective-permute-start | bytes 1572872 | tf_op jit(solution)/shard_map/ppermute | solution.py:60
  366.8 21.8 %collective-permute-start.43 = (bf16[1024,256]{1,0:T(8,128)(2,1)S(1)}, bf16[1024,256]{1,0:T(8,128)(2,1)S(1)}, u32[]{:S(2)}, u32[]{:S(2)}) collective-permute-start(bf16[1024,256]{1,0:T(8,128)(2,1)S(1)} %fusion.17), channel_id=1, source_target_pairs={{0,8},{2,10},{8,16},{10,18},{16,24},{18,26},{24,28},{26,30},{28,20... | collective-permute-start | bytes 1572872 | tf_op jit(solution)/shard_map/ppermute | solution.py:60
  367.9 21.8 %collective-permute-start.47 = (bf16[1024,256]{1,0:T(8,128)(2,1)S(1)}, bf16[1024,256]{1,0:T(8,128)(2,1)S(1)}, u32[]{:S(2)}, u32[]{:S(2)}) collective-permute-start(bf16[1024,256]{1,0:T(8,128)(2,1)S(1)} %fusion.19), channel_id=1, source_target_pairs={{0,4},{2,6},{8,0},{10,2},{16,8},{18,10},{24,16},{26,18},{28,24},{3... | collective-permute-start | bytes 1572872 | tf_op jit(solution)/shard_map/ppermute | solution.py:63
  389.7 15.6 %collective-permute-start.75 = (bf16[1024,256]{1,0:T(8,128)(2,1)S(1)}, bf16[1024,256]{1,0:T(8,128)(2,1)S(1)}, u32[]{:S(2)}, u32[]{:S(2)}) collective-permute-start(bf16[1024,256]{1,0:T(8,128)(2,1)S(1)} %fusion.27), channel_id=1, source_target_pairs={{0,4},{2,6},{8,0},{10,2},{16,8},{18,10},{24,16},{26,18},{28,24},{3... | collective-permute-start | bytes 1572872 | tf_op jit(solution)/shard_map/ppermute | solution.py:63
  400.5 14.9 %collective-permute-start.56 = (bf16[1024,256]{1,0:T(8,128)(2,1)S(1)}, bf16[1024,256]{1,0:T(8,128)(2,1)S(1)}, u32[]{:S(2)}, u32[]{:S(2)}) collective-permute-start(bf16[1024,256]{1,0:T(8,128)(2,1)S(1)} %fusion.23), channel_id=1, source_target_pairs={{0,4},{2,6},{8,0},{10,2},{16,8},{18,10},{24,16},{26,18},{28,24},{3... | collective-permute-start | bytes 1572872 | tf_op jit(solution)/shard_map/ppermute | solution.py:63
  405.3 18.6 %collective-permute-start.48 = (bf16[1024,256]{1,0:T(8,128)(2,1)S(1)}, bf16[1024,256]{1,0:T(8,128)(2,1)S(1)}, u32[]{:S(2)}, u32[]{:S(2)}) collective-permute-start(bf16[1024,256]{1,0:T(8,128)(2,1)S(1)} %fusion.18), channel_id=1, source_target_pairs={{0,4},{2,6},{8,0},{10,2},{16,8},{18,10},{24,16},{26,18},{28,24},{3... | collective-permute-start | bytes 1572872 | tf_op jit(solution)/shard_map/ppermute | solution.py:63
  415.3 27.5 %collective-permute-start.72 = (bf16[1024,256]{1,0:T(8,128)(2,1)S(1)}, bf16[1024,256]{1,0:T(8,128)(2,1)S(1)}, u32[]{:S(2)}, u32[]{:S(2)}) collective-permute-start(bf16[1024,256]{1,0:T(8,128)(2,1)S(1)} %fusion.24), channel_id=1, source_target_pairs={{0,8},{2,10},{8,16},{10,18},{16,24},{18,26},{24,28},{26,30},{28,20... | collective-permute-start | bytes 1572872 | tf_op jit(solution)/shard_map/ppermute | solution.py:60
  416.5 19.8 %collective-permute-start.53 = (bf16[1024,256]{1,0:T(8,128)(2,1)S(1)}, bf16[1024,256]{1,0:T(8,128)(2,1)S(1)}, u32[]{:S(2)}, u32[]{:S(2)}) collective-permute-start(bf16[1024,256]{1,0:T(8,128)(2,1)S(1)} %fusion.20), channel_id=1, source_target_pairs={{0,8},{2,10},{8,16},{10,18},{16,24},{18,26},{24,28},{26,30},{28,20... | collective-permute-start | bytes 1572872 | tf_op jit(solution)/shard_map/ppermute | solution.py:60
  427.1 48.6 %collective-permute-start.40 = (bf16[512,2048]{1,0:T(8,128)(2,1)S(1)}, bf16[512,2048]{1,0:T(8,128)(2,1)S(1)}, u32[]{:S(2)}, u32[]{:S(2)}) collective-permute-start(bf16[512,2048]{1,0:T(8,128)(2,1)S(1)} %add_convert_fusion), channel_id=1, source_target_pairs={{0,1},{1,0},{2,3},{3,2},{4,5},{5,4},{6,7},{7,6},{8,9},{9,8},{10,11... | collective-permute-start | bytes 6291464 | tf_op jit(solution)/shard_map/ppermute | solution.py:628
  442.8 74.2 %collective-permute-start.32 = (bf16[512,2048]{1,0:T(8,128)(2,1)}, bf16[512,2048]{1,0:T(8,128)(2,1)}, u32[]{:S(2)}, u32[]{:S(2)}) collective-permute-start(bf16[512,2048]{1,0:T(8,128)(2,1)} %add_convert_fusion.1), channel_id=1, source_target_pairs={{0,1},{1,0},{2,3},{3,2},{4,5},{5,4},{6,7},{7,6},{8,9},{9,8},{10,11... | collective-permute-start | bytes 6291464 | tf_op jit(solution)/shard_map/ppermute | solution.py:628
  449.2 33.4 %collective-permute-start.77 = (f32[1024,128]{1,0:T(8,128)}, f32[1024,128]{1,0:T(8,128)}, u32[]{:S(2)}, u32[]{:S(2)}) collective-permute-start(f32[1024,128]{1,0:T(8,128)} %get-tuple-element.113), channel_id=1, source_target_pairs={{0,2},{2,0},{4,6},{6,4},{8,10},{10,8},{12,14},{14,12},{16,18},{18,... | collective-permute-start | bytes 1572872 | tf_op jit(solution)/shard_map/ppermute | solution.py:66
  492.9 31.8 %collective-permute-start.82 = (f32[3328]{0:T(1024)S(1)}, f32[3328]{0:T(1024)S(1)}, u32[]{:S(2)}, u32[]{:S(2)}) collective-permute-start(f32[3328]{0:T(1024)S(1)} %slice.386), channel_id=1, source_target_pairs={{0,2},{2,0},{4,6},{6,4},{8,10},{10,8},{12,14},{14,12},{16,18},{18,... | collective-permute-start | bytes 39944 | tf_op jit(solution)/shard_map/ppermute | solution.py:66
  (116 other events, 1364.0 us)

commit v2 on v1

v2 whole, which is shorter than its diff:
```python
import functools

import jax
import jax.numpy as jnp
from jax import lax
from jax.experimental import pallas as pl
from jax.experimental.pallas import tpu as pltpu
from jax.sharding import PartitionSpec as P

EPS = 1e-05
Q = 128
NEG = -1e30
F32 = jnp.float32
BF16 = jnp.bfloat16
HIGH = lax.Precision.HIGHEST
MIB = 1024 * 1024
HEAD = 64
STATE = 128


BRIEF = pl.CostEstimate(flops=1, bytes_accessed=1, transcendentals=0)


def dot(a, b, dims, precision=None):
    return lax.dot_general(a, b, (dims, ((), ())), precision=precision, preferred_element_type=F32)


def params(mib):
    return pltpu.CompilerParams(vmem_limit_bytes=mib * MIB)


def after(value, *others):
    return lax.optimization_barrier((value, others))[0]


def ring_order(chips):
    if chips == 8:
        return [0, 2, 4, 6, 7, 5, 3, 1]
    half = chips // 2
    return list(range(half)) + list(range(chips - 1, half - 1, -1))


class Ring:
    def __init__(self, n_dp):
        self.n = n_dp // 2
        self.order = ring_order(self.n)
        place = [0] * self.n
        for position, chip in enumerate(self.order):
            place[chip] = position
        me = lax.axis_index("dp")
        self.core = me % 2
        self.mine = me // 2
        self.pos = jnp.asarray(place, jnp.int32)[self.mine]
        self.right = self.perm(1)
        self.left = self.perm(-1)
        self.full = self.n // 2 - 1

    def perm(self, step):
        pairs = []
        for p in range(self.n):
            for c in range(2):
                pairs.append((self.order[p] * 2 + c, self.order[(p + step) % self.n] * 2 + c))
        return pairs

    def table(self):
        table = [[self.order[(p + s) % self.n] for s in range(self.n)] for p in range(self.n)]
        row = lax.dynamic_index_in_dim(jnp.asarray(table, jnp.int32), self.pos, 0, keepdims=False)
        return jnp.concatenate([row, self.core.reshape(1).astype(jnp.int32)])

    def offsets(self, dd):
        steps = [0] + [-k for k in range(1, self.full + 1)] + list(range(1, self.full + 1)) + [self.n // 2]
        table = [[self.order[(p + s) % self.n] * dd for s in steps] for p in range(self.n)]
        return lax.dynamic_index_in_dim(jnp.asarray(table, jnp.int32), self.pos, 0, keepdims=False)

    def go_right(self, v):
        return lax.ppermute(v, "dp", self.right)

    def go_left(self, v):
        return lax.ppermute(v, "dp", self.left)

    def swap(self, v):
        return lax.ppermute(v, "dp", [(i, i ^ 1) for i in range(2 * self.n)])

    def ahead(self, k):
        pairs = []
        for chip in range(self.n):
            for c in range(2):
                pairs.append((chip * 2 + c, (chip + k) % self.n * 2 + c))
        return pairs


class Gather:
    def __init__(self, ring, unit, far, cut=None):
        self.ring, self.far, self.cut = ring, far, cut
        self.r, self.l = [unit], [unit]
        self.last = []

    def step(self):
        self.r.append(self.ring.go_right(self.r[-1]))
        self.l.append(self.ring.go_left(self.l[-1]))
        return self.newest()

    def newest(self):
        return self.r[-1], self.l[-1]

    def finish(self):
        while len(self.r) <= self.ring.full:
            self.step()
        r, l, cut = self.r[-1], self.l[-1], self.cut
        if self.far == "both":
            self.last = [self.ring.go_right(r[:cut]), self.ring.go_left(l[cut:])]
        elif self.far == "right":
            self.last = [self.ring.go_right(r)]
        else:
            self.last = [self.ring.go_left(l)]
        return self.last

    def blocks(self):
        return self.r + self.l[1:] + self.last


def both_parts(vt, own, other):
    half = own.shape[0]
    return dot(vt[:, :half], own[...], (((1,), (0,)))) + dot(vt[:, half:], other[...], (((1,), (0,))))


def term_kernel(plan, table, vt, *refs):
    i, half = pl.program_id(0), pl.num_programs(0) // 2
    n = len(plan)
    acts, refs = refs[: 2 * n], refs[2 * n :]
    came, outs = refs[: sum(p != "" for p in plan)], refs[sum(p != "" for p in plan) :]
    k = 0
    for b in range(n):
        total = both_parts(vt, acts[2 * b], acts[2 * b + 1])
        if plan[b]:
            part = came[k][...].astype(F32)
            k += 1
            if plan[b] == "top":
                part = jnp.where(i < half, part, 0.0)
            elif plan[b] == "bottom":
                part = jnp.where(i >= half, part, 0.0)
            total = total + part
        outs[b][...] = total.astype(BF16)


def far_kernel(table, vt, own, other, top, bottom):
    i, half = pl.program_id(0), pl.num_programs(0) // 2
    total = both_parts(vt, own, other).astype(BF16)

    @pl.when(i < half)
    def _():
        top[...] = total

    @pl.when(i >= half)
    def _():
        bottom[...] = total


def last_kernel(table, vt, own, other, r, l, keep, give):
    total = both_parts(vt, own, other) + r[...].astype(F32) + l[...].astype(F32)
    dd = keep.shape[1]
    core = table[table.shape[0] - 1]
    low, high = total[:, :dd], total[:, dd:]
    keep[...] = jnp.where(core == 0, low, high)
    give[...] = jnp.where(core == 0, high, low)


class Scatter:
    def __init__(self, ring, table, vt, acts, dd, far):
        self.ring, self.table, self.vt, self.acts, self.dd, self.far = ring, table, vt, acts, dd, far
        self.rows = vt.shape[0]
        self.tile = self.rows // 2
        self.left_to_do = ring.full
        opposite = ring.n // 2
        if far == "both":
            self.out = self.call(far_kernel, (), [opposite], [], ["top", "bottom"])
        else:
            self.out = self.call(functools.partial(term_kernel, [""]), (), [opposite], [], ["all"])
        self.send()

    def spec(self, kind, lanes):
        half = self.rows // self.tile // 2
        if kind == "top":
            return pl.BlockSpec((self.tile, lanes), lambda i, a: (jnp.minimum(i, half - 1), 0))
        if kind == "bottom":
            return pl.BlockSpec((self.tile, lanes), lambda i, a: (jnp.maximum(i - half, 0), 0))
        return pl.BlockSpec((self.tile, lanes), lambda i, a: (i, 0))

    def call(self, kernel, others, steps, came, kinds, lanes=None, dtype=BF16):
        table = after(self.table, *others) if others else self.table
        tokens = self.vt.shape[1]
        lanes = lanes or self.dd
        half = self.rows // 2
        columns = []
        for step in steps:
            place = step % self.ring.n
            columns += [pl.BlockSpec((tokens // 2, self.dd), lambda i, a, place=place: (0, a[place]))] * 2
        shape = lambda kind: jax.ShapeDtypeStruct((half if kind in ("top", "bottom") else self.rows, lanes), dtype)
        return pl.pallas_call(
            kernel,
            out_shape=tuple(shape(k) for k in kinds),
            grid_spec=pltpu.PrefetchScalarGridSpec(
                num_scalar_prefetch=1,
                grid=(self.rows // self.tile,),
                in_specs=[pl.BlockSpec((self.tile, tokens), lambda i, a: (i, 0))]
                + columns
                + [self.spec(kind, self.dd) for kind, _ in came],
                out_specs=tuple(self.spec(k, lanes) for k in kinds),
            ),
            compiler_params=params(20),
            cost_estimate=BRIEF,
        )(table, self.vt, *(self.acts * len(steps)), *[v for _, v in came])

    def send(self):
        self.r = self.l = None
        if self.far != "left" or len(self.out) == 2:
            self.r = self.ring.go_right(self.out[0])
        if self.far != "right" or len(self.out) == 2:
            self.l = self.ring.go_left(self.out[-1])

    def step(self, *others):
        if not self.left_to_do:
            return self.out
        j, ring = self.left_to_do, self.ring
        split = j == ring.full and self.far == "both"
        plan, came = [], []
        for kind, v in (("top", self.r), ("bottom", self.l)):
            kind = kind if split else "all"
            plan.append("" if v is None else kind)
            if v is not None:
                came.append((kind, v))
        self.out = self.call(functools.partial(term_kernel, plan), others, [j, -j], came, ["all", "all"])
        self.left_to_do -= 1
        self.send()
        return self.out

    def finish(self, *others):
        while self.left_to_do:
            self.step()
        return self.call(
            last_kernel, others, [0], [("all", self.r), ("all", self.l)], ["all", "all"], self.dd // 2, F32
        )


def prep_x_kernel(place, own, other, small_own, small_other, out):
    core = place[0]
    dd = own.shape[1]
    chans = own.shape[2] // 2
    padded = out.shape[0] - chans - STATE
    for b in range(2):
        lanes = slice(b * dd, (b + 1) * dd)
        near = core == b
        src = jnp.where(near, own[0], other[0])
        src = jnp.where(core == 0, src[:, :chans], src[:, chans:])
        out[:chans, lanes] = src.T
        small = jnp.where(near, small_own[...], small_other[...])
        states = jnp.where(core == 0, small[:, :STATE], small[:, STATE : 2 * STATE])
        out[chans : chans + STATE, lanes] = states.T
        steps = jnp.where(core == 0, small[:, 2 * STATE : 3 * STATE], small[:, 3 * STATE :])
        out[chans + STATE :, lanes] = steps.T[:padded]


def prep_x(place, own, other, small_own, small_other, padded):
    _, dd, inner = own.shape
    rows = inner // 2 + STATE + padded
    return pl.pallas_call(
        prep_x_kernel,
        out_shape=jax.ShapeDtypeStruct((rows, 2 * dd), BF16),
        grid_spec=pltpu.PrefetchScalarGridSpec(
            num_scalar_prefetch=1,
            grid=(1,),
            in_specs=[pl.BlockSpec((1, dd, inner), lambda i, p: (1, 0, 0))] * 2
            + [pl.BlockSpec((dd, 4 * STATE), lambda i, p: (0, 0))] * 2,
            out_specs=pl.BlockSpec((rows, 2 * dd), lambda i, p: (0, 0)),
        ),
        compiler_params=params(12),
        cost_estimate=BRIEF,
    )(place, own, other, small_own, small_other)


def prep_zo_kernel(place, own, other, out_own, out_other, z, o):
    core = place[0]
    dd = own.shape[1]
    chans = own.shape[2] // 2
    for b in range(2):
        lanes = slice(b * dd, (b + 1) * dd)
        near = core == b
        src = jnp.where(near, own[0], other[0])
        src = jnp.where(core == 0, src[:, :chans], src[:, chans:])
        z[:, lanes] = src.T
        src = jnp.where(near, out_own[...], out_other[...])
        o[:, lanes] = jnp.where(core == 0, src[:chans], src[chans:])


def prep_zo(place, own, other, out_own, out_other):
    _, dd, inner = own.shape
    shape = (inner // 2, 2 * dd)
    return pl.pallas_call(
        prep_zo_kernel,
        out_shape=(jax.ShapeDtypeStruct(shape, BF16),) * 2,
        grid_spec=pltpu.PrefetchScalarGridSpec(
            num_scalar_prefetch=1,
            grid=(1,),
            in_specs=[pl.BlockSpec((1, dd, inner), lambda i, p: (0, 0, 0))] * 2
            + [pl.BlockSpec((inner, dd), lambda i, p: (0, 0))] * 2,
            out_specs=(pl.BlockSpec(shape, lambda i, p: (0, 0)),) * 2,
        ),
        compiler_params=params(12),
        cost_estimate=BRIEF,
    )(place, own, other, out_own, out_other)


class Weight:
    def __init__(self, blocks, first, rows, cut=None):
        self.args, self.specs, self.plan = [], [], []
        self.rows, self.dd = rows, blocks[0].shape[1]

        def view(array, start, size):
            index = start // size
            self.args.append(array)
            self.specs.append(pl.BlockSpec((size, self.dd), lambda i, o, index=index: (index, 0)))

        whole = blocks if cut is None else blocks[:-2]
        for block in whole:
            view(block, first, rows)
            self.plan.append(1)
        if cut is not None:
            pieces = 0
            if first < cut:
                view(blocks[-2], first, min(rows, cut - first))
                pieces += 1
            if first + rows > cut:
                start = max(first, cut)
                view(blocks[-1], start - cut, first + rows - start)
                pieces += 1
            self.plan.append(pieces)

    def read(self, refs):
        at, out = 0, []
        for pieces in self.plan:
            part = [r[...] for r in refs[at : at + pieces]]
            out.append(part[0] if pieces == 1 else jnp.concatenate(part, axis=0))
            at += pieces
        return out


def projected(weight, refs, act, offs):
    total = None
    for b, w in enumerate(weight.read(refs)):
        off = pl.multiple_of(offs[b], weight.dd)
        part = dot(w, act[:, pl.ds(off, weight.dd)], (((1,), (1,))))
        total = part if total is None else total + part
    return total


def projection(body, weight, acts, offs, extra, extra_specs, out_shape, out_specs, mib=40):
    tile, width = acts[0].shape
    tokens = 2 * tile
    n = len(weight.args)

    def kernel(offs, *refs):
        for k in range(2):

            @pl.when(pl.program_id(0) == k)
            def _():
                acc = projected(weight, refs[:n], refs[n + k], offs)
                body(acc, refs[n + 2 : n + 2 + len(extra)], refs[n + 2 + len(extra) :])

    return pl.pallas_call(
        kernel,
        out_shape=out_shape,
        grid_spec=pltpu.PrefetchScalarGridSpec(
            num_scalar_prefetch=1,
            grid=(tokens // tile,),
            in_specs=weight.specs + [pl.BlockSpec((tile, width), lambda i, o: (0, 0))] * 2 + extra_specs,
            out_specs=out_specs,
        ),
        compiler_params=params(mib),
        cost_estimate=BRIEF,
    )(offs, *weight.args, *acts, *extra)


def plain_projection(weight, acts, offs):
    tile = acts[0].shape[0]

    def body(acc, extra, outs):
        outs[0][...] = acc

    return projection(
        body, weight, acts, offs, (), [],
        jax.ShapeDtypeStruct((weight.rows, 2 * tile), F32),
        pl.BlockSpec((weight.rows, tile), lambda i, o: (0, i)),
    )


def two_projections(first, second, acts, offs):
    tile, width = acts[0].shape
    n, m = len(first.args), len(second.args)

    def kernel(offs, *refs):
        parts = [jnp.concatenate(p, axis=0) for p in zip(first.read(refs[:n]), second.read(refs[n : n + m]))]
        for k in range(2):
            total = None
            for b, w in enumerate(parts):
                off = pl.multiple_of(offs[b], first.dd)
                part = dot(w, refs[n + m + k][:, pl.ds(off, first.dd)], (((1,), (1,))))
                total = part if total is None else total + part
            refs[-2][:, k * tile : (k + 1) * tile] = total[: first.rows]
            refs[-1][:, k * tile : (k + 1) * tile] = total[first.rows :]

    whole = lambda i, o: (0, 0)
    return pl.pallas_call(
        kernel,
        out_shape=tuple(jax.ShapeDtypeStruct((w.rows, 2 * tile), F32) for w in (first, second)),
        grid_spec=pltpu.PrefetchScalarGridSpec(
            num_scalar_prefetch=1,
            grid=(1,),
            in_specs=first.specs + second.specs + [pl.BlockSpec((tile, width), whole)] * 2,
            out_specs=tuple(pl.BlockSpec((w.rows, 2 * tile), whole) for w in (first, second)),
        ),
        compiler_params=params(40),
        cost_estimate=BRIEF,
    )(offs, *first.args, *second.args, *acts)


def sigmoid(v):
    return 0.5 * jnp.tanh(0.5 * v) + 0.5


def gate_projection(weight, acts, offs, y):
    rows, tokens = y.shape
    tile = tokens // 2

    def body(z, extra, outs):
        outs[0][...] = z
        g = extra[0][...] * (z * sigmoid(z))
        outs[1][...] = jnp.sum(g * g, axis=0, keepdims=True)

    wide = pl.BlockSpec((rows, tile), lambda i, o: (0, i))
    line = pl.BlockSpec((1, tile), lambda i, o: (0, i))
    return projection(
        body, weight, acts, offs, (y,), [wide],
        (jax.ShapeDtypeStruct((rows, tokens), F32), jax.ShapeDtypeStruct((1, tokens), F32)),
        (wide, line),
    )


def back_projection(weight, acts, offs, y, z, gain):
    rows, tokens = y.shape
    tile = tokens // 2

    def body(dyn, extra, outs):
        y, z, gain = extra
        outs[0][...] = dyn
        zv = z[...]
        g = y[...] * (zv * sigmoid(zv))
        outs[1][...] = jnp.sum(dyn * gain[...] * g, axis=0, keepdims=True)

    wide = pl.BlockSpec((rows, tile), lambda i, o: (0, i))
    line = pl.BlockSpec((1, tile), lambda i, o: (0, i))
    return projection(
        body, weight, acts, offs, (y, z, gain),
        [wide, wide, pl.BlockSpec((rows, 1), lambda i, o: (0, 0))],
        (jax.ShapeDtypeStruct((rows, tokens), F32), jax.ShapeDtypeStruct((1, tokens), F32)),
        (wide, line),
    )


def back(groups, offs, width, base=None, hiddens=None):
    dd = groups[0][0].dd
    tokens = groups[0][1].shape[1]
    half = tokens // 2
    args, specs = [], []
    flops = 0
    for weight, vt in groups:
        args += weight.args + [vt]
        specs += weight.specs + [pl.BlockSpec((vt.shape[0], tokens), lambda i, o: (0, 0))]
        flops += 2 * vt.shape[0] * tokens * width
    out_spec = pl.BlockSpec((half, width), lambda i, o: (0, 0))
    if base is not None:
        args += list(base)
        specs += [out_spec, out_spec]
    shapes = [jax.ShapeDtypeStruct((half, width), BF16)] * 2
    out_specs = [out_spec, out_spec]
    if hiddens is not None:
        args += list(hiddens)
        specs += [out_spec, out_spec]
        shapes.append(jax.ShapeDtypeStruct((1, width), F32))
        out_specs.append(pl.BlockSpec((1, width), lambda i, o: (0, 0)))

    def kernel(offs, *refs):
        outs = refs[len(args) :]
        at, terms = 0, []
        for weight, _ in groups:
            n = len(weight.args)
            terms.append((refs[at + n][...].T, weight.read(refs[at : at + n])))
            at += n + 1
        scales = []
        if hiddens is not None:
            for h in refs[len(args) - 2 : len(args)]:
                v = h[...].astype(F32)
                scales.append(lax.rsqrt(jnp.mean(v * v, axis=1, keepdims=True) + EPS))
        for b in range(len(terms[0][1])):
            off = pl.multiple_of(offs[b], dd)
            along = None
            total = None
            for v, blocks in terms:
                part = dot(v, blocks[b], (((1,), (0,))))
                total = part if total is None else total + part
            for k in range(2):
                part = total[k * half : (k + 1) * half]
                if base is not None:
                    part = part + refs[at + k][:, pl.ds(off, dd)].astype(F32)
                outs[k][:, pl.ds(off, dd)] = part.astype(BF16)
                if hiddens is not None:
                    h = refs[len(args) - 2 + k][:, pl.ds(off, dd)].astype(F32)
                    line = jnp.sum(part * (h * scales[k]), axis=0, keepdims=True)
                    along = line if along is None else along + line
            if hiddens is not None:
                outs[2][:, pl.ds(off, dd)] = along

    return pl.pallas_call(
        kernel,
        out_shape=tuple(shapes),
        grid_spec=pltpu.PrefetchScalarGridSpec(
            num_scalar_prefetch=1, grid=(1,), in_specs=specs, out_specs=tuple(out_specs)
        ),
        compiler_params=params(40),
        cost_estimate=BRIEF,
    )(offs, *args)


def messages_kernel(n, table, rows_ref, own, other, common, *refs):
    outs, terms = refs[:n], refs[n]
    rows = rows_ref.shape[0]
    dd = outs[0].shape[1]
    terms[...] = both_parts(rows_ref, own, other)
    me = table[0]
    for k in range(n):
        off = pl.multiple_of(lax.rem(me + k, n) * dd, dd)
        outs[k][:rows, :] = terms[:, pl.ds(off, dd)].astype(BF16)
        outs[k][rows:, :] = common[...].astype(BF16)


def messages(ring, table, rows, acts, common):
    dd = common.shape[1]
    m, tokens = rows.shape
    width = acts[0].shape[1]
    whole = lambda i, t: (0, 0)
    shape = (m + common.shape[0], dd)
    return pl.pallas_call(
        functools.partial(messages_kernel, ring.n),
        out_shape=(jax.ShapeDtypeStruct(shape, BF16),) * ring.n,
        grid_spec=pltpu.PrefetchScalarGridSpec(
            num_scalar_prefetch=1,
            grid=(1,),
            in_specs=[pl.BlockSpec((m, tokens), whole)]
            + [pl.BlockSpec((tokens // 2, width), whole)] * 2
            + [pl.BlockSpec(common.shape, whole)],
            out_specs=(pl.BlockSpec(shape, whole),) * ring.n,
            scratch_shapes=[pltpu.VMEM((m, width), F32)],
        ),
        compiler_params=params(20),
        cost_estimate=BRIEF,
    )(table, rows, *acts, common)


def norm_back_kernel(own, came, hidden, cot, gain, out):
    h = hidden[...].astype(F32)
    width = h.shape[1]
    r = lax.rsqrt(jnp.mean(h * h, axis=1, keepdims=True) + EPS)
    weighted = (own[...].astype(F32) + came[...].astype(F32)) * gain[...]
    along = jnp.sum(weighted * h, axis=1, keepdims=True) * (1.0 / width)
    out[...] = (weighted * r - h * (r * r * r * along) + cot[...].astype(F32)).astype(BF16)


def norm_back(own, came, hidden, cot, gain):
    rows, width = own.shape
    tile = 128
    block = pl.BlockSpec((tile, width), lambda i: (i, 0))
    return pl.pallas_call(
        norm_back_kernel,
        grid=(rows // tile,),
        out_shape=jax.ShapeDtypeStruct((rows, width), BF16),
        in_specs=[block] * 4 + [pl.BlockSpec((1, width), lambda i: (0, 0))],
        out_specs=block,
        compiler_params=params(16),
        cost_estimate=BRIEF,
    )(own, came, hidden, cot, gain)


def turn_kernel(place, *refs):
    out = refs[-1]
    chans = refs[0].shape[0]
    first = place[0] == 0
    for k in range(2):
        own, other = refs[2 * k][...], refs[2 * k + 1][...]
        out[k, :, :chans] = jnp.where(first, own, other).T
        out[k, :, chans:] = jnp.where(first, other, own).T


def turn(place, *parts):
    chans, dd = parts[0].shape
    return pl.pallas_call(
        turn_kernel,
        out_shape=jax.ShapeDtypeStruct((2, dd, 2 * chans), F32),
        grid_spec=pltpu.PrefetchScalarGridSpec(
            num_scalar_prefetch=1,
            grid=(1,),
            in_specs=[pl.BlockSpec((chans, dd), lambda i, p: (0, 0))] * 4,
            out_specs=pl.BlockSpec((2, dd, 2 * chans), lambda i, p: (0, 0, 0)),
        ),
        compiler_params=params(16),
        cost_estimate=BRIEF,
    )(place, *parts)


def gate_back_kernel(total, dyn, y, z, s, q, gain, dz, dy, dgain):
    zv, yv, sv = z[...], y[...], s[...]
    sig = sigmoid(zv)
    silu = zv * sig
    g = yv * silu
    scaled = dyn[...] * sv
    dgain[...] = jnp.sum(scaled * g, axis=1, keepdims=True)
    dg = scaled * gain[...] - g * (sv * sv * sv * q[...] * (1.0 / total))
    dz[...] = (dg * yv * (sig * (1.0 + zv * (1.0 - sig)))).astype(BF16)
    dy[...] = (dg * silu).astype(BF16)


def gate_back(total, dyn, y, z, s, q, gain):
    rows, tokens = dyn.shape
    tile = rows // 4
    wide = pl.BlockSpec((tile, tokens), lambda i: (i, 0))
    line = pl.BlockSpec((1, tokens), lambda i: (0, 0))
    return pl.pallas_call(
        functools.partial(gate_back_kernel, float(total)),
        grid=(rows // tile,),
        out_shape=(jax.ShapeDtypeStruct((rows, tokens), BF16),) * 2
        + (jax.ShapeDtypeStruct((rows, 1), F32),),
        in_specs=[wide, wide, wide, line, line, pl.BlockSpec((tile, 1), lambda i: (i, 0))],
        out_specs=(wide, wide, pl.BlockSpec((tile, 1), lambda i: (i, 0))),
        compiler_params=params(24),
        cost_estimate=BRIEF,
    )(dyn, y, z, s, q, gain)


def head_terms(raw, hp_ref):
    pre = raw + hp_ref[:, 0:1]
    small = jnp.exp(-jnp.abs(pre))
    one = 1.0 + small
    away = one - 1.0
    log1p = jnp.where(away == 0.0, small, jnp.log(one) * (small / jnp.where(away == 0.0, 1.0, away)))
    dt = jnp.maximum(pre, 0.0) + log1p
    logistic = jnp.where(pre >= 0.0, 1.0, small) / one
    rows = lax.broadcasted_iota(jnp.int32, (Q, Q), 0)
    lanes = lax.broadcasted_iota(jnp.int32, (Q, Q), 1)
    upto = (rows <= lanes).astype(F32)
    logs = dt * hp_ref[:, 1:2]
    cums = dot(logs, upto, (((1,), (0,))), HIGH)
    return dt, logistic, cums


def to_columns(cums):
    n = cums.shape[0]
    square = jnp.concatenate([cums, jnp.zeros((Q - n, Q), F32)], axis=0)
    return square.T


def pair_bias(segr_ref, segc_ref):
    rows = lax.broadcasted_iota(jnp.int32, (Q, Q), 0)
    lanes = lax.broadcasted_iota(jnp.int32, (Q, Q), 1)
    keep = (segc_ref[...] == segr_ref[...]) & (rows <= lanes)
    return jnp.where(keep, 0.0, NEG)


def state_rows(place, own, other, r0):
    at = r0 % STATE
    rows = slice(at, at + HEAD)
    return jnp.where(place[0] == r0 // STATE, own[rows, :], other[rows, :])


def fwd_kernel(
    heads, given, place, xr_ref, bco_ref, bcs_ref, dt_ref, mask_ref, segr_ref, segc_ref, par_ref, hp_ref, *rest
):
    y_ref, xa_ref, u_ref, s_ref, prev, state, parb, xt = rest[given:]
    chans = heads * HEAD
    wide = chans + 2 * STATE

    @pl.when(pl.program_id(0) == 0)
    def _():
        for k in range(6):
            parb[k] = jnp.broadcast_to(par_ref[:, k : k + 1], (wide, Q))
        prev[...] = jnp.zeros_like(prev)
        state[...] = jnp.zeros_like(state)

    lane = lax.broadcasted_iota(jnp.int32, (HEAD, Q), 1)
    m1, m2, m3 = mask_ref[0:1, :], mask_ref[1:2, :], mask_ref[2:3, :]

    def conv(r0):
        rows = slice(r0, r0 + HEAD)
        cur = xr_ref[rows, :] if r0 < chans else state_rows(place, bco_ref, bcs_ref, r0 - chans)
        old = prev[rows, :]
        u = parb[4, rows, :] + parb[3, rows, :] * cur
        u = u + parb[2, rows, :] * (m1 * pltpu.roll(jnp.where(lane >= Q - 1, old, cur), 1, 1))
        u = u + parb[1, rows, :] * (m2 * pltpu.roll(jnp.where(lane >= Q - 2, old, cur), 2, 1))
        u = u + parb[0, rows, :] * (m3 * pltpu.roll(jnp.where(lane >= Q - 3, old, cur), 3, 1))
        prev[rows, :] = cur
        u_ref[rows, :] = u
        xa = (u * (0.5 * jnp.tanh(0.5 * u) + 0.5)).astype(BF16)
        xa_ref[rows, :] = xa
        return xa

    for r0 in range(chans, wide, HEAD):
        conv(r0)
    bt = xa_ref[chans : chans + STATE, :]
    ct = xa_ref[chans + STATE : wide, :]
    mix = dot(bt.T, ct, (((1,), (0,))))
    dt, _, cums = head_terms(dt_ref[...], hp_ref)
    cols = to_columns(cums)
    bias = pair_bias(segr_ref, segc_ref)
    enter = jnp.exp(cums) * mask_ref[3:4, :]
    last = jnp.broadcast_to(cums[:, Q - 1 : Q], cums.shape)
    tail = jnp.exp(last - cums) * mask_ref[4:5, :]
    passing = jnp.exp(last) * mask_ref[5:6, :]
    s_in = state[...].astype(BF16)
    s_ref[...] = s_in
    carried = dot(s_in, ct, (((1,), (0,))))
    for h in range(heads):
        rows = slice(h * HEAD, (h + 1) * HEAD)
        xa = conv(h * HEAD).astype(F32)
        decay = jnp.exp(cums[h : h + 1, :] - cols[:, h : h + 1] + bias)
        mixing = (mix * decay).astype(BF16)
        xd = xa * dt[h : h + 1, :]
        xt[rows, :] = (xd * tail[h : h + 1, :]).astype(BF16)
        y = dot(xd.astype(BF16), mixing, (((1,), (0,))))
        y = y + enter[h : h + 1, :] * carried[rows, :] + parb[5, rows, :] * xa
        y_ref[rows, :] = y
    fresh = dot(xt[...], bt, (((1,), (1,))))
    for h in range(heads):
        rows = slice(h * HEAD, (h + 1) * HEAD)
        state[rows, :] = state[rows, :] * passing[h : h + 1, :] + fresh[rows, :]


def scan_forward(place, xr, bco, bcs, dtr, masks, segr, segc, par, hp, heads, seqs, seq, given=()):
    chans, tokens = xr.shape
    padded = dtr.shape[0]
    wide = chans + 2 * STATE
    count = tokens // seqs // Q
    at = lambda k, p: (0, seq * count + k)
    swapped = lambda k, p: (0, (seqs - 1 - seq) * count + k)
    whole = lambda k, p: (0, 0)
    args = (xr, bco, bcs, dtr, masks, segr, segc, par, hp)
    return pl.pallas_call(
        functools.partial(fwd_kernel, heads, len(given)),
        out_shape=(
            jax.ShapeDtypeStruct((chans, tokens), F32),
            jax.ShapeDtypeStruct((wide, tokens), BF16),
            jax.ShapeDtypeStruct((wide, tokens), F32),
            jax.ShapeDtypeStruct((chans, tokens), BF16),
        ),
        grid_spec=pltpu.PrefetchScalarGridSpec(
            num_scalar_prefetch=1,
            grid=(count,),
            in_specs=[
                pl.BlockSpec((chans, Q), at),
                pl.BlockSpec((STATE, Q), at),
                pl.BlockSpec((STATE, Q), swapped),
                pl.BlockSpec((padded, Q), at),
                pl.BlockSpec((8, Q), at),
                pl.BlockSpec((1, Q), at),
                pl.BlockSpec((Q, 1), lambda k, p: (seq * count + k, 0)),
                pl.BlockSpec(par.shape, whole),
                pl.BlockSpec(hp.shape, whole),
            ]
            + [pl.BlockSpec(memory_space=pl.ANY)] * len(given),
            out_specs=(
                pl.BlockSpec((chans, Q), at),
                pl.BlockSpec((wide, Q), at),
                pl.BlockSpec((wide, Q), at),
                pl.BlockSpec((chans, STATE), at),
            ),
            scratch_shapes=[
                pltpu.VMEM((wide, Q), F32),
                pltpu.VMEM((chans, STATE), F32),
                pltpu.VMEM((6, wide, Q), F32),
                pltpu.VMEM((chans, Q), BF16),
            ],
        ),
        input_output_aliases={1 + len(args) + k: k for k in range(len(given))},
        compiler_params=params(58),
        cost_estimate=BRIEF,
    )(place, *args, *given)


def bwd_kernel(
    heads, given, place, xr_ref, bco_ref, bcs_ref, dt_ref, mask_ref, segr_ref, segc_ref, par_ref, hp_ref, xa_ref,
    u_ref, s_ref,
    dy_ref, y_ref, *rest,
):
    dx_ref, dbc_ref, ddt_ref, cgo_ref, hg_ref, dstate, parb, after, nmask, xt, dye, cg_ref = rest[given:]
    chans = heads * HEAD
    wide = chans + 2 * STATE

    @pl.when(pl.program_id(0) == 0)
    def _():
        for k in range(6):
            parb[k] = jnp.broadcast_to(par_ref[:, k : k + 1], (wide, Q))
        cg_ref[...] = jnp.zeros_like(cg_ref)
        hg_ref[...] = jnp.zeros_like(hg_ref)
        dstate[...] = jnp.zeros_like(dstate)
        after[...] = jnp.zeros_like(after)
        nmask[...] = jnp.zeros_like(nmask)

    lane = lax.broadcasted_iota(jnp.int32, (HEAD, Q), 1)
    lane8 = lax.broadcasted_iota(jnp.int32, (8, Q), 1)
    sub8 = lax.broadcasted_iota(jnp.int32, (8, Q), 0)
    masks = mask_ref[...]
    shifted_masks = jnp.where(lane8 <= sub8, nmask[...], masks)
    nmask[...] = masks

    def conv_back(r0, dxa, out, out0):
        rows = slice(r0, r0 + HEAD)
        u = u_ref[rows, :]
        sig = 0.5 * jnp.tanh(0.5 * u) + 0.5
        dc = dxa * (sig * (1.0 + u * (1.0 - sig)))
        xr = xr_ref[rows, :] if r0 < chans else state_rows(place, bco_ref, bcs_ref, r0 - chans)
        old = after[rows, :]
        after[rows, :] = dc
        dx = parb[3, rows, :] * dc
        cg_ref[4, rows, :] += dc
        cg_ref[3, rows, :] += xr * dc
        for k in (1, 2, 3):
            e = jnp.where(lane < k, old, dc) * shifted_masks[k - 1 : k, :]
            e = pltpu.roll(e, Q - k, 1)
            dx = dx + parb[3 - k, rows, :] * e
            cg_ref[3 - k, rows, :] += xr * e
        out[out0 : out0 + HEAD, :] = dx.astype(out.dtype)

    bt = xa_ref[chans : chans + STATE, :]
    ct = xa_ref[chans + STATE : wide, :]
    mix = dot(bt.T, ct, (((1,), (0,))))
    dt, logistic, cums = head_terms(dt_ref[...], hp_ref)
    cols = to_columns(cums)
    bias = pair_bias(segr_ref, segc_ref)
    enter = jnp.exp(cums) * masks[3:4, :]
    last = jnp.broadcast_to(cums[:, Q - 1 : Q], cums.shape)
    tail = jnp.exp(last - cums) * masks[4:5, :]
    passing = jnp.exp(last) * masks[5:6, :]
    ds = dstate[...].astype(BF16)
    spread = dot(ds, bt, (((1,), (0,))))
    dmix = jnp.zeros((Q, Q), F32)
    s_in = s_ref[...]
    direct, cross, skip, outward, through, inward = [], [], [], [], [], []
    for h in range(heads):
        rows = slice(h * HEAD, (h + 1) * HEAD)
        xa = xa_ref[rows, :].astype(F32)
        dyb = dy_ref[rows, :]
        dy = dyb.astype(F32)
        decay = jnp.exp(cums[h : h + 1, :] - cols[:, h : h + 1] + bias)
        mixing = (mix * decay).astype(BF16)
        xd = xa * dt[h : h + 1, :]
        xdb = xd.astype(BF16)
        xt[rows, :] = (xd * tail[h : h + 1, :]).astype(BF16)
        dye[rows, :] = (dy * enter[h : h + 1, :]).astype(BF16)
        dmix = dmix + dot(xdb, dyb, (((0,), (0,)))) * decay
        near = dot(dyb, mixing, (((1,), (1,))))
        far = tail[h : h + 1, :] * spread[rows, :]
        pull = near + far
        direct.append(jnp.sum(xa * pull, axis=0, keepdims=True))
        cross.append(jnp.sum(xdb.astype(F32) * near, axis=0, keepdims=True))
        outward.append(jnp.sum(xd * far, axis=0, keepdims=True))
        through.append(jnp.sum(dstate[rows, :] * s_in[rows, :].astype(F32), axis=0, keepdims=True))
        skip.append(jnp.sum(xa * dy, axis=0, keepdims=True))
        inward.append(jnp.sum(y_ref[rows, :] * dy, axis=0, keepdims=True))
        dxa = dt[h : h + 1, :] * pull + parb[5, rows, :] * dy
        conv_back(h * HEAD, dxa, dx_ref, h * HEAD)
    pad = ddt_ref.shape[0] - heads
    if pad:
        zero = [jnp.zeros((pad, Q), F32)]
        direct, cross, skip = direct + zero, cross + zero, skip + zero
        outward, through, inward = outward + zero, through + zero, inward + zero
    direct, cross, skip, outward, through, inward = (
        jnp.concatenate(v, axis=0) for v in (direct, cross, skip, outward, through, inward)
    )
    dlog = inward - hp_ref[:, 2:3] * skip - cross
    rows = lax.broadcasted_iota(jnp.int32, (Q, Q), 0)
    lanes = lax.broadcasted_iota(jnp.int32, (Q, Q), 1)
    dl = dot(dlog, (rows >= lanes).astype(F32), (((1,), (0,))), HIGH)
    dl = dl + dot(outward, (rows < lanes).astype(F32), (((1,), (0,))), HIGH)
    dl = dl + passing * jnp.sum(through, axis=1, keepdims=True)
    ddt = (direct + hp_ref[:, 1:2] * dl) * logistic
    ddt_ref[...] = ddt
    hg_ref[0] += ddt
    hg_ref[1] += dt * dl
    hg_ref[2] += skip
    dmixb = dmix.astype(BF16)
    xtv, dyev = xt[...], dye[...]
    dbt = dot(ct, dmixb, (((1,), (1,)))) + dot(ds, xtv, (((0,), (0,))))
    dct = dot(bt, dmixb, (((1,), (0,)))) + dot(s_ref[...], dyev, (((0,), (0,))))
    dbca = jnp.concatenate([dbt, dct], axis=0)
    for r0 in range(0, 2 * STATE, HEAD):
        conv_back(chans + r0, dbca[r0 : r0 + HEAD, :], dbc_ref, r0)
    fresh = dot(dyev, ct, (((1,), (1,))))
    for h in range(heads):
        rows = slice(h * HEAD, (h + 1) * HEAD)
        dstate[rows, :] = dstate[rows, :] * passing[h : h + 1, :] + fresh[rows, :]

    @pl.when(pl.program_id(0) == pl.num_programs(0) - 1)
    def _():
        for r0 in range(0, wide, HEAD):
            rows = slice(r0, r0 + HEAD)
            for k in range(5):
                cgo_ref[rows, k : k + 1] = jnp.sum(cg_ref[k, rows, :], axis=1, keepdims=True)


def scan_backward(
    place, xr, bco, bcs, dtr, masks, segr, segc, par, hp, xa, u, s_in, dy, y, heads, seqs, seq, given=()
):
    chans, tokens = xr.shape
    padded = dtr.shape[0]
    wide = chans + 2 * STATE
    count = tokens // seqs // Q
    at = lambda k, p: (0, seq * count + count - 1 - k)
    swapped = lambda k, p: (0, (seqs - 1 - seq) * count + count - 1 - k)
    whole = lambda k, p: (0, 0)
    args = (xr, bco, bcs, dtr, masks, segr, segc, par, hp, xa, u, s_in, dy, y)
    return pl.pallas_call(
        functools.partial(bwd_kernel, heads, len(given)),
        out_shape=(
            jax.ShapeDtypeStruct((chans, tokens), BF16),
            jax.ShapeDtypeStruct((2 * STATE, tokens), F32),
            jax.ShapeDtypeStruct((padded, tokens), F32),
            jax.ShapeDtypeStruct((wide, 8), F32),
            jax.ShapeDtypeStruct((3, padded, Q), F32),
        ),
        grid_spec=pltpu.PrefetchScalarGridSpec(
            num_scalar_prefetch=1,
            grid=(count,),
            in_specs=[
                pl.BlockSpec((chans, Q), at),
                pl.BlockSpec((STATE, Q), at),
                pl.BlockSpec((STATE, Q), swapped),
                pl.BlockSpec((padded, Q), at),
                pl.BlockSpec((8, Q), at),
                pl.BlockSpec((1, Q), at),
                pl.BlockSpec((Q, 1), lambda k, p: (seq * count + count - 1 - k, 0)),
                pl.BlockSpec(par.shape, whole),
                pl.BlockSpec(hp.shape, whole),
                pl.BlockSpec((wide, Q), at),
                pl.BlockSpec((wide, Q), at),
                pl.BlockSpec((chans, STATE), at),
                pl.BlockSpec((chans, Q), at),
                pl.BlockSpec((chans, Q), at),
            ]
            + [pl.BlockSpec(memory_space=pl.ANY)] * len(given),
            out_specs=(
                pl.BlockSpec((chans, Q), at),
                pl.BlockSpec((2 * STATE, Q), at),
                pl.BlockSpec((padded, Q), at),
                pl.BlockSpec((wide, 8), whole),
                pl.BlockSpec((3, padded, Q), lambda k, p: (0, 0, 0)),
            ),
            scratch_shapes=[
                pltpu.VMEM((chans, STATE), F32),
                pltpu.VMEM((6, wide, Q), F32),
                pltpu.VMEM((wide, Q), F32),
                pltpu.VMEM((8, Q), F32),
                pltpu.VMEM((chans, Q), BF16),
                pltpu.VMEM((chans, Q), BF16),
                pltpu.VMEM((5, wide, Q), F32),
            ],
        ),
        input_output_aliases={1 + len(args) + k: k for k in range(len(given))},
        compiler_params=params(58),
        cost_estimate=BRIEF,
    )(place, *args, *given)


def block_masks(segs, seqs):
    s = segs.reshape(seqs, -1)
    length = s.shape[1]
    rows = []
    for k in (1, 2, 3):
        old = jnp.pad(s, ((0, 0), (k, 0)), constant_values=-1)[:, :length]
        rows.append(old == s)
    b = s.reshape(seqs, length // Q, Q)
    ends = b[:, :, -1:]
    before = jnp.concatenate([jnp.full((seqs, 1, 1), -1, s.dtype), ends[:, :-1]], axis=1)
    rows += [b == before, b == ends, jnp.broadcast_to(ends == before, b.shape)]
    rows = [r.reshape(1, -1).astype(F32) for r in rows]
    return jnp.concatenate(rows + [jnp.zeros((2, segs.shape[0]), F32)], axis=0)


def local(
    hidden, segment_ids, cotangent, w_zx, w_dt, w_bc, w_out, conv_x, conv_bias_x, conv_bc, conv_bias_bc,
    dt_bias, a_log, d_skip, pre_gain, gate_gain,
):
    n_dp, n_t = lax.axis_size("dp"), lax.axis_size("tensor")
    t_index = lax.axis_index("tensor")
    ring = Ring(n_dp)
    core = ring.core
    mine, width = hidden.shape
    inner_here = w_zx.shape[2]
    chans = inner_here // 2
    heads = w_dt.shape[1] // 2
    padded = max(16, heads)
    wide = chans + 2 * STATE
    inner_all = inner_here * n_t
    dd = 2 * w_zx.shape[1]

    def tensor_sum(v):
        if n_t == 2:
            return v + lax.ppermute(v, "tensor", [(0, 1), (1, 0)])
        return lax.psum(v, "tensor")

    def over_tensor(v):
        if n_t == 2:
            return v.astype(F32) + lax.ppermute(v, "tensor", [(0, 1), (1, 0)]).astype(F32)
        return lax.psum(v.astype(F32), "tensor")

    def pick(v, which, axis=0):
        size = v.shape[axis] // 2
        return lax.dynamic_slice_in_dim(v, which * size, size, axis)

    def in_order(own, other, axis):
        return jnp.where(
            core == 0, jnp.concatenate([own, other], axis), jnp.concatenate([other, own], axis)
        )

    pad_dt = lambda v: jnp.pad(v, ((0, 0), (0, STATE - heads)))
    small = jnp.concatenate([w_bc, pad_dt(w_dt[:, :heads]), pad_dt(w_dt[:, heads:])], axis=1)
    zx_other = ring.swap(w_zx)
    small_other = ring.swap(small)
    place = core.reshape(1).astype(jnp.int32)
    ux = prep_x(place, w_zx, zx_other, small, small_other, padded)
    cut = chans // 2
    gx = Gather(ring, ux, "both", cut)
    gx.step()

    hiddens = [hidden, ring.swap(after(hidden, ux))]

    def norm(h):
        h = h.astype(F32)
        return (h * lax.rsqrt(jnp.mean(h * h, -1, keepdims=True) + EPS) * pre_gain).astype(BF16)

    normed = [norm(h) for h in hiddens]
    segs = jnp.concatenate([segment_ids, ring.swap(after(segment_ids, ux))])
    masks = block_masks(segs, 2)
    segr, segc = segs[None, :], segs[:, None]
    offs = ring.offsets(dd)
    table = ring.table()

    def own_chans(v):
        return pick(v, core, v.ndim - 1)

    taps = jnp.concatenate([own_chans(conv_x), conv_bc], axis=1)
    biases = jnp.concatenate([own_chans(conv_bias_x), conv_bias_bc])
    skips = jnp.repeat(own_chans(d_skip), HEAD)
    par = jnp.concatenate(
        [taps, biases[None], jnp.pad(skips, (0, 2 * STATE))[None], jnp.zeros((2, wide), F32)], axis=0
    ).T
    a_own = -jnp.exp(own_chans(a_log))
    hp = jnp.stack([own_chans(dt_bias), a_own, own_chans(d_skip)], axis=1)
    hp = jnp.pad(hp, ((0, padded - heads), (0, 5)))
    gain = own_chans(gate_gain)[:, None]

    out_other = ring.swap(after(w_out, ux))
    uz, uo = prep_zo(place, w_zx, zx_other, w_out, out_other)
    cots = [cotangent, ring.swap(after(cotangent, uz))]

    gx.step()
    gx.step()
    third = gx.newest()
    gx.finish()
    gz = Gather(ring, after(uz, *third), "right")
    gz.step()

    blocks = gx.blocks()
    bc_own, dtr = two_projections(
        Weight(blocks, chans, STATE, cut), Weight(blocks, chans + STATE, padded, cut), normed, offs
    )
    bc_other = ring.swap(bc_own)
    xr = plain_projection(Weight(blocks, 0, chans, cut), normed, after(offs, bc_own))
    gz.r[-1], gz.l[-1] = after(gz.r[-1], xr), after(gz.l[-1], xr)
    go = Gather(ring, after(uo, *gz.newest()), "left")
    go.step()
    scan_args = (bc_own, bc_other, dtr, masks, segr, segc, par, hp)
    ahead = gz.newest()
    gz.step()
    half = scan_forward(place, after(xr, *ahead), *scan_args, heads, 2, 0)
    gz.r[-1], gz.l[-1] = after(gz.r[-1], half[0]), after(gz.l[-1], half[0])
    ahead = gz.newest()
    gz.step()
    y, xa, u, s_in = scan_forward(place, after(xr, *ahead), *scan_args, heads, 2, 1, half)
    gz.r[-1] = after(gz.r[-1], y)
    ahead = gz.newest()
    gz.finish()
    go.r[-1], go.l[-1] = after(go.r[-1], *ahead), after(go.l[-1], *ahead)
    go.step()
    go.step()
    z, squares = gate_projection(Weight(gz.blocks(), 0, chans), normed, after(offs, y, *gz.last), y)
    go.finish()

    def group_sum(v):
        return tensor_sum(v + ring.swap(jnp.concatenate([v[:, mine:], v[:, :mine]], axis=1)))

    total_sq = group_sum(squares)
    s = lax.rsqrt(total_sq / inner_all + EPS)
    ynt = (y * (z * sigmoid(z)) * s * gain).astype(BF16)
    ro = Scatter(ring, table, ynt, cots, dd, "right")

    weight_o = Weight(go.blocks(), 0, chans)
    dyn, q = back_projection(weight_o, cots, after(offs, *ro.out), y, z, gain)
    q_total = group_sum(q)
    out_own, out_rest = back([(weight_o, after(ynt, q))], offs, width)
    sent = ro.step(out_own)
    out_came = ring.swap(out_rest)
    dzt, dyt, dgain = gate_back(inner_all, after(dyn, *sent), y, z, s, q_total, gain)
    rz = Scatter(ring, table, dzt, normed, dd, "left")
    out_own = after(out_own.astype(F32) + out_came.astype(F32), *rz.out).astype(BF16)

    scan_args = (*scan_args, xa, u, s_in)
    first = scan_backward(
        place, xr, *scan_args, after(dyt, *rz.out, out_own), y, heads, 2, 0
    )
    sent_o = ro.step(first[3])
    sent_z = rz.step(*sent_o)
    second = scan_backward(
        place, xr, *scan_args, after(dyt, *sent_o, *sent_z), y, heads, 2, 1, first[:3]
    )
    dxt, dbc, ddt = second[:3]
    dbc_low = dbc.astype(BF16)
    dbc_came = ring.swap(dbc_low[:, mine:])
    rx = Scatter(ring, table, dxt, normed, dd, "both")
    sent_o = ro.step(*rx.out)
    sent_z = rz.step(*sent_o)

    quarter = 2 * STATE // (2 * n_t)
    dbc_own = after(dbc_low[:, :mine].astype(F32) + dbc_came.astype(F32), *sent_z).astype(BF16)
    dbc_own = over_tensor(dbc_own).astype(BF16)
    dn_z = back([(Weight(gz.blocks(), 0, chans), dzt)], after(offs, *sent_z), width)
    sent_x = rx.step(dn_z[0])
    dbc_all = jnp.concatenate([dbc_own, ring.swap(after(dbc_own, dn_z[0]))], axis=1)
    keep_o, give_o = ro.finish(*sent_x)
    sent_z = rz.step(keep_o)
    ddt_low = ddt.astype(BF16)
    bc_here = lax.dynamic_slice_in_dim(dbc_all, core * STATE + t_index * quarter, quarter, 0)
    bc_full = jnp.zeros((STATE, 2 * mine), BF16)
    bc_full = lax.dynamic_update_slice_in_dim(bc_full, bc_here, t_index * quarter, 0)
    dn_own, dn_rest, pre_part = back(
        [
            (Weight(blocks, 0, chans, cut), dxt),
            (Weight(blocks, chans, STATE, cut), bc_full),
            (Weight(blocks, chans + STATE, padded, cut), ddt_low),
        ],
        after(offs, *sent_z), width, dn_z, hiddens,
    )
    dn_came = ring.swap(dn_rest)
    sent_x = rx.step(dn_own)

    cg = (first[3] + second[3]).T[:5]
    hg = jnp.sum(first[4] + second[4], 2)[:, :heads]
    hg = hg * jnp.stack([jnp.ones_like(a_own), a_own, jnp.ones_like(a_own)])
    split = jnp.concatenate([cg[:, :chans].reshape(-1), dgain[:, 0], hg.reshape(-1)])
    shared = jnp.concatenate([cg[:, chans:].reshape(-1), pre_part[0]])
    n_split, n_shared = split.shape[0], shared.shape[0]
    lines = -(-(n_split + n_shared) // (16 * dd)) * 16
    common = jnp.concatenate([split, shared])
    common = jnp.pad(common, (0, lines * dd - common.shape[0])).reshape(lines, dd)
    bc_ours = lax.dynamic_slice_in_dim(dbc_all, (t_index * 2 + core) * quarter, quarter, 0)
    small_rows = after(jnp.concatenate([bc_ours, ddt_low], axis=0), *sent_x)
    letters = messages(ring, table, small_rows, normed, common)
    dn_own = after(dn_own.astype(F32) + dn_came.astype(F32), letters[0]).astype(BF16)
    if n_t == 2:
        dn_other = lax.ppermute(dn_own, "tensor", [(0, 1), (1, 0)])
    else:
        dn_other = (lax.psum(dn_own.astype(F32), "tensor") - dn_own.astype(F32)).astype(BF16)
    answers = [lax.ppermute(after(letters[k], dn_own), "dp", ring.ahead(k)) for k in range(1, ring.n)]
    keep_z, give_z = rz.finish(dn_own)
    sent_x = rx.step(keep_z)
    grad_out = in_order(keep_o, ring.swap(give_o), 0)
    output = (hidden.astype(F32) + over_tensor(out_own)).astype(BF16)
    sums = after(letters[0], *sent_x).astype(F32)
    for answer in answers:
        sums = sums + answer.astype(F32)
    sum_small, common = sums[: quarter + padded], sums[quarter + padded :].reshape(-1)
    split, shared = common[:n_split], common[n_split : n_split + n_shared]
    split_other = ring.swap(split)
    shared = tensor_sum(shared + ring.swap(shared))

    def parts(v):
        a = v[: 5 * chans].reshape(5, chans)
        b = v[5 * chans : 6 * chans]
        c = v[6 * chans :].reshape(3, heads)
        return a, b, c

    (a0, b0, c0), (a1, b1, c1) = parts(split), parts(split_other)
    cg_x = in_order(a0, a1, 1)
    grad_gate = in_order(b0, b1, 0)
    hg = in_order(c0, c1, 1)
    cg_bc = shared[: 5 * 2 * STATE].reshape(5, 2 * STATE)
    grad_pre = shared[5 * 2 * STATE :]

    grad_hidden = norm_back(dn_own, after(dn_other, *sent_x), hidden, cotangent, pre_gain[None])
    keep_x, give_x = rx.finish(grad_hidden)
    grad_zx = turn(place, keep_z, ring.swap(give_z), keep_x, ring.swap(give_x))
    ks = pick(sum_small, core, 1)
    os = ring.swap(pick(sum_small, 1 - core, 1))
    grad_bc = in_order(ks[:quarter], os[:quarter], 0).T
    grad_dt = in_order(ks[quarter : quarter + heads], os[quarter : quarter + heads], 0).T
    return (
        output, grad_hidden, grad_zx, grad_dt, grad_bc, grad_out, cg_x[:4], cg_x[4], cg_bc[:4], cg_bc[4],
        hg[0], hg[1], hg[2], grad_pre, grad_gate,
    )


def solution(mesh):
    in_specs = (
        P("dp", None), P("dp"), P("dp", None), P(None, "dp", "tensor"), P("dp", "tensor"), P("dp", None),
        P("tensor", "dp"), P(None, "tensor"), P("tensor"), P(), P(), P("tensor"), P("tensor"), P("tensor"),
        P(), P("tensor"),
    )
    out_specs = (
        P("dp", None), P("dp", None), P(None, "dp", "tensor"), P("dp", "tensor"), P("dp", "tensor"),
        P("tensor", "dp"), P(None, "tensor"), P("tensor"), P(), P(), P("tensor"), P("tensor"), P("tensor"),
        P(), P("tensor"),
    )
    return jax.shard_map(local, mesh=mesh, in_specs=in_specs, out_specs=out_specs, check_vma=False)
```

time: 538 us -> 476 us (0.88)
  Pallas kernels: 99.5 us -> 172 us
  waiting for transfers between devices: 190 us -> 133 us
  other arithmetic: 69.8 us -> 31.3 us
  matrix products: 36.1 us -> 0 us
  local copies, waits for them, and re-layouts: 50.2 us -> 60.9 us
  between operations: 14.5 us -> 4.25 us
    pallas_call x7 -> x32, Pallas kernels: 99.5 us -> 172 us  [the longest x15 48.3 us: call(): pl.pallas_call(kernel, out_shape=tuple((shape(k) for k in kinds)), grid_s...]
    ppermute x28 -> x22, waiting for transfers between devices: 107 us -> 60.2 us  [go_right(): return lax.ppermute(v, 'dp', self.right)]
    ppermute x3 -> x2, waiting for transfers between devices: 49.4 us -> 8.03 us  [over_tensor(): lax.ppermute(v, 'tensor', [(0, 1), (1, 0)]).astype(F32)]
    dot_general x32 -> x0, matrix products: 36.1 us -> none  [dot(): lax.dot_general(a, b, (dims, ((), ())), precision=precision, preferred_el...]
    unnamed x162 -> x200, local copies, waits for them, and re-layouts: 10.8 us -> 42.2 us
    ppermute x3 -> x8, waiting for transfers between devices: 3.81 us -> 20 us  [the longest x1 20 us: local(): dn_other = lax.ppermute(dn_own, 'tensor', [(0, 1), (1, 0)])]
    concatenate x14 -> x6, other arithmetic: 18 us -> 3.16 us  [the longest x1 1.93 us: local(): jnp.concatenate([dbc_own, ring.swap(after(dbc_own, dn_z[0]))], axis=1)]
    ppermute x28 -> x22, starting transfers between devices: 24 us -> 11.5 us  [go_left(): return lax.ppermute(v, 'dp', self.left)]
  transfers between devices with their start and end apart: 84 -> 76, of which waited for: 33 -> 24; matrix products, arithmetic and copies ran while one was open for 22% -> 11% of each run, Pallas kernels for 14% -> 30%
where the time goes in v2:
time: 476 us; the launch traced here: 468 us
  Pallas kernels  172 us (36%)
  waiting for transfers between devices  133 us (28%)
  starting transfers between devices  66.1 us (14%)
  local copies, waits for them, and re-layouts  60.9 us (13%)
  other arithmetic  31.3 us (7%)
    ppermute x22, waiting for transfers between devices, go_right(): return lax.ppermute(v, 'dp', self.right)  60.2 us
    pallas_call x15, Pallas kernels, call(): pl.pallas_call(kernel, out_shape=tuple((shape(k) for k in kinds)), grid_s...  48.3 us
    unnamed x200, local copies, waits for them, and re-layouts  42.2 us
    ppermute x22, waiting for transfers between devices, go_left(): return lax.ppermute(v, 'dp', self.left)  39.7 us
    ppermute x22, starting transfers between devices, go_right(): return lax.ppermute(v, 'dp', self.right)  35.4 us
    pallas_call x2, Pallas kernels, scan_backward(): pl.pallas_call(functools.partial(bwd_kernel, heads, len(given)), out_shap...  29.9 us
    pallas_call x3, Pallas kernels, back(): pl.pallas_call(kernel, out_shape=tuple(shapes), grid_spec=pltpu.PrefetchS...  28.2 us
    pallas_call x3, Pallas kernels, projection(): pl.pallas_call(kernel, out_shape=out_shape, grid_spec=pltpu.PrefetchScala...  26.6 us
  transfers between devices with their start and end apart: 76, of which 24 were waited for; matrix products, arithmetic and copies ran while one was open for 11% of the time, Pallas kernels for 30%

profile of v2, /device:TPU:0, one launch (start us, length us, event | category | flops | bytes accessed | tf_op | source)
XLA Modules:
  0.0 467.5 jit_solution(11468107615648596389)
XLA Ops:
  8.5 2.8 collective-permute-start.3
  12.0 13.1 %collective-permute-done.3.refs_1_.refs_9_.refs_11_.refs_20_ = bf16[1168,256]{1,0:T(8,128)(2,1)S(1)} collective-permute-done((bf16[1168,256]{1,0:T(8,128)(2,1)S(1)}, bf16[1168,256]{1,0:T(8,128)(2,1)S(1)}, u32[]{:S(2)}, u32[]{:S(2)}) %collective-permute-start.3) | collective-permute-done | bytes 598048 | tf_op jit(solution)/shard_map/ppermute | solution.py:76
  28.4 11.9 %collective-permute-done.4.refs_2_.refs_10_.refs_12_.refs_21_ = bf16[1168,256]{1,0:T(8,128)(2,1)} collective-permute-done((bf16[1168,256]{1,0:T(8,128)(2,1)S(1)}, bf16[1168,256]{1,0:T(8,128)(2,1)}, u32[]{:S(2)}, u32[]{:S(2)}) %collective-permute-start.4) | collective-permute-done | bytes 598048 | tf_op jit(solution)/shard_map/ppermute | solution.py:76
  52.6 2.4 shard_map.299
  63.7 2.7 fusion.2
  66.4 10.9 %collective-permute-done.10.refs_7_.refs_15_.refs_8_.refs_17_.refs_26_ = bf16[656,256]{1,0:T(8,128)(2,1)S(1)} collective-permute-done((bf16[656,256]{1,0:T(8,128)(2,1)S(1)}, bf16[656,256]{1,0:T(8,128)(2,1)S(1)}, u32[]{:S(2)}, u32[]{:S(2)}) %collective-permute-start.10) | collective-permute-done | bytes 335904 | tf_op jit(solution)/shard_map/ppermute | solution.py:79
  77.3 3.8 shard_map.300
  81.2 7.2 %shard_map.301.xr_ref = f32[1024,1024]{1,0:T(8,128)S(1)} custom-call(s32[8]{0:T(128)S(1)} %fusion.22.offs, bf16[1168,256]{1,0:T(8,128)(2,1)S(1)} %shard_map.298.refs_0_.refs_8_.refs_10_.refs_19_, bf16[1168,256]{1,0:T(8,128)(2,1)S(1)} %copy-done.35, bf16[1168,256]{1,0:T(8,128)(2,1)} %collective-permute-done.4.refs_2_.refs_10_.refs_12_.refs_21_, ...), custom_call_target="tpu_custom_call" | custom-call | flops 1 | bytes 1 | tf_op jit(solution)/shard_map/pallas_call | solution.py:369
  95.0 9.7 %shard_map.302 = (f32[1024,1024]{1,0:T(8,128)}, bf16[1280,1024]{1,0:T(8,128)(2,1)}, f32[1280,1024]{1,0:T(8,128)}, bf16[1024,1024]{1,0:T(8,128)(2,1)}) custom-call(s32[1]{0:T(128)} %bitcast.2.place, f32[1024,1024]{1,0:T(8,128)} %copy-done.12, f32[128,1024]{1,0:T(8,128)} %get-tuple-element.140.bco_ref, f32[128,1024]{1,0:T(8,128)} %collective-permute-done.16.bcs_ref, ...), custom_call_target="tpu_custom_call" | custom-call | flops 1 | bytes 1 | tf_op jit(solution)/shard_map/pallas_call | solution.py:753
  109.1 9.8 %shard_map.303 = (f32[1024,1024]{1,0:T(8,128)}, bf16[1280,1024]{1,0:T(8,128)(2,1)}, f32[1280,1024]{1,0:T(8,128)}, bf16[1024,1024]{1,0:T(8,128)(2,1)}) custom-call(s32[1]{0:T(128)} %bitcast.2.place, f32[1024,1024]{1,0:T(8,128)} %copy-done.12, ...), custom_call_target="tpu_custom_call", output_to_operand_aliasing={{0}: (10, {}), {1}: (11, {}), {2}: (12, {}), {3}: (13, {})} | custom-call | flops 1 | bytes 1 | tf_op jit(solution)/shard_map/pallas_call | solution.py:753
  121.8 9.7 %collective-permute-done.20.refs_6_ = bf16[1024,256]{1,0:T(8,128)(2,1)} collective-permute-done((bf16[1024,256]{1,0:T(8,128)(2,1)}, bf16[1024,256]{1,0:T(8,128)(2,1)}, u32[]{:S(2)}, u32[]{:S(2)}) %collective-permute-start.20) | collective-permute-done | bytes 524320 | tf_op jit(solution)/shard_map/ppermute | solution.py:79
  133.5 9.0 %collective-permute-done.27.refs_7_ = bf16[1024,256]{1,0:T(8,128)(2,1)S(1)} collective-permute-done((bf16[1024,256]{1,0:T(8,128)(2,1)}, bf16[1024,256]{1,0:T(8,128)(2,1)S(1)}, u32[]{:S(2)}, u32[]{:S(2)}) %collective-permute-start.27) | collective-permute-done | bytes 524320 | tf_op jit(solution)/shard_map/ppermute | solution.py:76
  144.6 8.8 %shard_map.304 = (f32[1024,1024]{1,0:T(8,128)S(1)}, f32[1,1024]{1,0:T(1,128)S(1)}) custom-call(s32[8]{0:T(128)S(1)} %fusion.22.offs, bf16[1024,256]{1,0:T(8,128)(2,1)S(1)} %copy-done.51, bf16[1024,256]{1,0:T(8,128)(2,1)} %collective-permute-done.9.refs_1_, bf16[1024,256]{1,0:T(8,128)(2,1)} %collective-permute-done.15.refs_2_, ...), custom_call_target="tpu_custom_call" | custom-call | flops 1 | bytes 1 | tf_op jit(solution)/shard_map/pallas_call | solution.py:369
  161.7 4.2 multiply_convert_fusion.vt.refs_8_
  165.9 2.8 shard_map.305
  168.8 4.3 collective-permute-done.22.refs_3_
  174.8 10.7 %shard_map.306 = (f32[1024,1024]{1,0:T(8,128)S(1)}, f32[1,1024]{1,0:T(1,128)S(1)}) custom-call(s32[8]{0:T(128)S(1)} %fusion.22.offs, bf16[1024,256]{1,0:T(8,128)(2,1)} %get-tuple-element.144.refs_0_, bf16[1024,256]{1,0:T(8,128)(2,1)} %collective-permute-done.14.refs_1_, bf16[1024,256]{1,0:T(8,128)(2,1)} %collective-permute-done.21.refs_2_, ...), custom_call_target="tpu_custom_call" | custom-call | flops 1 | bytes 1 | tf_op jit(solution)/shard_map/pallas_call | solution.py:369
  187.5 7.3 %shard_map.307 = (bf16[512,2048]{1,0:T(8,128)(2,1)S(1)}, bf16[512,2048]{1,0:T(8,128)(2,1)S(1)}) custom-call(s32[8]{0:T(128)S(1)} %fusion.22.offs, bf16[1024,256]{1,0:T(8,128)(2,1)} %get-tuple-element.144.refs_0_, bf16[1024,256]{1,0:T(8,128)(2,1)} %collective-permute-done.14.refs_1_, bf16[1024,256]{1,0:T(8,128)(2,1)} %collective-permute-done.21.refs_2_, ...), custom_call_target="tpu_custom_call" | custom-call | flops 1 | bytes 1 | tf_op jit(solution)/shard_map/pallas_call | solution.py:522
  196.8 2.3 collective-permute-done.33
  199.6 9.6 %collective-permute-done.32.refs_4_ = bf16[1024,256]{1,0:T(8,128)(2,1)S(1)} collective-permute-done((bf16[1024,256]{1,0:T(8,128)(2,1)S(1)}, bf16[1024,256]{1,0:T(8,128)(2,1)S(1)}, u32[]{:S(2)}, u32[]{:S(2)}) %collective-permute-start.32) | collective-permute-done | bytes 524320 | tf_op jit(solution)/shard_map/ppermute | solution.py:76
  209.2 4.2 shard_map.308
  217.7 3.4 shard_map.309
  227.1 15.0 %shard_map.311 = (bf16[1024,1024]{1,0:T(8,128)(2,1)}, f32[256,1024]{1,0:T(8,128)}, f32[16,1024]{1,0:T(8,128)}, f32[1280,8]{1,0:T(8,128)}, f32[3,16,128]{2,1,0:T(8,128)}) custom-call(s32[1]{0:T(128)} %bitcast.2.place, f32[1024,1024]{1,0:T(8,128)} %copy-done.12, f32[128,1024]{1,0:T(8,128)} %get-tuple-element.140.bco_ref, ...), custom_call_target="tpu_custom_call" | custom-call | flops 1 | bytes 1 | tf_op jit(solution)/shard_map/pallas_call | solution.py:927
  243.6 4.3 shard_map.312
  249.9 3.8 shard_map.313
  255.8 15.0 %shard_map.314 = (bf16[1024,1024]{1,0:T(8,128)(2,1)}, f32[256,1024]{1,0:T(8,128)}, f32[16,1024]{1,0:T(8,128)}, f32[1280,8]{1,0:T(8,128)}, f32[3,16,128]{2,1,0:T(8,128)}) custom-call(s32[1]{0:T(128)} %bitcast.2.place, f32[1024,1024]{1,0:T(8,128)} %copy-done.12, ...), custom_call_target="tpu_custom_call", output_to_operand_aliasing={{0}: (15, {}), {1}: (16, {}), {2}: (17, {})} | custom-call | flops 1 | bytes 1 | tf_op jit(solution)/shard_map/pallas_call | solution.py:927
  276.0 4.2 shard_map.316
  280.3 3.9 shard_map.317
  289.5 2.8 collective-permute-done.50
  292.9 7.3 %shard_map.318 = (bf16[512,2048]{1,0:T(8,128)(2,1)S(1)}, bf16[512,2048]{1,0:T(8,128)(2,1)S(1)}) custom-call(s32[8]{0:T(128)S(1)} %fusion.22.offs, bf16[1024,256]{1,0:T(8,128)(2,1)S(1)} %copy-done.52, bf16[1024,256]{1,0:T(8,128)(2,1)} %collective-permute-done.9.refs_1_, bf16[1024,256]{1,0:T(8,128)(2,1)} %collective-permute-done.15.refs_2_, ...), custom_call_target="tpu_custom_call" | custom-call | flops 1 | bytes 1 | tf_op jit(solution)/shard_map/pallas_call | solution.py:522
  303.6 12.8 %collective-permute-done.44.refs_5_ = bf16[512,256]{1,0:T(8,128)(2,1)S(1)} collective-permute-done((bf16[512,256]{1,0:T(8,128)(2,1)S(1)}, bf16[512,256]{1,0:T(8,128)(2,1)S(1)}, u32[]{:S(2)}, u32[]{:S(2)}) %collective-permute-start.44) | collective-permute-done | bytes 262176 | tf_op jit(solution)/shard_map/ppermute | solution.py:79
  326.1 3.0 shard_map.320
  330.0 3.6 shard_map.321
  335.6 13.6 %shard_map.322 = (bf16[512,2048]{1,0:T(8,128)(2,1)S(1)}, bf16[512,2048]{1,0:T(8,128)(2,1)}, f32[1,2048]{1,0:T(1,128)S(1)}) custom-call(s32[8]{0:T(128)S(1)} %fusion.22.offs, bf16[1168,256]{1,0:T(8,128)(2,1)S(1)} %shard_map.298.refs_0_.refs_8_.refs_10_.refs_19_, bf16[1168,256]{1,0:T(8,128)(2,1)S(1)} %copy-done.36, ...), custom_call_target="tpu_custom_call" | custom-call | flops 1 | bytes 1 | tf_op jit(solution)/shard_map/pallas_call | solution.py:522
  361.2 7.7 %collective-permute-done.53.refs_4_ = bf16[1024,256]{1,0:T(8,128)(2,1)S(1)} collective-permute-done((bf16[1024,256]{1,0:T(8,128)(2,1)}, bf16[1024,256]{1,0:T(8,128)(2,1)S(1)}, u32[]{:S(2)}, u32[]{:S(2)}) %collective-permute-start.53) | collective-permute-done | bytes 524320 | tf_op jit(solution)/shard_map/ppermute | solution.py:76
  372.8 2.9 shard_map.323
  381.8 3.8 convert_add_fusion.1.own
  385.6 2.3 collective-permute-start.70
  387.9 2.9 collective-permute-done.58.refs_4_
  394.6 5.2 %collective-permute-done.35 = bf16[512,2048]{1,0:T(8,128)(2,1)} collective-permute-done((bf16[512,2048]{1,0:T(8,128)(2,1)}, bf16[512,2048]{1,0:T(8,128)(2,1)}, u32[]{:S(2)}, u32[]{:S(2)}) %collective-permute-start.35) | collective-permute-done | bytes 2097184 | tf_op jit(solution)/shard_map/ppermute | solution.py:1018
  399.9 2.3 collective-permute-start.67
  403.3 2.6 collective-permute-start.64
  405.9 4.6 fusion.6
  410.5 3.3 shard_map.325
  413.8 3.0 shard_map.326
  423.9 20.0 %collective-permute-done.55.came = bf16[512,2048]{1,0:T(8,128)(2,1)} collective-permute-done((bf16[512,2048]{1,0:T(8,128)(2,1)}, bf16[512,2048]{1,0:T(8,128)(2,1)}, u32[]{:S(2)}, u32[]{:S(2)}) %collective-permute-start.55) | collective-permute-done | bytes 2097184 | tf_op jit(solution)/shard_map/ppermute | solution.py:1175
  447.0 6.1 %shard_map.327 = bf16[512,2048]{1,0:T(8,128)(2,1)} custom-call(bf16[512,2048]{1,0:T(8,128)(2,1)} %convert_add_fusion.1.own, bf16[512,2048]{1,0:T(8,128)(2,1)} %collective-permute-done.55.came, bf16[512,2048]{1,0:T(8,128)(2,1)S(1)} %copy-done.31, bf16[512,2048]{1,0:T(8,128)(2,1)} %cot.1, f32[1,2048]{1,0:T(1,128)S(1)} %bitcast.58), custom_call_target="tpu_custom_call" | custom-call | flops 1 | bytes 1 | tf_op jit(solution)/shard_map/pallas_call | solution.py:581
  453.1 3.2 shard_map.328
  (453 shorter events, 153.3 us)
Async XLA Ops:
  8.3 53.3 %collective-permute-start.11 = (bf16[512,2048]{1,0:T(8,128)(2,1)S(1)}, bf16[512,2048]{1,0:T(8,128)(2,1)}, u32[]{:S(2)}, u32[]{:S(2)}) collective-permute-start(bf16[512,2048]{1,0:T(8,128)(2,1)S(1)} %copy-done.28), channel_id=1, source_target_pairs={{0,2},{2,0},{4,6},{6,4},{8,10},{10,8},{12,14},{14,12},{16,18},{18,... | collective-permute-start | bytes 6291464 | tf_op jit(solution)/shard_map/ppermute | solution.py:82
  8.5 16.6 %collective-permute-start.3 = (bf16[1168,256]{1,0:T(8,128)(2,1)S(1)}, bf16[1168,256]{1,0:T(8,128)(2,1)S(1)}, u32[]{:S(2)}, u32[]{:S(2)}) collective-permute-start(bf16[1168,256]{1,0:T(8,128)(2,1)S(1)} %shard_map.298.refs_0_.refs_8_.refs_10_.refs_19_), channel_id=1, source_target_pairs={{0,8},{2,10},{8,16},{10,18},{16,24},{18,26},{24,28},{26,30},{28,20... | collective-permute-start | bytes 1794056 | tf_op jit(solution)/shard_map/ppermute | solution.py:76
  11.3 16.4 %collective-permute-start.6 = (bf16[1168,256]{1,0:T(8,128)(2,1)S(1)}, bf16[1168,256]{1,0:T(8,128)(2,1)}, u32[]{:S(2)}, u32[]{:S(2)}) collective-permute-start(bf16[1168,256]{1,0:T(8,128)(2,1)S(1)} %shard_map.298.refs_0_.refs_8_.refs_10_.refs_19_), channel_id=1, source_target_pairs={{0,4},{2,6},{8,0},{10,2},{16,8},{18,10},{24,16},{26,18},{28,24},{3... | collective-permute-start | bytes 1794056 | tf_op jit(solution)/shard_map/ppermute | solution.py:79
  25.1 15.3 %collective-permute-start.4 = (bf16[1168,256]{1,0:T(8,128)(2,1)S(1)}, bf16[1168,256]{1,0:T(8,128)(2,1)}, u32[]{:S(2)}, u32[]{:S(2)}) collective-permute-start(bf16[1168,256]{1,0:T(8,128)(2,1)S(1)} %collective-permute-done.3.refs_1_.refs_9_.refs_11_.refs_20_), channel_id=1, source_target_pairs={{0,8},{2,10},{8,16},{10,18},{16,24},{18,26},{24,28},{26,30},{28,20... | collective-permute-start | bytes 1794056 | tf_op jit(solution)/shard_map/ppermute | solution.py:76
  56.4 33.9 %collective-permute-start.9 = (bf16[1024,256]{1,0:T(8,128)(2,1)S(1)}, bf16[1024,256]{1,0:T(8,128)(2,1)}, u32[]{:S(2)}, u32[]{:S(2)}) collective-permute-start(bf16[1024,256]{1,0:T(8,128)(2,1)S(1)} %get-tuple-element.138.refs_0_), channel_id=1, source_target_pairs={{0,8},{2,10},{8,16},{10,18},{16,24},{18,26},{24,28},{26,30},{28,20... | collective-permute-start | bytes 1572872 | tf_op jit(solution)/shard_map/ppermute | solution.py:76
  58.0 32.3 %collective-permute-start.13 = (bf16[1024,256]{1,0:T(8,128)(2,1)S(1)}, bf16[1024,256]{1,0:T(8,128)(2,1)}, u32[]{:S(2)}, u32[]{:S(2)}) collective-permute-start(bf16[1024,256]{1,0:T(8,128)(2,1)S(1)} %get-tuple-element.138.refs_0_), channel_id=1, source_target_pairs={{0,4},{2,6},{8,0},{10,2},{16,8},{18,10},{24,16},{26,18},{28,24},{3... | collective-permute-start | bytes 1572872 | tf_op jit(solution)/shard_map/ppermute | solution.py:79
  58.5 18.8 %collective-permute-start.10 = (bf16[656,256]{1,0:T(8,128)(2,1)S(1)}, bf16[656,256]{1,0:T(8,128)(2,1)S(1)}, u32[]{:S(2)}, u32[]{:S(2)}) collective-permute-start(bf16[656,256]{1,0:T(8,128)(2,1)S(1)} %slice.204), channel_id=1, source_target_pairs={{0,4},{2,6},{8,0},{10,2},{16,8},{18,10},{24,16},{26,18},{28,24},{3... | collective-permute-start | bytes 1007624 | tf_op jit(solution)/shard_map/ppermute | solution.py:79
  60.4 20.8 %collective-permute-start.12 = (bf16[512,256]{1,0:T(8,128)(2,1)S(1)}, bf16[512,256]{1,0:T(8,128)(2,1)S(1)}, u32[]{:S(2)}, u32[]{:S(2)}) collective-permute-start(bf16[512,256]{1,0:T(8,128)(2,1)S(1)} %slice.205), channel_id=1, source_target_pairs={{0,8},{2,10},{8,16},{10,18},{16,24},{18,26},{24,28},{26,30},{28,20... | collective-permute-start | bytes 786440 | tf_op jit(solution)/shard_map/ppermute | solution.py:76
  92.0 15.1 %collective-permute-start.19 = (bf16[1024,256]{1,0:T(8,128)(2,1)}, bf16[1024,256]{1,0:T(8,128)(2,1)}, u32[]{:S(2)}, u32[]{:S(2)}) collective-permute-start(bf16[1024,256]{1,0:T(8,128)(2,1)} %collective-permute-done.13.refs_4_), channel_id=1, source_target_pairs={{0,4},{2,6},{8,0},{10,2},{16,8},{18,10},{24,16},{26,18},{28,24},{3... | collective-permute-start | bytes 1572872 | tf_op jit(solution)/shard_map/ppermute | solution.py:79
  105.0 15.1 %collective-permute-start.18 = (bf16[1024,256]{1,0:T(8,128)(2,1)}, bf16[1024,256]{1,0:T(8,128)(2,1)}, u32[]{:S(2)}, u32[]{:S(2)}) collective-permute-start(bf16[1024,256]{1,0:T(8,128)(2,1)} %collective-permute-done.15.refs_2_), channel_id=1, source_target_pairs={{0,8},{2,10},{8,16},{10,18},{16,24},{18,26},{24,28},{26,30},{28,20... | collective-permute-start | bytes 1572872 | tf_op jit(solution)/shard_map/ppermute | solution.py:76
  106.6 15.2 %collective-permute-start.23 = (bf16[1024,256]{1,0:T(8,128)(2,1)}, bf16[1024,256]{1,0:T(8,128)(2,1)}, u32[]{:S(2)}, u32[]{:S(2)}) collective-permute-start(bf16[1024,256]{1,0:T(8,128)(2,1)} %get-tuple-element.144.refs_0_), channel_id=1, source_target_pairs={{0,4},{2,6},{8,0},{10,2},{16,8},{18,10},{24,16},{26,18},{28,24},{3... | collective-permute-start | bytes 1572872 | tf_op jit(solution)/shard_map/ppermute | solution.py:79
  107.0 24.4 %collective-permute-start.20 = (bf16[1024,256]{1,0:T(8,128)(2,1)}, bf16[1024,256]{1,0:T(8,128)(2,1)}, u32[]{:S(2)}, u32[]{:S(2)}) collective-permute-start(bf16[1024,256]{1,0:T(8,128)(2,1)} %collective-permute-done.19.refs_5_), channel_id=1, source_target_pairs={{0,4},{2,6},{8,0},{10,2},{16,8},{18,10},{24,16},{26,18},{28,24},{3... | collective-permute-start | bytes 1572872 | tf_op jit(solution)/shard_map/ppermute | solution.py:79
  107.6 58.3 %collective-permute-start.30 = (bf16[512,2048]{1,0:T(8,128)(2,1)}, bf16[512,2048]{1,0:T(8,128)(2,1)}, u32[]{:S(2)}, u32[]{:S(2)}) collective-permute-start(bf16[512,2048]{1,0:T(8,128)(2,1)} %cot.1), channel_id=1, source_target_pairs={{0,2},{2,0},{4,6},{6,4},{8,10},{10,8},{12,14},{14,12},{16,18},{18,... | collective-permute-start | bytes 6291464 | tf_op jit(solution)/shard_map/ppermute | solution.py:82
  107.6 24.3 %collective-permute-start.14 = (bf16[1024,256]{1,0:T(8,128)(2,1)}, bf16[1024,256]{1,0:T(8,128)(2,1)}, u32[]{:S(2)}, u32[]{:S(2)}) collective-permute-start(bf16[1024,256]{1,0:T(8,128)(2,1)} %get-tuple-element.144.refs_0_), channel_id=1, source_target_pairs={{0,8},{2,10},{8,16},{10,18},{16,24},{18,26},{24,28},{26,30},{28,20... | collective-permute-start | bytes 1572872 | tf_op jit(solution)/shard_map/ppermute | solution.py:76
  120.1 22.4 %collective-permute-start.27 = (bf16[1024,256]{1,0:T(8,128)(2,1)}, bf16[1024,256]{1,0:T(8,128)(2,1)S(1)}, u32[]{:S(2)}, u32[]{:S(2)}) collective-permute-start(bf16[1024,256]{1,0:T(8,128)(2,1)} %collective-permute-done.18.refs_3_), channel_id=1, source_target_pairs={{0,8},{2,10},{8,16},{10,18},{16,24},{18,26},{24,28},{26,30},{28,20... | collective-permute-start | bytes 1572872 | tf_op jit(solution)/shard_map/ppermute | solution.py:76
  131.9 27.3 %collective-permute-start.21 = (bf16[1024,256]{1,0:T(8,128)(2,1)}, bf16[1024,256]{1,0:T(8,128)(2,1)}, u32[]{:S(2)}, u32[]{:S(2)}) collective-permute-start(bf16[1024,256]{1,0:T(8,128)(2,1)} %collective-permute-done.14.refs_1_), channel_id=1, source_target_pairs={{0,8},{2,10},{8,16},{10,18},{16,24},{18,26},{24,28},{26,30},{28,20... | collective-permute-start | bytes 1572872 | tf_op jit(solution)/shard_map/ppermute | solution.py:76
  144.1 16.6 %collective-permute-start.25 = (bf16[1024,256]{1,0:T(8,128)(2,1)}, bf16[1024,256]{1,0:T(8,128)(2,1)}, u32[]{:S(2)}, u32[]{:S(2)}) collective-permute-start(bf16[1024,256]{1,0:T(8,128)(2,1)} %collective-permute-done.24.refs_5_), channel_id=1, source_target_pairs={{0,4},{2,6},{8,0},{10,2},{16,8},{18,10},{24,16},{26,18},{28,24},{3... | collective-permute-start | bytes 1572872 | tf_op jit(solution)/shard_map/ppermute | solution.py:79
  194.8 30.0 %collective-permute-start.31 = (bf16[512,2048]{1,0:T(8,128)(2,1)S(1)}, bf16[512,2048]{1,0:T(8,128)(2,1)S(1)}, u32[]{:S(2)}, u32[]{:S(2)}) collective-permute-start(bf16[512,2048]{1,0:T(8,128)(2,1)S(1)} %get-tuple-element.167), channel_id=1, source_target_pairs={{0,2},{2,0},{4,6},{6,4},{8,10},{10,8},{12,14},{14,12},{16,18},{18,... | collective-permute-start | bytes 6291464 | tf_op jit(solution)/shard_map/ppermute | solution.py:82
  199.0 16.4 %collective-permute-start.34 = (f32[1,1024]{1,0:T(1,128)S(1)}, f32[1,1024]{1,0:T(1,128)S(1)}, u32[]{:S(2)}, u32[]{:S(2)}) collective-permute-start(f32[1,1024]{1,0:T(1,128)S(1)} %add.164), channel_id=1, source_target_pairs={{0,1},{1,0},{2,3},{3,2},{4,5},{5,4},{6,7},{7,6},{8,9},{9,8},{10,11... | collective-permute-start | bytes 12296 | tf_op jit(solution)/shard_map/ppermute | solution.py:1013
  213.5 28.6 %collective-permute-start.36 = (bf16[1024,256]{1,0:T(8,128)(2,1)}, bf16[1024,256]{1,0:T(8,128)(2,1)}, u32[]{:S(2)}, u32[]{:S(2)}) collective-permute-start(bf16[1024,256]{1,0:T(8,128)(2,1)} %get-tuple-element.170), channel_id=1, source_target_pairs={{0,8},{2,10},{8,16},{10,18},{16,24},{18,26},{24,28},{26,30},{28,20... | collective-permute-start | bytes 1572872 | tf_op jit(solution)/shard_map/ppermute | solution.py:76
  215.0 27.0 %collective-permute-start.37 = (bf16[1024,256]{1,0:T(8,128)(2,1)S(1)}, bf16[1024,256]{1,0:T(8,128)(2,1)}, u32[]{:S(2)}, u32[]{:S(2)}) collective-permute-start(bf16[1024,256]{1,0:T(8,128)(2,1)S(1)} %get-tuple-element.171), channel_id=1, source_target_pairs={{0,4},{2,6},{8,0},{10,2},{16,8},{18,10},{24,16},{26,18},{28,24},{3... | collective-permute-start | bytes 1572872 | tf_op jit(solution)/shard_map/ppermute | solution.py:79
  224.2 25.7 %collective-permute-start.38 = (bf16[1024,256]{1,0:T(8,128)(2,1)}, bf16[1024,256]{1,0:T(8,128)(2,1)}, u32[]{:S(2)}, u32[]{:S(2)}) collective-permute-start(bf16[1024,256]{1,0:T(8,128)(2,1)} %shard_map.310), channel_id=1, source_target_pairs={{0,4},{2,6},{8,0},{10,2},{16,8},{18,10},{24,16},{26,18},{28,24},{3... | collective-permute-start | bytes 1572872 | tf_op jit(solution)/shard_map/ppermute | solution.py:79
  247.9 28.1 %collective-permute-start.39 = (bf16[1024,256]{1,0:T(8,128)(2,1)}, bf16[1024,256]{1,0:T(8,128)(2,1)S(1)}, u32[]{:S(2)}, u32[]{:S(2)}) collective-permute-start(bf16[1024,256]{1,0:T(8,128)(2,1)} %get-tuple-element.182), channel_id=1, source_target_pairs={{0,8},{2,10},{8,16},{10,18},{16,24},{18,26},{24,28},{26,30},{28,20... | collective-permute-start | bytes 1572872 | tf_op jit(solution)/shard_map/ppermute | solution.py:76
  249.5 26.5 %collective-permute-start.40 = (bf16[1024,256]{1,0:T(8,128)(2,1)}, bf16[1024,256]{1,0:T(8,128)(2,1)}, u32[]{:S(2)}, u32[]{:S(2)}) collective-permute-start(bf16[1024,256]{1,0:T(8,128)(2,1)} %get-tuple-element.183), channel_id=1, source_target_pairs={{0,4},{2,6},{8,0},{10,2},{16,8},{18,10},{24,16},{26,18},{28,24},{3... | collective-permute-start | bytes 1572872 | tf_op jit(solution)/shard_map/ppermute | solution.py:79
  253.7 26.5 %collective-permute-start.41 = (bf16[1024,256]{1,0:T(8,128)(2,1)}, bf16[1024,256]{1,0:T(8,128)(2,1)}, u32[]{:S(2)}, u32[]{:S(2)}) collective-permute-start(bf16[1024,256]{1,0:T(8,128)(2,1)} %get-tuple-element.185), channel_id=1, source_target_pairs={{0,8},{2,10},{8,16},{10,18},{16,24},{18,26},{24,28},{26,30},{28,20... | collective-permute-start | bytes 1572872 | tf_op jit(solution)/shard_map/ppermute | solution.py:76
  255.3 25.0 %collective-permute-start.42 = (bf16[1024,256]{1,0:T(8,128)(2,1)}, bf16[1024,256]{1,0:T(8,128)(2,1)}, u32[]{:S(2)}, u32[]{:S(2)}) collective-permute-start(bf16[1024,256]{1,0:T(8,128)(2,1)} %get-tuple-element.186), channel_id=1, source_target_pairs={{0,4},{2,6},{8,0},{10,2},{16,8},{18,10},{24,16},{26,18},{28,24},{3... | collective-permute-start | bytes 1572872 | tf_op jit(solution)/shard_map/ppermute | solution.py:79
  284.7 41.4 %collective-permute-start.45 = (bf16[1024,256]{1,0:T(8,128)(2,1)}, bf16[1024,256]{1,0:T(8,128)(2,1)}, u32[]{:S(2)}, u32[]{:S(2)}) collective-permute-start(bf16[1024,256]{1,0:T(8,128)(2,1)} %get-tuple-element.195), channel_id=1, source_target_pairs={{0,8},{2,10},{8,16},{10,18},{16,24},{18,26},{24,28},{26,30},{28,20... | collective-permute-start | bytes 1572872 | tf_op jit(solution)/shard_map/ppermute | solution.py:76
  286.3 39.9 %collective-permute-start.46 = (bf16[1024,256]{1,0:T(8,128)(2,1)}, bf16[1024,256]{1,0:T(8,128)(2,1)}, u32[]{:S(2)}, u32[]{:S(2)}) collective-permute-start(bf16[1024,256]{1,0:T(8,128)(2,1)} %get-tuple-element.196), channel_id=1, source_target_pairs={{0,4},{2,6},{8,0},{10,2},{16,8},{18,10},{24,16},{26,18},{28,24},{3... | collective-permute-start | bytes 1572872 | tf_op jit(solution)/shard_map/ppermute | solution.py:79
  286.7 43.2 %collective-permute-start.47 = (bf16[1024,256]{1,0:T(8,128)(2,1)}, bf16[1024,256]{1,0:T(8,128)(2,1)}, u32[]{:S(2)}, u32[]{:S(2)}) collective-permute-start(bf16[1024,256]{1,0:T(8,128)(2,1)} %get-tuple-element.198), channel_id=1, source_target_pairs={{0,8},{2,10},{8,16},{10,18},{16,24},{18,26},{24,28},{26,30},{28,20... | collective-permute-start | bytes 1572872 | tf_op jit(solution)/shard_map/ppermute | solution.py:76
  289.0 41.0 %collective-permute-start.48 = (bf16[1024,256]{1,0:T(8,128)(2,1)}, bf16[1024,256]{1,0:T(8,128)(2,1)}, u32[]{:S(2)}, u32[]{:S(2)}) collective-permute-start(bf16[1024,256]{1,0:T(8,128)(2,1)} %get-tuple-element.199), channel_id=1, source_target_pairs={{0,4},{2,6},{8,0},{10,2},{16,8},{18,10},{24,16},{26,18},{28,24},{3... | collective-permute-start | bytes 1572872 | tf_op jit(solution)/shard_map/ppermute | solution.py:79
  292.2 24.2 %collective-permute-start.44 = (bf16[512,256]{1,0:T(8,128)(2,1)S(1)}, bf16[512,256]{1,0:T(8,128)(2,1)S(1)}, u32[]{:S(2)}, u32[]{:S(2)}) collective-permute-start(bf16[512,256]{1,0:T(8,128)(2,1)S(1)} %get-tuple-element.193), channel_id=1, source_target_pairs={{0,4},{2,6},{8,0},{10,2},{16,8},{18,10},{24,16},{26,18},{28,24},{3... | collective-permute-start | bytes 786440 | tf_op jit(solution)/shard_map/ppermute | solution.py:79
  317.2 16.5 %collective-permute-start.51 = (bf16[256,512]{1,0:T(8,128)(2,1)}, bf16[256,512]{1,0:T(8,128)(2,1)}, u32[]{:S(2)}, u32[]{:S(2)}) collective-permute-start(bf16[256,512]{1,0:T(8,128)(2,1)} %add_convert_fusion), channel_id=1, source_target_pairs={{0,2},{2,0},{4,6},{6,4},{8,10},{10,8},{12,14},{14,12},{16,18},{18,... | collective-permute-start | bytes 786440 | tf_op jit(solution)/shard_map/ppermute | solution.py:82
  350.6 31.2 %collective-permute-start.52 = (bf16[512,2048]{1,0:T(8,128)(2,1)}, bf16[512,2048]{1,0:T(8,128)(2,1)}, u32[]{:S(2)}, u32[]{:S(2)}) collective-permute-start(bf16[512,2048]{1,0:T(8,128)(2,1)} %get-tuple-element.217), channel_id=1, source_target_pairs={{0,2},{2,0},{4,6},{6,4},{8,10},{10,8},{12,14},{14,12},{16,18},{18,... | collective-permute-start | bytes 6291464 | tf_op jit(solution)/shard_map/ppermute | solution.py:82
  351.1 48.8 %collective-permute-start.35 = (bf16[512,2048]{1,0:T(8,128)(2,1)}, bf16[512,2048]{1,0:T(8,128)(2,1)}, u32[]{:S(2)}, u32[]{:S(2)}) collective-permute-start(bf16[512,2048]{1,0:T(8,128)(2,1)} %convert_add_fusion.2), channel_id=1, source_target_pairs={{0,1},{1,0},{2,3},{3,2},{4,5},{5,4},{6,7},{7,6},{8,9},{9,8},{10,11... | collective-permute-start | bytes 6291464 | tf_op jit(solution)/shard_map/ppermute | solution.py:1018
  353.8 15.1 %collective-permute-start.53 = (bf16[1024,256]{1,0:T(8,128)(2,1)}, bf16[1024,256]{1,0:T(8,128)(2,1)S(1)}, u32[]{:S(2)}, u32[]{:S(2)}) collective-permute-start(bf16[1024,256]{1,0:T(8,128)(2,1)} %copy-done.76), channel_id=1, source_target_pairs={{0,8},{2,10},{8,16},{10,18},{16,24},{18,26},{24,28},{26,30},{28,20... | collective-permute-start | bytes 1572872 | tf_op jit(solution)/shard_map/ppermute | solution.py:76
  355.9 25.4 %collective-permute-start.56 = (bf16[1024,256]{1,0:T(8,128)(2,1)}, bf16[1024,256]{1,0:T(8,128)(2,1)}, u32[]{:S(2)}, u32[]{:S(2)}) collective-permute-start(bf16[1024,256]{1,0:T(8,128)(2,1)} %copy-done.74), channel_id=1, source_target_pairs={{0,8},{2,10},{8,16},{10,18},{16,24},{18,26},{24,28},{26,30},{28,20... | collective-permute-start | bytes 1572872 | tf_op jit(solution)/shard_map/ppermute | solution.py:76
  368.9 16.7 %collective-permute-start.57 = (bf16[1024,256]{1,0:T(8,128)(2,1)}, bf16[1024,256]{1,0:T(8,128)(2,1)}, u32[]{:S(2)}, u32[]{:S(2)}) collective-permute-start(bf16[1024,256]{1,0:T(8,128)(2,1)} %copy-done.73), channel_id=1, source_target_pairs={{0,4},{2,6},{8,0},{10,2},{16,8},{18,10},{24,16},{26,18},{28,24},{3... | collective-permute-start | bytes 1572872 | tf_op jit(solution)/shard_map/ppermute | solution.py:79
  385.6 16.6 %collective-permute-start.70 = (bf16[128,256]{1,0:T(8,128)(2,1)S(1)}, bf16[128,256]{1,0:T(8,128)(2,1)S(1)}, u32[]{:S(2)}, u32[]{:S(2)}) collective-permute-start(bf16[128,256]{1,0:T(8,128)(2,1)S(1)} %get-tuple-element.253), channel_id=1, source_target_pairs={{0,28},{2,30},{4,0},{6,2},{8,4},{10,6},{12,8},{14,10},{16,12},{18,... | collective-permute-start | bytes 196616 | tf_op jit(solution)/shard_map/ppermute | solution.py:1178
  393.7 50.2 %collective-permute-start.55 = (bf16[512,2048]{1,0:T(8,128)(2,1)}, bf16[512,2048]{1,0:T(8,128)(2,1)}, u32[]{:S(2)}, u32[]{:S(2)}) collective-permute-start(bf16[512,2048]{1,0:T(8,128)(2,1)} %convert_add_fusion.1.own), channel_id=1, source_target_pairs={{0,1},{1,0},{2,3},{3,2},{4,5},{5,4},{6,7},{7,6},{8,9},{9,8},{10,11... | collective-permute-start | bytes 6291464 | tf_op jit(solution)/shard_map/ppermute | solution.py:1175
  399.9 16.9 %collective-permute-start.67 = (bf16[128,256]{1,0:T(8,128)(2,1)S(1)}, bf16[128,256]{1,0:T(8,128)(2,1)S(1)}, u32[]{:S(2)}, u32[]{:S(2)}) collective-permute-start(bf16[128,256]{1,0:T(8,128)(2,1)S(1)} %get-tuple-element.247), channel_id=1, source_target_pairs={{0,16},{2,18},{4,20},{6,22},{8,24},{10,26},{12,28},{14,30},{16,0},... | collective-permute-start | bytes 196616 | tf_op jit(solution)/shard_map/ppermute | solution.py:1178
  402.2 15.9 %collective-permute-start.66 = (bf16[128,256]{1,0:T(8,128)(2,1)S(1)}, bf16[128,256]{1,0:T(8,128)(2,1)S(1)}, u32[]{:S(2)}, u32[]{:S(2)}) collective-permute-start(bf16[128,256]{1,0:T(8,128)(2,1)S(1)} %get-tuple-element.245), channel_id=1, source_target_pairs={{0,12},{2,14},{4,16},{6,18},{8,20},{10,22},{12,24},{14,26},{16,28}... | collective-permute-start | bytes 196616 | tf_op jit(solution)/shard_map/ppermute | solution.py:1178
  402.6 16.2 %collective-permute-start.65 = (bf16[128,256]{1,0:T(8,128)(2,1)S(1)}, bf16[128,256]{1,0:T(8,128)(2,1)S(1)}, u32[]{:S(2)}, u32[]{:S(2)}) collective-permute-start(bf16[128,256]{1,0:T(8,128)(2,1)S(1)} %get-tuple-element.243), channel_id=1, source_target_pairs={{0,8},{2,10},{4,12},{6,14},{8,16},{10,18},{12,20},{14,22},{16,24},... | collective-permute-start | bytes 196616 | tf_op jit(solution)/shard_map/ppermute | solution.py:1178
  403.3 15.5 %collective-permute-start.64 = (bf16[128,256]{1,0:T(8,128)(2,1)S(1)}, bf16[128,256]{1,0:T(8,128)(2,1)S(1)}, u32[]{:S(2)}, u32[]{:S(2)}) collective-permute-start(bf16[128,256]{1,0:T(8,128)(2,1)S(1)} %get-tuple-element.241), channel_id=1, source_target_pairs={{0,4},{2,6},{4,8},{6,10},{8,12},{10,14},{12,16},{14,18},{16,20},{1... | collective-permute-start | bytes 196616 | tf_op jit(solution)/shard_map/ppermute | solution.py:1178
  416.8 36.3 %collective-permute-start.61 = (bf16[1024,256]{1,0:T(8,128)(2,1)}, bf16[1024,256]{1,0:T(8,128)(2,1)}, u32[]{:S(2)}, u32[]{:S(2)}) collective-permute-start(bf16[1024,256]{1,0:T(8,128)(2,1)} %get-tuple-element.232), channel_id=1, source_target_pairs={{0,8},{2,10},{8,16},{10,18},{16,24},{18,26},{24,28},{26,30},{28,20... | collective-permute-start | bytes 1572872 | tf_op jit(solution)/shard_map/ppermute | solution.py:76
  418.1 35.0 %collective-permute-start.62 = (bf16[1024,256]{1,0:T(8,128)(2,1)}, bf16[1024,256]{1,0:T(8,128)(2,1)}, u32[]{:S(2)}, u32[]{:S(2)}) collective-permute-start(bf16[1024,256]{1,0:T(8,128)(2,1)} %get-tuple-element.233), channel_id=1, source_target_pairs={{0,4},{2,6},{8,0},{10,2},{16,8},{18,10},{24,16},{26,18},{28,24},{3... | collective-permute-start | bytes 1572872 | tf_op jit(solution)/shard_map/ppermute | solution.py:79
  418.8 45.3 %collective-permute-start.60 = (f32[1024,128]{1,0:T(8,128)}, f32[1024,128]{1,0:T(8,128)S(1)}, u32[]{:S(2)}, u32[]{:S(2)}) collective-permute-start(f32[1024,128]{1,0:T(8,128)} %get-tuple-element.235), channel_id=1, source_target_pairs={{0,2},{2,0},{4,6},{6,4},{8,10},{10,8},{12,14},{14,12},{16,18},{18,... | collective-permute-start | bytes 1572872 | tf_op jit(solution)/shard_map/ppermute | solution.py:82
  422.4 38.9 %collective-permute-start.71 = (f32[80,128]{1,0:T(8,128)S(1)}, f32[80,128]{1,0:T(8,128)}, u32[]{:S(2)}, u32[]{:S(2)}) collective-permute-start(f32[80,128]{1,0:T(8,128)S(1)} %constant_dynamic-slice_fusion), channel_id=1, source_target_pairs={{0,2},{2,0},{4,6},{6,4},{8,10},{10,8},{12,14},{14,12},{16,18},{18,... | collective-permute-start | bytes 122888 | tf_op jit(solution)/shard_map/ppermute | solution.py:82
  443.9 15.6 %collective-permute-start.75 = (f32[3328]{0:T(1024)S(1)}, f32[3328]{0:T(1024)S(1)}, u32[]{:S(2)}, u32[]{:S(2)}) collective-permute-start(f32[3328]{0:T(1024)S(1)} %slice_add_fusion), channel_id=1, source_target_pairs={{0,1},{1,0},{2,3},{3,2},{4,5},{5,4},{6,7},{7,6},{8,9},{9,8},{10,11... | collective-permute-start | bytes 39944 | tf_op jit(solution)/shard_map/ppermute | solution.py:1013
  (125 other events, 1072.1 us)
